TPU v7x, 128 devices: a whole 4x4x4 slice. The times are simulated.
128 devices in a mesh: owner: 32 (over y, x, core), replica: 4 (over z).
Axes of the slice: x: 4, y: 4, z: 4, core: 2. Of those that a mesh axis runs over, the one named last changes fastest.
Arguments:
- queries: bfloat16 [4096, 1024], P(('owner', 'replica')), may hold values from -6 to 6
- probes: int32 [4096, 8], P(('owner', 'replica')), may hold values from 0 to 127, as said below
- list_slot: int32 [128], replicated, may hold values from 0 to 127, each once
- valid_rows: int32 [128], P('owner'), may hold values from 128 to 1024
- database: bfloat16 [128, 1024, 1024], P('owner', 'replica'), may hold values from -0.1875 to 0.1875
Outputs:
- nearest: float32 [4096, 32], P(('owner', 'replica'))
Inputs may be any that keep to these rules, and one draw needn't show every extreme that they name: `probes`: each query names 8 different lists; in every aligned block of 32 query rows no list is named by more than 4 queries. `list_slot`: each position once.
All inputs are finite; a program needn't handle non-finite values.
Results may differ from a plain program's by a relative error of at most 0.0003.
Values may be sent and summed in bfloat16 or wider, within the bound.
No kernel may reach another device: no remote copies, remote signals or barrier semaphores. Data moves between devices by JAX's collectives and lax.ppermute only.
A program may use at most 64 MiB of HBM per device.

v0:
```python
import jax
import jax.numpy as jnp
from jax import lax
from jax.sharding import PartitionSpec as P

TOPK = 32
CAPL = 4


def nearest_part(slot_rows, database, half_norm, row_valid):
    count, slots, feature_dim = slot_rows.shape
    lists_dev = database.shape[0]
    grouped = slot_rows.reshape(count, lists_dev, slots // lists_dev, feature_dim)
    scores = jnp.einsum("slcd,lrd->slcr", grouped, database, preferred_element_type=jnp.float32)
    scores = scores - half_norm[None, :, None, :]
    scores = jnp.where(row_valid[None, :, None, :], scores, -1e30)
    best_vals = lax.top_k(scores, TOPK)[0]
    return best_vals.reshape(count, slots, TOPK)


def per_device(queries, probes, list_slot, valid_rows, database):
    query_count, probe_count = probes.shape
    lists_dev, rows_dev, feature_dim = database.shape
    owners = lax.axis_size("owner")
    replicas = lax.axis_size("replica")
    list_total = lists_dev * owners
    slot_width = lists_dev * CAPL
    pair_count = query_count * probe_count
    positions = list_slot[probes].reshape(-1)
    pair_ids = jnp.arange(pair_count, dtype=jnp.int32)
    ordering = jnp.argsort(positions * pair_count + pair_ids)
    sorted_pos = positions[ordering]
    is_new = jnp.concatenate([jnp.ones((1,), bool), sorted_pos[1:] != sorted_pos[:-1]])
    first_pos = lax.cummax(jnp.where(is_new, pair_ids, 0))
    bucket_rank = jnp.zeros((pair_count,), jnp.int32).at[ordering].set(pair_ids - first_pos)
    target = positions * CAPL + bucket_rank
    sources = queries[pair_ids // probe_count]
    outgoing = jnp.zeros((list_total * CAPL, feature_dim), jnp.bfloat16).at[target].set(sources)
    outgoing = outgoing.reshape(owners, slot_width, feature_dim)
    replica_index = lax.axis_index("replica")
    half_norm = 0.5 * jnp.sum(jnp.square(database.astype(jnp.float32)), -1)
    row_ids = replica_index * rows_dev + jnp.arange(rows_dev, dtype=jnp.int32)
    row_valid = row_ids[None, :] < valid_rows[:, None]
    copies = jnp.broadcast_to(outgoing[:, None], (owners, replicas, slot_width, feature_dim))
    copies = copies.reshape(owners * replicas, slot_width, feature_dim)
    arrived = lax.all_to_all(copies, ("owner", "replica"), split_axis=0, concat_axis=0, tiled=True)
    partial_value = nearest_part(arrived, database, half_norm, row_valid)
    returned = lax.all_to_all(
        partial_value, ("owner", "replica"), split_axis=0, concat_axis=0, tiled=True
    )
    returned = returned.reshape(owners, replicas, slot_width, TOPK)
    candidates = returned[target // slot_width, :, target % slot_width]
    candidates = candidates.reshape(query_count, probe_count * replicas * TOPK)
    return lax.top_k(candidates, TOPK)[0]


def solution(mesh):
    in_specs = (
        P(("owner", "replica"), None),
        P(("owner", "replica"), None),
        P(),
        P("owner"),
        P("owner", "replica", None),
    )
    out_specs = P(("owner", "replica"), None)
    return jax.shard_map(
        per_device, mesh=mesh, in_specs=in_specs, out_specs=out_specs, check_vma=False
    )
```

profile of v0, /device:TPU:0, one launch (start us, length us, event | category | flops | bytes accessed | tf_op | source)
XLA Modules:
  0.0 166.4 jit_solution(2605348658471039355)
XLA Ops:
  0.0 0.7 compare_select_fusion
  0.7 0.1 copy.12
  0.8 0.1 reshape.119
  0.9 1.9 %gather_fusion = s32[256]{0:T(256)S(1)} fusion(s32[128]{0:T(128)S(1)} %copy-done.1, s32[1024]{0:T(1024)S(1)} %pad_clamp_fusion.2), kind=kCustom, calls=%fused_computation | custom fusion | bytes 3072 | tf_op jit(solution)/shard_map/gather | solution.py:29
  2.8 3.2 %sort.21 = (s32[256]{0:T(256)}, s32[256]{0:T(256)S(1)}) sort(s32[256]{0:T(256)S(1)} %iota_add_fusion, s32[256]{0:T(256)S(1)} %iota.38), dimensions={0}, to_apply=%region_0.0 | sort | flops 2048 | bytes 4096 | tf_op jit(solution)/shard_map/jit(argsort)/sort | solution.py:31
  6.0 1.9 %gather_fusion.1 = s32[256]{0:T(256)S(1)} fusion(s32[256]{0:T(256)S(1)} %gather_fusion, s32[1024]{0:T(1024)S(1)} %pad_clamp_fusion.1), kind=kCustom, calls=%fused_computation.1 | custom fusion | bytes 3072 | tf_op jit(solution)/shard_map/gather | solution.py:32
  8.0 0.1 fusion.7
  8.1 0.3 reduce-window.9
  8.5 0.1 slice_reduce_fusion
  8.7 1.4 scatter_custom_fusion
  10.2 3.7 %scatter_custom_fusion.1 = bf16[512,1024]{1,0:T(8,128)(2,1)S(1)} fusion(s32[256]{0:T(256)S(1)} %get-tuple-element.17, bf16[32,1024]{1,0:T(8,128)(2,1)S(1)} %copy-done, s32[1024]{0:T(1024)S(1)} %pad_clamp_fusion, bf16[]{:T(256)} %constant.70.clone.1), kind=kCustom, calls=%fused_computation.10 | custom fusion | bytes 1048578 | tf_op jit(solution)/shard_map/scatter | solution.py:38
  13.9 2.5 %broadcast_in_dim.51 = bf16[32,4,16,1024]{3,2,1,0:T(8,128)(2,1)} broadcast(bf16[32,16,1024]{2,1,0:T(8,128)(2,1)S(1)} %bitcast.23), dimensions={0,2,3} | broadcast | bytes 5242880 | tf_op jit(solution)/shard_map/broadcast_in_dim | solution.py:44
  16.4 11.9 %all-to-all-start = ((bf16[128,16,1024]{2,1,0:T(8,128)(2,1)}), bf16[128,16,1024]{2,1,0:T(8,128)(2,1)}, u32[]{:S(2)}, u32[]{:S(2)}) async-start(bf16[128,16,1024]{2,1,0:T(8,128)(2,1)} %bitcast.22), calls=%async_computation | async-start | bytes 8388608 | tf_op jit(solution)/shard_map/all_to_all | solution.py:46
  28.4 0.5 multiply_reduce_fusion
  28.9 50.7 %all-to-all-done = bf16[128,16,1024]{2,1,0:T(8,128)(2,1)} async-done(((bf16[128,16,1024]{2,1,0:T(8,128)(2,1)}), bf16[128,16,1024]{2,1,0:T(8,128)(2,1)}, u32[]{:S(2)}, u32[]{:S(2)}) %all-to-all-start) | async-done | bytes 4194336 | tf_op jit(solution)/shard_map/all_to_all | solution.py:46
  79.6 4.5 %copy.13 = bf16[128,16,1024]{2,0,1:T(8,128)(2,1)S(1)} copy(bf16[128,16,1024]{2,1,0:T(8,128)(2,1)} %all-to-all-done) | data formatting | bytes 8388608 | tf_op jit(solution)/shard_map/all_to_all | solution.py:46
  84.1 2.7 %select_bitcast_fusion = f32[128,4,4,256]{3,0,2,1:T(8,128)} fusion(bf16[128,4,4,1024]{3,0,2,1:T(8,128)(2,1)S(1)} %bitcast.25, bf16[4,256,1024]{2,1,0:T(8,128)(2,1)S(1)} %copy-done.2, f32[4,256]{1,0:T(4,128)S(1)} %broadcast_multiply_fusion, pred[4,256]{1,0:T(4,128)(4,1)S(1)} %broadcast_compare_fusion), kind=kOutput, calls=%fused_computation.9 | convolution fusion | flops 1074790400 | bytes 8393728 | tf_op jit(solution)/shard_map/slcd,lrd->slcr/dot_general | solution.py:14
  86.8 1.9 %copy.17 = f32[128,4,4,256]{0,3,2,1:T(8,128)S(1)} copy(f32[128,4,4,256]{3,0,2,1:T(8,128)} %select_bitcast_fusion) | data formatting | bytes 4194304
  88.7 1.5 iota.46.clone
  90.2 49.4 %top_k.14 = (f32[128,4,4,256]{0,3,2,1:T(8,128)}, s32[128,4,4,256]{0,3,2,1:T(8,128)}) sort(f32[128,4,4,256]{0,3,2,1:T(8,128)S(1)} %copy.17, s32[128,4,4,256]{0,3,2,1:T(8,128)} %iota.46.clone), dimensions={3}, to_apply=%region_6.7 | sort | flops 9961472 | bytes 8388608 | tf_op jit(solution)/shard_map/top_k | solution.py:17
  139.6 1.9 %copy.19 = f32[128,4,4,256]{3,0,2,1:T(8,128)S(1)} copy(f32[128,4,4,256]{0,3,2,1:T(8,128)} %get-tuple-element.13) | data formatting | bytes 4194304 | tf_op jit(solution)/shard_map/top_k | solution.py:17
  141.5 0.1 top_k.22
  141.6 0.6 copy.14
  142.2 0.5 reshape.191
  142.7 15.2 %all_to_all.10 = f32[128,1,512]{2,1,0:T(1,128)S(1)} all-to-all(f32[128,1,512]{2,1,0:T(1,128)S(1)} %reshape.191), channel_id=1, replica_groups=mesh['owner'=32,'replica'=4] {'owner','replica'}, dimensions={0} | all-to-all | bytes 524288 | tf_op jit(solution)/shard_map/all_to_all | solution.py:48
  157.8 0.5 broadcast.184
  158.4 1.3 reduce.2
  159.6 0.3 reshape.192
  159.9 0.4 copy.15
  160.3 1.3 gather_fusion.2
  161.6 0.4 reshape.116
  162.1 4.4 %sort_prefixfusion = f32[32,32]{1,0:T(8,128)} fusion(f32[32,1024]{1,0:T(8,128)S(1)} %reshape.116), kind=kCustom, calls=%top_k.20.sort_prefix | custom fusion | flops 491520 | bytes 135168 | tf_op jit(solution)/shard_map/top_k | solution.py:54
  (23 shorter events, 0.4 us)
Async XLA Ops:
  0.0 10.2 %copy-start = (bf16[32,1024]{1,0:T(8,128)(2,1)S(1)}, bf16[32,1024]{1,0:T(8,128)(2,1)}, u32[]{:S(2)}) copy-start(bf16[32,1024]{1,0:T(8,128)(2,1)} %param.5) | copy-start | bytes 196612
  0.0 0.9 copy-start.1
  16.4 11.9 %copy-start.3 = (s32[4]{0:T(128)S(1)}, s32[4]{0:T(128)}, u32[]{:S(2)}) copy-start(s32[4]{0:T(128)} %param.8) | copy-start | bytes 52
  16.4 12.0 %copy-start.2 = (bf16[4,256,1024]{2,1,0:T(8,128)(2,1)S(1)}, bf16[4,256,1024]{2,1,0:T(8,128)(2,1)}, u32[]{:S(2)}) copy-start(bf16[4,256,1024]{2,1,0:T(8,128)(2,1)} %param.9) | copy-start | bytes 6291460
  16.4 63.2 %all-to-all-start = ((bf16[128,16,1024]{2,1,0:T(8,128)(2,1)}), bf16[128,16,1024]{2,1,0:T(8,128)(2,1)}, u32[]{:S(2)}, u32[]{:S(2)}) async-start(bf16[128,16,1024]{2,1,0:T(8,128)(2,1)} %bitcast.22), calls=%async_computation | async-start | bytes 8388608 | tf_op jit(solution)/shard_map/all_to_all | solution.py:46
where the time goes:
time: 168 us; the launch traced here: 166 us
  other arithmetic  60.1 us (36%)
  waiting for transfers between devices  50.7 us (30%)
  local copies, waits for them, and re-layouts  25.7 us (15%)
  blocking collectives  15.2 us (9%)
  starting transfers between devices  11.9 us (7%)
  matrix products  2.66 us (2%)
    all_to_all x1, waiting for transfers between devices, per_device(): lax.all_to_all(copies, ('owner', 'replica'), split_axis=0, concat_axis=0,...  50.7 us
    top_k x1, other arithmetic, nearest_part(): best_vals = lax.top_k(scores, TOPK)[0]  49.4 us
    all_to_all x1, blocking collectives, per_device(): lax.all_to_all(partial_value, ('owner', 'replica'), split_axis=0, concat_...  15.2 us
    all_to_all x1, starting transfers between devices, per_device(): lax.all_to_all(copies, ('owner', 'replica'), split_axis=0, concat_axis=0,...  11.9 us
    all_to_all x1, local copies, waits for them, and re-layouts, per_device(): lax.all_to_all(copies, ('owner', 'replica'), split_axis=0, concat_axis=0,...  4.51 us
    top_k x1, other arithmetic, per_device(): return lax.top_k(candidates, TOPK)[0]  4.35 us
    scatter x1, local copies, waits for them, and re-layouts, per_device(): jnp.zeros((list_total * CAPL, feature_dim), jnp.bfloat16).at[target]  3.71 us
  transfers between devices with their start and end apart: 1, of which 1 were waited for; matrix products, arithmetic and copies ran while one was open for 0% of the time, Pallas kernels for 0%

commit v1 on v0

v1 whole, which is shorter than its diff:
```python
import itertools

import jax
import jax.numpy as jnp
import numpy as np
from jax import lax
from jax.experimental import pallas as pl
from jax.experimental.pallas import tpu as pltpu
from jax.sharding import PartitionSpec as P

D = 1024
WIDE = D + 128
TOPK = 32
AXES = ("owner", "replica")
N_DEV = 128
N_CORE = 64
BIG = 1e30
F32 = jnp.float32
BF16 = jnp.bfloat16

PAIRING = {"a": (1, 0, 3, 2), "b": (3, 2, 1, 0)}
DIMS_A = ("za", "ya", "xa")
DIMS_B = ("zb", "yb", "xb")


def moved(device, dim):
    z, core, x, y = device % 4, device // 4 % 2, device // 8 % 4, device // 32
    place = {"x": x, "y": y, "z": z}
    place[dim[0]] = PAIRING[dim[1]][place[dim[0]]]
    return ((place["y"] * 4 + place["x"]) * 2 + core) * 4 + place["z"]


def core_of(device):
    return device // 4 % 2


def far(device, mask, first):
    dims = DIMS_A if (core_of(device) == 0) == first else DIMS_B
    for bit, dim in enumerate(dims):
        if mask >> bit & 1:
            device = moved(device, dim)
    return device


def near_group(device):
    return tuple(sorted(far(device, mask, True) for mask in range(8)))


NEAR_GROUPS = [list(group) for group in sorted({near_group(device) for device in range(N_DEV)})]
CORE_GROUPS = [[device for device in range(N_DEV) if core_of(device) == core] for core in range(2)]
CORE_SWAP = [(device, device ^ 4) for device in range(N_DEV)]
FIRST_HALF = (0, 1, 2, 4)
SECOND_HALF = (3, 6, 5, 7)


def block_places():
    table = np.zeros((N_DEV, N_CORE), np.int32)
    for device in range(N_DEV):
        owners = itertools.chain.from_iterable(near_group(far(device, mask, False)) for mask in FIRST_HALF + SECOND_HALF)
        table[device] = [owner // 8 * 4 + owner % 4 for owner in owners]
    return table


def sort_pairs(count):
    pairs = []
    p = 1
    while p < count:
        k = p
        while k >= 1:
            for j in range(k % p, count - k, 2 * k):
                for i in range(min(k, count - j - k)):
                    if (i + j) // (p * 2) == (i + j + k) // (p * 2):
                        pairs.append((i + j, i + j + k))
            k //= 2
        p *= 2
    return pairs


SORT_PAIRS = sort_pairs(TOPK)
MERGE_PAIRS = [(i, i + d) for d in (16, 8, 4, 2, 1) for i in range(TOPK) if not i & d]


def exchange(values, pairs):
    values = list(values)
    for i, j in pairs:
        values[i], values[j] = jnp.maximum(values[i], values[j]), jnp.minimum(values[i], values[j])
    return values


def merged(first, second):
    return exchange([jnp.maximum(first[i], second[TOPK - 1 - i]) for i in range(TOPK)], MERGE_PAIRS)


def merged_rows(first, second, shift):
    row = lax.broadcasted_iota(jnp.int32, (8, 128), 0)
    odd = (row & shift) != 0
    here = [jnp.where(odd, b, a) for a, b in zip(first, second)]
    there = [pltpu.roll(jnp.where(odd, a, b), 8 - shift, 0) for a, b in zip(first, second)]
    return merged(here, there)


def place_matrix(slot_ref):
    core = lax.rem(lax.axis_index("owner"), 2)
    places = jnp.bitwise_xor(slot_ref[...], 4 * core)
    return (places == lax.broadcasted_iota(jnp.int32, (128, 128), 0)).astype(BF16)


def rank_table(probes_ref, place):
    probes = probes_ref[...]
    lists = lax.broadcasted_iota(jnp.int32, (32, 128), 1)
    named = jnp.zeros((32, 128), F32)
    for j in range(8):
        named = jnp.where(probes[:, j : j + 1] == lists, 1.0, named)
    probed = lax.dot_general(named.astype(BF16), place, (((1,), (1,)), ((), ())), preferred_element_type=F32)
    before = lax.broadcasted_iota(jnp.int32, (32, 32), 1) < lax.broadcasted_iota(jnp.int32, (32, 32), 0)
    rank = jnp.dot(before.astype(BF16), probed.astype(BF16), preferred_element_type=F32)
    return jnp.where(probed > 0.5, rank, -1.0).astype(BF16)


def widen_kernel(queries_ref, probes_ref, slot_ref, out_ref):
    out_ref[:, :D] = queries_ref[...]
    out_ref[:, D:] = rank_table(probes_ref, place_matrix(slot_ref))


def wanted_kernel(probes_ref, flat_ref, slot_ref, pick_ref, group_ref):
    place = place_matrix(slot_ref)
    rank = rank_table(probes_ref, place)
    named = (flat_ref[...] == lax.broadcasted_iota(jnp.int32, (128, 256), 0)).astype(BF16)
    placed = jnp.dot(place, named, preferred_element_type=F32)
    index = lax.broadcasted_iota(jnp.int32, (128, 256), 0)
    where = jnp.sum(placed * index.astype(F32), 0, keepdims=True).astype(jnp.int32)
    ranks = jnp.dot(rank, placed.astype(BF16), preferred_element_type=F32)
    own = lax.broadcasted_iota(jnp.int32, (32, 256), 0) == (lax.broadcasted_iota(jnp.int32, (32, 256), 1) & 31)
    slot = jnp.sum(jnp.where(own, ranks, 0.0), 0, keepdims=True).astype(jnp.int32)
    row = (where >> 2) * 4 + slot
    pick_ref[...] = (index == row).astype(BF16)
    group_ref[...] = jnp.broadcast_to(where & 3, (8, 256))


def norm_kernel(own_ref, sibling_ref, own_valid_ref, sibling_valid_ref, out_ref):
    first_row = lax.axis_index("replica") * 256
    row = first_row + lax.broadcasted_iota(jnp.int32, (256, 128), 0)
    lane = lax.broadcasted_iota(jnp.int32, (256, 128), 1)
    total = jnp.zeros((256, 128), F32)
    for t in range(8):
        ref, valid = (own_ref, own_valid_ref) if t < 4 else (sibling_ref, sibling_valid_ref)
        rows = ref[t % 4].astype(F32)
        norm = 0.5 * jnp.sum(rows * rows, 1, keepdims=True)
        total = jnp.where(lane == t, jnp.where(row < valid[t % 4], norm, BIG), total)
    out_ref[...] = total


def score_lists(group_refs, own_ref, sibling_ref, norm_ref, block_ref, query_buf, list_buf, chosen, best, sems):
    copies = []
    for g, ref in enumerate(group_refs):
        copies.append(pltpu.make_async_copy(ref, query_buf.at[g], sems.at[g]))
    for t in range(8):
        source = own_ref.at[t] if t < 4 else sibling_ref.at[t - 4]
        copies.append(pltpu.make_async_copy(source, list_buf.at[t], sems.at[4 + t]))
    for copy in copies:
        copy.start()
    chip = lax.axis_index("owner") // 2
    column = lax.broadcasted_iota(jnp.int32, (256, 128), 0)
    wanted = (lax.broadcasted_iota(jnp.int32, (256, 128), 1) == chip * 8 + (column >> 5)).astype(BF16)
    column = lax.broadcasted_iota(jnp.int32, (256, 256), 0)
    same_block = (lax.broadcasted_iota(jnp.int32, (256, 256), 1) >> 5) == (column & 7)
    column_rank = ((column >> 3) & 3).astype(F32)
    for g in range(4):
        copies[g].wait()
        rank = lax.dot_general(wanted, query_buf[g, :, D:], (((1,), (1,)), ((), ())), preferred_element_type=F32)
        pick = (same_block & (rank == column_rank)).astype(BF16)
        picked = jnp.dot(pick, query_buf[g, :, :D], preferred_element_type=F32).astype(BF16)
        for t in range(8):
            chosen[t, 32 * g : 32 * g + 32, :] = picked[32 * t : 32 * t + 32]

    def sorted_list(t):
        copies[4 + t].wait()
        scores = lax.dot_general(list_buf[t], chosen[t], (((1,), (1,)), ((), ())), preferred_element_type=F32)
        scores = scores - norm_ref[:, t : t + 1]
        return exchange([scores[8 * i : 8 * i + 8] for i in range(TOPK)], SORT_PAIRS)

    quads = []
    for quad in range(2):
        pairs = [merged_rows(sorted_list(4 * quad + 2 * p), sorted_list(4 * quad + 2 * p + 1), 1) for p in range(2)]
        quads.append(merged_rows(pairs[0], pairs[1], 2))
    for i, value in enumerate(merged_rows(quads[0], quads[1], 4)):
        best[8 * i : 8 * i + 8, :] = value
    for half in range(2):
        rows = jnp.concatenate([best[pl.ds(4 * half + t, TOPK, stride=8), :] for t in range(4)], 0)
        turned = rows.T
        for g in range(4):
            for k in range(4):
                block_ref[pl.ds(64 * g + 4 * half + k, 8, stride=8), :] = turned[32 * g + 8 * k : 32 * g + 8 * k + 8]


def first_kernel(*refs):
    groups, (own, sibling, norm, out), scratch = refs[:4], refs[4:8], refs[8:]
    score_lists(groups, own, sibling, norm, out, *scratch)


def second_kernel(*refs):
    groups, (own, sibling, norm, earlier, place_ref, out, block_buf), scratch = refs[:4], refs[4:11], refs[11:]
    score_lists(groups, own, sibling, norm, block_buf, *scratch)
    for b in range(32):
        out[place_ref[b]] = earlier[8 * b : 8 * b + 8, :]
        out[place_ref[32 + b]] = block_buf[8 * b : 8 * b + 8, :]


def final_kernel(back_ref, pick_ref, group_ref, out_ref, tiles, rows):
    pick = pick_ref[...]
    group = jnp.concatenate([group_ref[...]] * 4, 0)
    for z in range(4):
        left = back_ref[:, z].reshape(128, 128).T
        found = jnp.zeros((128, 256), F32)
        for _ in range(3):
            piece = left.astype(BF16)
            left = left - piece.astype(F32)
            found = found + jnp.dot(piece, pick, preferred_element_type=F32)
        scores = found[:32]
        for t in range(1, 4):
            scores = jnp.where(group == t, found[32 * t : 32 * t + 32], scores)
        for half in range(2):
            tiles[pl.ds(2 * z + half, TOPK, stride=8), :] = scores[:, 128 * half : 128 * half + 128]
    values = [tiles[8 * i : 8 * i + 8, :] for i in range(TOPK)]
    for axis, shift in ((0, 4), (0, 2), (0, 1), (1, 64), (1, 32)):
        values = merged(values, [pltpu.roll(value, shift, axis) for value in values])
    for i, value in enumerate(values):
        rows[i : i + 1, :] = value[:1]
    out_ref[...] = rows[...].T[:32]


def params():
    return pltpu.CompilerParams(vmem_limit_bytes=40 * 1024 * 1024)


def spaces(text):
    kinds = {"v": pltpu.VMEM, "s": pltpu.SMEM, "a": pl.ANY}
    return [pl.BlockSpec(memory_space=kinds[kind]) for kind in text]


def hop(value, mask):
    return lax.ppermute(value, AXES, [(device, far(device, mask, False)) for device in range(N_DEV)])


def per_device(queries, probes, list_slot, valid_rows, database):
    shape = jax.ShapeDtypeStruct
    slots = list_slot.reshape(1, 128)
    sibling = lax.ppermute(database, AXES, CORE_SWAP)
    sibling_valid = lax.ppermute(valid_rows, AXES, CORE_SWAP)
    wide = pl.pallas_call(
        widen_kernel, out_shape=shape((32, WIDE), BF16), in_specs=spaces("vvv"), out_specs=spaces("v")[0], name="widen"
    )(queries, probes, slots)
    copies = jnp.broadcast_to(wide[None], (8, 32, WIDE))
    near = lax.all_to_all(copies, AXES, 0, 0, axis_index_groups=NEAR_GROUPS, tiled=True).reshape(256, WIDE)
    gathered = {0: near}
    for mask in (1, 2, 4):
        gathered[mask] = hop(near, mask)
    for mask, source, step in ((3, 1, 2), (6, 2, 4), (5, 4, 1)):
        gathered[mask] = hop(gathered[source], step)
    gathered[7] = hop(gathered[3], 4)

    norms = pl.pallas_call(
        norm_kernel, out_shape=shape((256, 128), F32), in_specs=spaces("vvss"), out_specs=spaces("v")[0], name="norms",
        compiler_params=params(),
    )(database, sibling, valid_rows, sibling_valid)
    pick, group = pl.pallas_call(
        wanted_kernel, out_shape=(shape((128, 256), BF16), shape((8, 256), jnp.int32)), in_specs=spaces("vvv"),
        out_specs=spaces("vv"), name="wanted",
    )(probes, probes.T.reshape(1, 256), slots)
    places = jnp.asarray(block_places())[lax.axis_index(AXES)]

    scratch = [
        pltpu.VMEM((4, 256, WIDE), BF16),
        pltpu.VMEM((8, 256, D), BF16),
        pltpu.VMEM((8, 128, D), BF16),
        pltpu.VMEM((256, 128), F32),
        pltpu.SemaphoreType.DMA((12,)),
    ]
    early = pl.pallas_call(
        first_kernel, out_shape=shape((256, 128), F32), in_specs=spaces("aaaaaav"), out_specs=spaces("v")[0],
        scratch_shapes=scratch, compiler_params=params(), name="score_first",
    )(*[gathered[mask] for mask in FIRST_HALF], database, sibling, norms)
    blocks = pl.pallas_call(
        second_kernel, out_shape=shape((N_CORE, 8, 128), F32), in_specs=spaces("aaaaaavvs"), out_specs=spaces("v")[0],
        scratch_shapes=[pltpu.VMEM((256, 128), F32)] + scratch, compiler_params=params(), name="score_second",
    )(*[gathered[mask] for mask in SECOND_HALF], database, sibling, norms, early, places)
    back = lax.all_to_all(blocks, AXES, 0, 0, axis_index_groups=CORE_GROUPS, tiled=True)
    return pl.pallas_call(
        final_kernel, out_shape=shape((32, TOPK), F32), in_specs=spaces("vvv"), out_specs=spaces("v")[0],
        scratch_shapes=[pltpu.VMEM((256, 128), F32), pltpu.VMEM((32, 128), F32)], compiler_params=params(), name="final",
    )(back.reshape(16, 4, 8, 128), pick, group)


def solution(mesh):
    in_specs = (P(AXES, None), P(AXES, None), P(), P("owner"), P("owner", "replica", None))
    return jax.shard_map(per_device, mesh=mesh, in_specs=in_specs, out_specs=P(AXES, None), check_vma=False)
```

time: 168 us -> 83.6 us (0.50)
  other arithmetic: 60.1 us -> 0 us
  waiting for transfers between devices: 50.7 us -> 22.9 us
  Pallas kernels: 0 us -> 20.8 us
  starting transfers between devices: 11.9 us -> 30.1 us
  local copies, waits for them, and re-layouts: 25.7 us -> 9.05 us
  blocking collectives: 15.2 us -> 0 us
  matrix products: 2.66 us -> 0 us
    top_k x2 -> x0, other arithmetic: 53.7 us -> none  [the longest x1 49.4 us: nearest_part(): best_vals = lax.top_k(scores, TOPK)[0]]
    all_to_all x1 -> x2, waiting for transfers between devices: 50.7 us -> 12.7 us  [the longest x1 8.4 us: per_device(): lax.all_to_all(blocks, AXES, 0, 0, axis_index_groups=CORE_GROUPS, tiled=T...]
    pallas_call x0 -> x6, Pallas kernels: none -> 20.8 us  [the longest x1 7.82 us: per_device(): pl.pallas_call(second_kernel, out_shape=shape((N_CORE, 8, 128), F32), in_...]
    ppermute x0 -> x9, starting transfers between devices: none -> 18.5 us  [the longest x7 13.7 us: hop(): lax.ppermute(value, AXES, [(device, far(device, mask, False)) for device...]
    all_to_all x1 -> x0, blocking collectives: 15.2 us -> none  [per_device(): lax.all_to_all(partial_value, ('owner', 'replica'), split_axis=0, concat_...]
    ppermute x0 -> x9, waiting for transfers between devices: none -> 10.2 us  [the longest x7 9.91 us: hop(): lax.ppermute(value, AXES, [(device, far(device, mask, False)) for device...]
    scatter x2 -> x0, local copies, waits for them, and re-layouts: 5.1 us -> none  [the longest x1 3.71 us: per_device(): jnp.zeros((list_total * CAPL, feature_dim), jnp.bfloat16).at[target]]
    gather x3 -> x0, local copies, waits for them, and re-layouts: 5.1 us -> none  [the longest x1 1.95 us: per_device(): sorted_pos = positions[ordering]]
  transfers between devices with their start and end apart: 1 -> 11, of which waited for: 1 -> 5; matrix products, arithmetic and copies ran while one was open for 0% -> 2% of each run, Pallas kernels for 0% -> 12%
where the time goes in v1:
time: 83.6 us; the launch traced here: 83 us
  starting transfers between devices  30.1 us (36%)
  waiting for transfers between devices  22.9 us (27%)
  Pallas kernels  20.8 us (25%)
  local copies, waits for them, and re-layouts  9.05 us (11%)
    ppermute x7, starting transfers between devices, hop(): lax.ppermute(value, AXES, [(device, far(device, mask, False)) for device...  13.7 us
    ppermute x7, waiting for transfers between devices, hop(): lax.ppermute(value, AXES, [(device, far(device, mask, False)) for device...  9.91 us
    all_to_all x1, waiting for transfers between devices, per_device(): lax.all_to_all(blocks, AXES, 0, 0, axis_index_groups=CORE_GROUPS, tiled=T...  8.4 us
    pallas_call x1, Pallas kernels, per_device(): pl.pallas_call(second_kernel, out_shape=shape((N_CORE, 8, 128), F32), in_...  7.82 us
    all_to_all x1, starting transfers between devices, per_device(): lax.all_to_all(blocks, AXES, 0, 0, axis_index_groups=CORE_GROUPS, tiled=T...  6.42 us
    pallas_call x1, Pallas kernels, per_device(): pl.pallas_call(first_kernel, out_shape=shape((256, 128), F32), in_specs=s...  6.38 us
    unnamed x15, local copies, waits for them, and re-layouts  5.99 us
    all_to_all x1, starting transfers between devices, per_device(): lax.all_to_all(copies, AXES, 0, 0, axis_index_groups=NEAR_GROUPS, tiled=T...  5.22 us
  transfers between devices with their start and end apart: 11, of which 5 were waited for; matrix products, arithmetic and copies ran while one was open for 2% of the time, Pallas kernels for 12%

profile of v1, /device:TPU:0, one launch (start us, length us, event | category | flops | bytes accessed | tf_op | source)
XLA Modules:
  0.0 83.0 jit_solution(11462804047571755679)
XLA Ops:
  0.0 1.4 %copy.7.probes_ref = s32[32,8]{1,0:T(8,128)} copy(s32[32,8]{0,1:T(8,128)} %param.7) | data formatting | bytes 2048 | tf_op args[1]
  1.4 1.8 %widen.1 = bf16[32,1152]{1,0:T(8,128)(2,1)} custom-call(bf16[32,1024]{1,0:T(8,128)(2,1)} %queries_ref.1, s32[32,8]{1,0:T(8,128)} %copy.7.probes_ref, s32[1,128]{1,0:T(1,128)} %bitcast.12), custom_call_target="tpu_custom_call" | custom-call | tf_op jit(solution)/shard_map/widen/pallas_call | solution.py:250
  3.2 1.8 %broadcast_in_dim.2 = bf16[8,32,1152]{2,1,0:T(8,128)(2,1)} broadcast(bf16[32,1152]{1,0:T(8,128)(2,1)} %widen.1), dimensions={1,2} | broadcast | bytes 663552 | tf_op jit(solution)/shard_map/broadcast_in_dim | solution.py:253
  5.0 5.2 %all-to-all-start = ((bf16[8,32,1152]{2,1,0:T(8,128)(2,1)}), bf16[8,32,1152]{2,1,0:T(8,128)(2,1)S(1)}, u32[]{:S(2)}, u32[]{:S(2)}) async-start(bf16[8,32,1152]{2,1,0:T(8,128)(2,1)} %broadcast_in_dim.2), calls=%async_computation | async-start | bytes 1179648 | tf_op jit(solution)/shard_map/all_to_all | solution.py:254
  10.2 4.4 %collective-permute-start.7 = (bf16[4,256,1024]{2,1,0:T(8,128)(2,1)}, bf16[4,256,1024]{2,1,0:T(8,128)(2,1)S(1)}, u32[]{:S(2)}, u32[]{:S(2)}) collective-permute-start(bf16[4,256,1024]{2,1,0:T(8,128)(2,1)} %refs_4_.3), channel_id=1, source_target_pairs={{0,4},{1,5},{2,6},{3,7},{4,0},{5,1},{6,2},{7,3},{8,12},{9,13},{10,... | collective-permute-start | bytes 6291464 | tf_op jit(solution)/shard_map/ppermute | solution.py:248
  14.6 4.3 %all-to-all-done = bf16[8,32,1152]{2,1,0:T(8,128)(2,1)S(1)} async-done(((bf16[8,32,1152]{2,1,0:T(8,128)(2,1)}), bf16[8,32,1152]{2,1,0:T(8,128)(2,1)S(1)}, u32[]{:S(2)}, u32[]{:S(2)}) %all-to-all-start) | async-done | bytes 589856 | tf_op jit(solution)/shard_map/all_to_all | solution.py:254
  18.9 1.1 %collective-permute-start = (bf16[256,1152]{1,0:T(8,128)(2,1)S(1)}, bf16[256,1152]{1,0:T(8,128)(2,1)S(1)}, u32[]{:S(2)}, u32[]{:S(2)}) collective-permute-start(bf16[256,1152]{1,0:T(8,128)(2,1)S(1)} %bitcast.6), channel_id=1, source_target_pairs={{0,3},{1,2},{2,1},{3,0},{4,5},{5,4},{6,7},{7,6},{8,11},{9,10},{10,... | collective-permute-start | bytes 1769480 | tf_op jit(solution)/shard_map/ppermute | solution.py:242
  20.0 2.1 %collective-permute-start.2 = (bf16[256,1152]{1,0:T(8,128)(2,1)S(1)}, bf16[256,1152]{1,0:T(8,128)(2,1)}, u32[]{:S(2)}, u32[]{:S(2)}) collective-permute-start(bf16[256,1152]{1,0:T(8,128)(2,1)S(1)} %bitcast.7), channel_id=1, source_target_pairs={{0,96},{1,97},{2,98},{3,99},{4,36},{5,37},{6,38},{7,39},{8,104},{9... | collective-permute-start | bytes 1769480 | tf_op jit(solution)/shard_map/ppermute | solution.py:242
  22.1 3.3 %collective-permute-start.4 = (bf16[256,1152]{1,0:T(8,128)(2,1)S(1)}, bf16[256,1152]{1,0:T(8,128)(2,1)}, u32[]{:S(2)}, u32[]{:S(2)}) collective-permute-start(bf16[256,1152]{1,0:T(8,128)(2,1)S(1)} %bitcast.8), channel_id=1, source_target_pairs={{0,24},{1,25},{2,26},{3,27},{4,12},{5,13},{6,14},{7,15},{8,16},{9,... | collective-permute-start | bytes 1769480 | tf_op jit(solution)/shard_map/ppermute | solution.py:242
  25.4 5.4 %collective-permute-done.refs_1_ = bf16[256,1152]{1,0:T(8,128)(2,1)S(1)} collective-permute-done((bf16[256,1152]{1,0:T(8,128)(2,1)S(1)}, bf16[256,1152]{1,0:T(8,128)(2,1)S(1)}, u32[]{:S(2)}, u32[]{:S(2)}) %collective-permute-start) | collective-permute-done | bytes 589856 | tf_op jit(solution)/shard_map/ppermute | solution.py:242
  30.8 2.0 %collective-permute-start.1 = (bf16[256,1152]{1,0:T(8,128)(2,1)S(1)}, bf16[256,1152]{1,0:T(8,128)(2,1)S(1)}, u32[]{:S(2)}, u32[]{:S(2)}) collective-permute-start(bf16[256,1152]{1,0:T(8,128)(2,1)S(1)} %collective-permute-done.refs_1_), channel_id=1, source_target_pairs={{0,96},{1,97},{2,98},{3,99},{4,36},{5,37},{6,38},{7,39},{8,104},{9... | collective-permute-start | bytes 1769480 | tf_op jit(solution)/shard_map/ppermute | solution.py:242
  32.8 0.8 %copy-done.1 = bf16[256,1152]{1,0:T(8,128)(2,1)} copy-done((bf16[256,1152]{1,0:T(8,128)(2,1)}, bf16[256,1152]{1,0:T(8,128)(2,1)S(1)}, u32[]{:S(2)}) %copy-start.1) | copy-done | bytes 589848
  33.7 1.1 %collective-permute-start.3 = (bf16[256,1152]{1,0:T(8,128)(2,1)}, bf16[256,1152]{1,0:T(8,128)(2,1)}, u32[]{:S(2)}, u32[]{:S(2)}) collective-permute-start(bf16[256,1152]{1,0:T(8,128)(2,1)} %collective-permute-done.2.refs_2_), channel_id=1, source_target_pairs={{0,24},{1,25},{2,26},{3,27},{4,12},{5,13},{6,14},{7,15},{8,16},{9,... | collective-permute-start | bytes 1769480 | tf_op jit(solution)/shard_map/ppermute | solution.py:242
  34.8 2.6 %collective-permute-start.5 = (bf16[256,1152]{1,0:T(8,128)(2,1)}, bf16[256,1152]{1,0:T(8,128)(2,1)}, u32[]{:S(2)}, u32[]{:S(2)}) collective-permute-start(bf16[256,1152]{1,0:T(8,128)(2,1)} %collective-permute-done.4.refs_3_), channel_id=1, source_target_pairs={{0,3},{1,2},{2,1},{3,0},{4,5},{5,4},{6,7},{7,6},{8,11},{9,10},{10,... | collective-permute-start | bytes 1769480 | tf_op jit(solution)/shard_map/ppermute | solution.py:242
  37.4 4.5 %collective-permute-done.1.refs_0_ = bf16[256,1152]{1,0:T(8,128)(2,1)S(1)} collective-permute-done((bf16[256,1152]{1,0:T(8,128)(2,1)S(1)}, bf16[256,1152]{1,0:T(8,128)(2,1)S(1)}, u32[]{:S(2)}, u32[]{:S(2)}) %collective-permute-start.1) | collective-permute-done | bytes 589856 | tf_op jit(solution)/shard_map/ppermute | solution.py:242
  41.9 1.5 %collective-permute-start.6 = (bf16[256,1152]{1,0:T(8,128)(2,1)S(1)}, bf16[256,1152]{1,0:T(8,128)(2,1)}, u32[]{:S(2)}, u32[]{:S(2)}) collective-permute-start(bf16[256,1152]{1,0:T(8,128)(2,1)S(1)} %collective-permute-done.1.refs_0_), channel_id=1, source_target_pairs={{0,24},{1,25},{2,26},{3,27},{4,12},{5,13},{6,14},{7,15},{8,16},{9,... | collective-permute-start | bytes 1769480 | tf_op jit(solution)/shard_map/ppermute | solution.py:242
  43.4 0.4 collective-permute-start.8
  43.7 0.7 dynamic-slice_bitcast_fusion.refs_8_
  44.4 0.3 collective-permute-done.8.sibling_valid_ref
  44.7 1.6 %copy-done = bf16[4,256,1024]{2,1,0:T(8,128)(2,1)S(1)} copy-done((bf16[4,256,1024]{2,1,0:T(8,128)(2,1)S(1)}, bf16[4,256,1024]{2,1,0:T(8,128)(2,1)}, u32[]{:S(2)}) %copy-start) | copy-done | bytes 2097176
  46.3 0.7 copy-done.5
  47.0 1.5 %norms.1.refs_6_ = f32[256,128]{1,0:T(8,128)S(1)} custom-call(bf16[4,256,1024]{2,1,0:T(8,128)(2,1)S(1)} %copy-done, bf16[4,256,1024]{2,1,0:T(8,128)(2,1)S(1)} %collective-permute-done.7.sibling_ref.refs_5_, s32[4]{0:T(128)S(1)} %copy-done.5, s32[4]{0:T(128)S(1)} %collective-permute-done.8.sibling_valid_ref), custom_call_target="tpu_custom_call" | custom-call | tf_op jit(solution)/shard_map/norms/pallas_call | solution.py:262
  48.5 6.4 %score_first.1.refs_7_ = f32[256,128]{1,0:T(8,128)S(1)} custom-call(bf16[256,1152]{1,0:T(8,128)(2,1)S(1)} %bitcast.9, bf16[256,1152]{1,0:T(8,128)(2,1)S(1)} %copy-done.2, bf16[256,1152]{1,0:T(8,128)(2,1)} %collective-permute-done.2.refs_2_, bf16[256,1152]{1,0:T(8,128)(2,1)} %collective-permute-done.4.refs_3_, bf16[4,256,1024]{2,1,0:T(8,128)(2,1)S(1)} %copy-done, ...), custom_call_target="tpu_custom_call" | custom-call | tf_op jit(solution)/shard_map/score_first/pallas_call | solution.py:279
  54.8 0.0 copy-start.6
  54.9 7.8 %score_second.1 = f32[64,8,128]{2,1,0:T(8,128)} custom-call(bf16[256,1152]{1,0:T(8,128)(2,1)S(1)} %collective-permute-done.1.refs_0_, bf16[256,1152]{1,0:T(8,128)(2,1)} %collective-permute-done.3.refs_1_, bf16[256,1152]{1,0:T(8,128)(2,1)} %collective-permute-done.5.refs_2_, bf16[256,1152]{1,0:T(8,128)(2,1)} %collective-permute-done.6.refs_3_, ...), custom_call_target="tpu_custom_call" | custom-call | tf_op jit(solution)/shard_map/score_second/pallas_call | solution.py:283
  62.7 6.4 %all-to-all-start.1 = ((f32[64,8,128]{2,1,0:T(8,128)}), f32[64,8,128]{2,1,0:T(8,128)S(1)}, u32[]{:S(2)}, u32[]{:S(2)}) async-start(f32[64,8,128]{2,1,0:T(8,128)} %score_second.1), calls=%async_computation.1 | async-start | bytes 524288 | tf_op jit(solution)/shard_map/all_to_all | solution.py:287
  69.2 0.6 reshape.16.flat_ref
  69.8 1.9 %wanted.1 = (bf16[128,256]{1,0:T(8,128)(2,1)}, s32[8,256]{1,0:T(8,128)}) custom-call(s32[32,8]{1,0:T(8,128)} %copy.7.probes_ref, s32[1,256]{1,0:T(1,128)} %reshape.16.flat_ref, s32[1,128]{1,0:T(1,128)} %bitcast.13), custom_call_target="tpu_custom_call" | custom-call | tf_op jit(solution)/shard_map/wanted/pallas_call | solution.py:266
  71.7 8.4 %all-to-all-done.1 = f32[64,8,128]{2,1,0:T(8,128)S(1)} async-done(((f32[64,8,128]{2,1,0:T(8,128)}), f32[64,8,128]{2,1,0:T(8,128)S(1)}, u32[]{:S(2)}, u32[]{:S(2)}) %all-to-all-start.1) | async-done | bytes 262176 | tf_op jit(solution)/shard_map/all_to_all | solution.py:287
  80.1 0.8 %copy-done.3 = bf16[128,256]{1,0:T(8,128)(2,1)S(1)} copy-done((bf16[128,256]{1,0:T(8,128)(2,1)S(1)}, bf16[128,256]{1,0:T(8,128)(2,1)}, u32[]{:S(2)}) %copy-start.3) | copy-done | bytes 65560
  80.9 0.7 copy-done.4
  81.6 1.4 %final.1 = f32[32,32]{1,0:T(8,128)} custom-call(f32[16,4,8,128]{3,2,1,0:T(8,128)S(1)} %bitcast.10, bf16[128,256]{1,0:T(8,128)(2,1)S(1)} %copy-done.3, s32[8,256]{1,0:T(8,128)S(1)} %copy-done.4), custom_call_target="tpu_custom_call" | custom-call | tf_op jit(solution)/shard_map/final/pallas_call | solution.py:288
  (14 shorter events, 0.0 us)
Async XLA Ops:
  5.0 13.9 %all-to-all-start = ((bf16[8,32,1152]{2,1,0:T(8,128)(2,1)}), bf16[8,32,1152]{2,1,0:T(8,128)(2,1)S(1)}, u32[]{:S(2)}, u32[]{:S(2)}) async-start(bf16[8,32,1152]{2,1,0:T(8,128)(2,1)} %broadcast_in_dim.2), calls=%async_computation | async-start | bytes 1179648 | tf_op jit(solution)/shard_map/all_to_all | solution.py:254
  10.2 34.5 %collective-permute-start.7 = (bf16[4,256,1024]{2,1,0:T(8,128)(2,1)}, bf16[4,256,1024]{2,1,0:T(8,128)(2,1)S(1)}, u32[]{:S(2)}, u32[]{:S(2)}) collective-permute-start(bf16[4,256,1024]{2,1,0:T(8,128)(2,1)} %refs_4_.3), channel_id=1, source_target_pairs={{0,4},{1,5},{2,6},{3,7},{4,0},{5,1},{6,2},{7,3},{8,12},{9,13},{10,... | collective-permute-start | bytes 6291464 | tf_op jit(solution)/shard_map/ppermute | solution.py:248
  18.9 11.9 %collective-permute-start = (bf16[256,1152]{1,0:T(8,128)(2,1)S(1)}, bf16[256,1152]{1,0:T(8,128)(2,1)S(1)}, u32[]{:S(2)}, u32[]{:S(2)}) collective-permute-start(bf16[256,1152]{1,0:T(8,128)(2,1)S(1)} %bitcast.6), channel_id=1, source_target_pairs={{0,3},{1,2},{2,1},{3,0},{4,5},{5,4},{6,7},{7,6},{8,11},{9,10},{10,... | collective-permute-start | bytes 1769480 | tf_op jit(solution)/shard_map/ppermute | solution.py:242
  20.0 13.7 %collective-permute-start.2 = (bf16[256,1152]{1,0:T(8,128)(2,1)S(1)}, bf16[256,1152]{1,0:T(8,128)(2,1)}, u32[]{:S(2)}, u32[]{:S(2)}) collective-permute-start(bf16[256,1152]{1,0:T(8,128)(2,1)S(1)} %bitcast.7), channel_id=1, source_target_pairs={{0,96},{1,97},{2,98},{3,99},{4,36},{5,37},{6,38},{7,39},{8,104},{9... | collective-permute-start | bytes 1769480 | tf_op jit(solution)/shard_map/ppermute | solution.py:242
  22.1 12.6 %collective-permute-start.4 = (bf16[256,1152]{1,0:T(8,128)(2,1)S(1)}, bf16[256,1152]{1,0:T(8,128)(2,1)}, u32[]{:S(2)}, u32[]{:S(2)}) collective-permute-start(bf16[256,1152]{1,0:T(8,128)(2,1)S(1)} %bitcast.8), channel_id=1, source_target_pairs={{0,24},{1,25},{2,26},{3,27},{4,12},{5,13},{6,14},{7,15},{8,16},{9,... | collective-permute-start | bytes 1769480 | tf_op jit(solution)/shard_map/ppermute | solution.py:242
  30.8 11.1 %collective-permute-start.1 = (bf16[256,1152]{1,0:T(8,128)(2,1)S(1)}, bf16[256,1152]{1,0:T(8,128)(2,1)S(1)}, u32[]{:S(2)}, u32[]{:S(2)}) collective-permute-start(bf16[256,1152]{1,0:T(8,128)(2,1)S(1)} %collective-permute-done.refs_1_), channel_id=1, source_target_pairs={{0,96},{1,97},{2,98},{3,99},{4,36},{5,37},{6,38},{7,39},{8,104},{9... | collective-permute-start | bytes 1769480 | tf_op jit(solution)/shard_map/ppermute | solution.py:242
  32.8 0.8 %copy-start.1 = (bf16[256,1152]{1,0:T(8,128)(2,1)}, bf16[256,1152]{1,0:T(8,128)(2,1)S(1)}, u32[]{:S(2)}) copy-start(bf16[256,1152]{1,0:T(8,128)(2,1)S(1)} %collective-permute-done.refs_1_) | copy-start | bytes 1769476
  33.7 21.2 %collective-permute-start.3 = (bf16[256,1152]{1,0:T(8,128)(2,1)}, bf16[256,1152]{1,0:T(8,128)(2,1)}, u32[]{:S(2)}, u32[]{:S(2)}) collective-permute-start(bf16[256,1152]{1,0:T(8,128)(2,1)} %collective-permute-done.2.refs_2_), channel_id=1, source_target_pairs={{0,24},{1,25},{2,26},{3,27},{4,12},{5,13},{6,14},{7,15},{8,16},{9,... | collective-permute-start | bytes 1769480 | tf_op jit(solution)/shard_map/ppermute | solution.py:242
  34.8 20.1 %collective-permute-start.5 = (bf16[256,1152]{1,0:T(8,128)(2,1)}, bf16[256,1152]{1,0:T(8,128)(2,1)}, u32[]{:S(2)}, u32[]{:S(2)}) collective-permute-start(bf16[256,1152]{1,0:T(8,128)(2,1)} %collective-permute-done.4.refs_3_), channel_id=1, source_target_pairs={{0,3},{1,2},{2,1},{3,0},{4,5},{5,4},{6,7},{7,6},{8,11},{9,10},{10,... | collective-permute-start | bytes 1769480 | tf_op jit(solution)/shard_map/ppermute | solution.py:242
  41.9 13.0 %collective-permute-start.6 = (bf16[256,1152]{1,0:T(8,128)(2,1)S(1)}, bf16[256,1152]{1,0:T(8,128)(2,1)}, u32[]{:S(2)}, u32[]{:S(2)}) collective-permute-start(bf16[256,1152]{1,0:T(8,128)(2,1)S(1)} %collective-permute-done.1.refs_0_), channel_id=1, source_target_pairs={{0,24},{1,25},{2,26},{3,27},{4,12},{5,13},{6,14},{7,15},{8,16},{9,... | collective-permute-start | bytes 1769480 | tf_op jit(solution)/shard_map/ppermute | solution.py:242
  43.4 1.3 %collective-permute-start.8 = (s32[4]{0:T(128)}, s32[4]{0:T(128)S(1)}, u32[]{:S(2)}, u32[]{:S(2)}) collective-permute-start(s32[4]{0:T(128)} %own_valid_ref.1), channel_id=1, source_target_pairs={{0,4},{1,5},{2,6},{3,7},{4,0},{5,1},{6,2},{7,3},{8,12},{9,13},{10,... | collective-permute-start | bytes 56 | tf_op jit(solution)/shard_map/ppermute | solution.py:249
  44.7 1.6 %copy-start = (bf16[4,256,1024]{2,1,0:T(8,128)(2,1)S(1)}, bf16[4,256,1024]{2,1,0:T(8,128)(2,1)}, u32[]{:S(2)}) copy-start(bf16[4,256,1024]{2,1,0:T(8,128)(2,1)} %refs_4_.3) | copy-start | bytes 6291460
  46.3 0.7 copy-start.5
  47.0 1.5 %copy-start.2 = (bf16[256,1152]{1,0:T(8,128)(2,1)S(1)}, bf16[256,1152]{1,0:T(8,128)(2,1)}, u32[]{:S(2)}) copy-start(bf16[256,1152]{1,0:T(8,128)(2,1)} %copy-done.1) | copy-start | bytes 1769476
  54.8 14.3 %copy-start.6 = (s32[32,8]{0,1:T(8,128)S(1)}, s32[32,8]{0,1:T(8,128)}, u32[]{:S(2)}) copy-start(s32[32,8]{0,1:T(8,128)} %param.7) | copy-start | bytes 3076
  62.7 17.4 %all-to-all-start.1 = ((f32[64,8,128]{2,1,0:T(8,128)}), f32[64,8,128]{2,1,0:T(8,128)S(1)}, u32[]{:S(2)}, u32[]{:S(2)}) async-start(f32[64,8,128]{2,1,0:T(8,128)} %score_second.1), calls=%async_computation.1 | async-start | bytes 524288 | tf_op jit(solution)/shard_map/all_to_all | solution.py:287
  80.1 0.8 %copy-start.3 = (bf16[128,256]{1,0:T(8,128)(2,1)S(1)}, bf16[128,256]{1,0:T(8,128)(2,1)}, u32[]{:S(2)}) copy-start(bf16[128,256]{1,0:T(8,128)(2,1)} %get-tuple-element.7.pick_ref) | copy-start | bytes 196612
  80.9 0.7 copy-start.4

commit v2 on v1

--- a/solution.py
+++ b/solution.py
@@ -51,6 +51,9 @@
 CORE_SWAP = [(device, device ^ 4) for device in range(N_DEV)]
 FIRST_HALF = (0, 1, 2, 4)
 SECOND_HALF = (3, 6, 5, 7)
+
+
+THIRDS = ((0, 96), (96, 176), (176, 256))
 
 
 def block_places():
@@ -106,35 +109,33 @@
 
 
 def rank_table(probes_ref, place):
-    probes = probes_ref[...]
-    lists = lax.broadcasted_iota(jnp.int32, (32, 128), 1)
-    named = jnp.zeros((32, 128), F32)
+    lists = lax.broadcasted_iota(jnp.int32, (128, 32), 0)
+    named = jnp.zeros((128, 32), F32)
     for j in range(8):
-        named = jnp.where(probes[:, j : j + 1] == lists, 1.0, named)
-    probed = lax.dot_general(named.astype(BF16), place, (((1,), (1,)), ((), ())), preferred_element_type=F32)
-    before = lax.broadcasted_iota(jnp.int32, (32, 32), 1) < lax.broadcasted_iota(jnp.int32, (32, 32), 0)
-    rank = jnp.dot(before.astype(BF16), probed.astype(BF16), preferred_element_type=F32)
-    return jnp.where(probed > 0.5, rank, -1.0).astype(BF16)
+        named = jnp.where(probes_ref[j : j + 1, :] == lists, 1.0, named)
+    probed = jnp.dot(place, named.astype(BF16), preferred_element_type=F32)
+    before = lax.broadcasted_iota(jnp.int32, (32, 32), 0) < lax.broadcasted_iota(jnp.int32, (32, 32), 1)
+    rank = jnp.dot(probed.astype(BF16), before.astype(BF16), preferred_element_type=F32)
+    return jnp.where(probed > 0.5, rank, -1.0)
 
 
 def widen_kernel(queries_ref, probes_ref, slot_ref, out_ref):
-    out_ref[:, :D] = queries_ref[...]
-    out_ref[:, D:] = rank_table(probes_ref, place_matrix(slot_ref))
-
-
-def wanted_kernel(probes_ref, flat_ref, slot_ref, pick_ref, group_ref):
+    table = rank_table(probes_ref, place_matrix(slot_ref)).T.astype(BF16)
+    for copy in range(8):
+        out_ref[copy, :, :D] = queries_ref[...]
+        out_ref[copy, :, D:] = table
+
+
+def wanted_kernel(probes_ref, slot_ref, pick_ref, group_ref):
     place = place_matrix(slot_ref)
     rank = rank_table(probes_ref, place)
-    named = (flat_ref[...] == lax.broadcasted_iota(jnp.int32, (128, 256), 0)).astype(BF16)
-    placed = jnp.dot(place, named, preferred_element_type=F32)
-    index = lax.broadcasted_iota(jnp.int32, (128, 256), 0)
-    where = jnp.sum(placed * index.astype(F32), 0, keepdims=True).astype(jnp.int32)
-    ranks = jnp.dot(rank, placed.astype(BF16), preferred_element_type=F32)
-    own = lax.broadcasted_iota(jnp.int32, (32, 256), 0) == (lax.broadcasted_iota(jnp.int32, (32, 256), 1) & 31)
-    slot = jnp.sum(jnp.where(own, ranks, 0.0), 0, keepdims=True).astype(jnp.int32)
-    row = (where >> 2) * 4 + slot
-    pick_ref[...] = (index == row).astype(BF16)
-    group_ref[...] = jnp.broadcast_to(where & 3, (8, 256))
+    index = lax.broadcasted_iota(jnp.int32, (128, 32), 0)
+    for j in range(8):
+        placed = jnp.dot(place, (probes_ref[j : j + 1, :] == index).astype(BF16), preferred_element_type=F32)
+        where = jnp.sum(placed * index.astype(F32), 0, keepdims=True).astype(jnp.int32)
+        slot = jnp.sum(placed * rank, 0, keepdims=True).astype(jnp.int32)
+        pick_ref[:, 32 * j : 32 * j + 32] = (index == (where >> 2) * 4 + slot).astype(BF16)
+        group_ref[:, 32 * j : 32 * j + 32] = jnp.broadcast_to(where & 3, (8, 32))
 
 
 def norm_kernel(own_ref, sibling_ref, own_valid_ref, sibling_valid_ref, out_ref):
@@ -150,15 +151,7 @@
     out_ref[...] = total
 
 
-def score_lists(group_refs, own_ref, sibling_ref, norm_ref, block_ref, query_buf, list_buf, chosen, best, sems):
-    copies = []
-    for g, ref in enumerate(group_refs):
-        copies.append(pltpu.make_async_copy(ref, query_buf.at[g], sems.at[g]))
-    for t in range(8):
-        source = own_ref.at[t] if t < 4 else sibling_ref.at[t - 4]
-        copies.append(pltpu.make_async_copy(source, list_buf.at[t], sems.at[4 + t]))
-    for copy in copies:
-        copy.start()
+def score_lists(group_refs, own_ref, sibling_ref, norm_ref, block_ref, chosen, best):
     chip = lax.axis_index("owner") // 2
     column = lax.broadcasted_iota(jnp.int32, (256, 128), 0)
     wanted = (lax.broadcasted_iota(jnp.int32, (256, 128), 1) == chip * 8 + (column >> 5)).astype(BF16)
@@ -166,16 +159,16 @@
     same_block = (lax.broadcasted_iota(jnp.int32, (256, 256), 1) >> 5) == (column & 7)
     column_rank = ((column >> 3) & 3).astype(F32)
     for g in range(4):
-        copies[g].wait()
-        rank = lax.dot_general(wanted, query_buf[g, :, D:], (((1,), (1,)), ((), ())), preferred_element_type=F32)
+        ref = group_refs[g]
+        rank = lax.dot_general(wanted, ref[:, D:], (((1,), (1,)), ((), ())), preferred_element_type=F32)
         pick = (same_block & (rank == column_rank)).astype(BF16)
-        picked = jnp.dot(pick, query_buf[g, :, :D], preferred_element_type=F32).astype(BF16)
+        picked = jnp.dot(pick, ref[:, :D], preferred_element_type=F32).astype(BF16)
         for t in range(8):
             chosen[t, 32 * g : 32 * g + 32, :] = picked[32 * t : 32 * t + 32]
 
     def sorted_list(t):
-        copies[4 + t].wait()
-        scores = lax.dot_general(list_buf[t], chosen[t], (((1,), (1,)), ((), ())), preferred_element_type=F32)
+        rows = own_ref[t] if t < 4 else sibling_ref[t - 4]
+        scores = lax.dot_general(rows, chosen[t], (((1,), (1,)), ((), ())), preferred_element_type=F32)
         scores = scores - norm_ref[:, t : t + 1]
         return exchange([scores[8 * i : 8 * i + 8] for i in range(TOPK)], SORT_PAIRS)
 
@@ -199,8 +192,10 @@
 
 
 def second_kernel(*refs):
-    groups, (own, sibling, norm, earlier, place_ref, out, block_buf), scratch = refs[:4], refs[4:11], refs[11:]
-    score_lists(groups, own, sibling, norm, block_buf, *scratch)
+    groups, pieces, (own, sibling, norm, earlier, place_ref, out, last, block_buf), scratch = refs[:3], refs[3:6], refs[6:14], refs[14:]
+    for piece, (start, stop) in zip(pieces, THIRDS):
+        last[start:stop, :] = piece[...]
+    score_lists(groups + (last,), own, sibling, norm, block_buf, *scratch)
     for b in range(32):
         out[place_ref[b]] = earlier[8 * b : 8 * b + 8, :]
         out[place_ref[32 + b]] = block_buf[8 * b : 8 * b + 8, :]
@@ -230,7 +225,7 @@
 
 
 def params():
-    return pltpu.CompilerParams(vmem_limit_bytes=40 * 1024 * 1024)
+    return pltpu.CompilerParams(vmem_limit_bytes=20 * 1024 * 1024)
 
 
 def spaces(text):
@@ -245,45 +240,44 @@
 def per_device(queries, probes, list_slot, valid_rows, database):
     shape = jax.ShapeDtypeStruct
     slots = list_slot.reshape(1, 128)
+    probes = probes.T
+    wide = pl.pallas_call(
+        widen_kernel, out_shape=shape((8, 32, WIDE), BF16), in_specs=spaces("vvv"), out_specs=spaces("v")[0], name="widen"
+    )(queries, probes, slots)
+    near = lax.all_to_all(wide, AXES, 0, 0, axis_index_groups=NEAR_GROUPS, tiled=True).reshape(256, WIDE)
     sibling = lax.ppermute(database, AXES, CORE_SWAP)
     sibling_valid = lax.ppermute(valid_rows, AXES, CORE_SWAP)
-    wide = pl.pallas_call(
-        widen_kernel, out_shape=shape((32, WIDE), BF16), in_specs=spaces("vvv"), out_specs=spaces("v")[0], name="widen"
-    )(queries, probes, slots)
-    copies = jnp.broadcast_to(wide[None], (8, 32, WIDE))
-    near = lax.all_to_all(copies, AXES, 0, 0, axis_index_groups=NEAR_GROUPS, tiled=True).reshape(256, WIDE)
+    pick, group = pl.pallas_call(
+        wanted_kernel, out_shape=(shape((128, 256), BF16), shape((8, 256), jnp.int32)), in_specs=spaces("vv"),
+        out_specs=spaces("vv"), name="wanted",
+    )(probes, slots)
+    places = jnp.asarray(block_places())[lax.axis_index(AXES)]
+    near, pick, group, places = lax.optimization_barrier((near, pick, group, places))
+
     gathered = {0: near}
     for mask in (1, 2, 4):
         gathered[mask] = hop(near, mask)
-    for mask, source, step in ((3, 1, 2), (6, 2, 4), (5, 4, 1)):
-        gathered[mask] = hop(gathered[source], step)
-    gathered[7] = hop(gathered[3], 4)
-
     norms = pl.pallas_call(
         norm_kernel, out_shape=shape((256, 128), F32), in_specs=spaces("vvss"), out_specs=spaces("v")[0], name="norms",
         compiler_params=params(),
     )(database, sibling, valid_rows, sibling_valid)
-    pick, group = pl.pallas_call(
-        wanted_kernel, out_shape=(shape((128, 256), BF16), shape((8, 256), jnp.int32)), in_specs=spaces("vvv"),
-        out_specs=spaces("vv"), name="wanted",
-    )(probes, probes.T.reshape(1, 256), slots)
-    places = jnp.asarray(block_places())[lax.axis_index(AXES)]
-
-    scratch = [
-        pltpu.VMEM((4, 256, WIDE), BF16),
-        pltpu.VMEM((8, 256, D), BF16),
-        pltpu.VMEM((8, 128, D), BF16),
-        pltpu.VMEM((256, 128), F32),
-        pltpu.SemaphoreType.DMA((12,)),
-    ]
+    gathered[1], gathered[2], gathered[4], norms = lax.optimization_barrier((gathered[1], gathered[2], gathered[4], norms))
+
+    for mask, source, step in ((3, 1, 2), (6, 2, 4), (5, 4, 1)):
+        gathered[mask] = hop(gathered[source], step)
+    scratch = [pltpu.VMEM((8, 128, D), BF16), pltpu.VMEM((256, 128), F32)]
     early = pl.pallas_call(
-        first_kernel, out_shape=shape((256, 128), F32), in_specs=spaces("aaaaaav"), out_specs=spaces("v")[0],
+        first_kernel, out_shape=shape((256, 128), F32), in_specs=spaces("vvvvvvv"), out_specs=spaces("v")[0],
         scratch_shapes=scratch, compiler_params=params(), name="score_first",
     )(*[gathered[mask] for mask in FIRST_HALF], database, sibling, norms)
+    gathered[3], gathered[6], gathered[5], early = lax.optimization_barrier((gathered[3], gathered[6], gathered[5], early))
+
+    last = [hop(gathered[source][start:stop], step) for (source, step), (start, stop) in zip(((3, 4), (6, 1), (5, 2)), THIRDS)]
     blocks = pl.pallas_call(
-        second_kernel, out_shape=shape((N_CORE, 8, 128), F32), in_specs=spaces("aaaaaavvs"), out_specs=spaces("v")[0],
-        scratch_shapes=[pltpu.VMEM((256, 128), F32)] + scratch, compiler_params=params(), name="score_second",
-    )(*[gathered[mask] for mask in SECOND_HALF], database, sibling, norms, early, places)
+        second_kernel, out_shape=shape((N_CORE, 8, 128), F32), in_specs=spaces("vvvvvvvvvvs"), out_specs=spaces("v")[0],
+        scratch_shapes=[pltpu.VMEM((256, WIDE), BF16), pltpu.VMEM((256, 128), F32)] + scratch,
+        compiler_params=params(), name="score_second",
+    )(*[gathered[mask] for mask in SECOND_HALF[:3]], *last, database, sibling, norms, early, places)
     back = lax.all_to_all(blocks, AXES, 0, 0, axis_index_groups=CORE_GROUPS, tiled=True)
     return pl.pallas_call(
         final_kernel, out_shape=shape((32, TOPK), F32), in_specs=spaces("vvv"), out_specs=spaces("v")[0],

time: 83.6 us -> 76.9 us (0.920)
  blocking collectives: 0 us -> 15.9 us
  Pallas kernels: 20.8 us -> 13.5 us
  local copies, waits for them, and re-layouts: 9.05 us -> 3 us
  starting transfers between devices: 30.1 us -> 24.1 us
  waiting for transfers between devices: 22.9 us -> 20 us
    all_to_all x0 -> x1, blocking collectives: none -> 15.9 us  [per_device(): lax.all_to_all(blocks, AXES, 0, 0, axis_index_groups=CORE_GROUPS, tiled=T...]
    all_to_all x2 -> x1, waiting for transfers between devices: 12.7 us -> 6.18 us  [per_device(): lax.all_to_all(wide, AXES, 0, 0, axis_index_groups=NEAR_GROUPS, tiled=True)]
    all_to_all x2 -> x1, starting transfers between devices: 11.6 us -> 5.22 us  [per_device(): lax.all_to_all(wide, AXES, 0, 0, axis_index_groups=NEAR_GROUPS, tiled=True)]
    ppermute x1, starting transfers between devices: 4.38 us -> 0.01 us  [per_device(): sibling = lax.ppermute(database, AXES, CORE_SWAP)]
    pallas_call x1, Pallas kernels: 7.82 us -> 3.67 us  [per_device(): pl.pallas_call(second_kernel, out_shape=shape((N_CORE, 8, 128), F32), in_...]
    unnamed x15 -> x8, local copies, waits for them, and re-layouts: 5.99 us -> 2.26 us
    pallas_call x1, Pallas kernels: 6.38 us -> 3.09 us  [per_device(): pl.pallas_call(first_kernel, out_shape=shape((256, 128), F32), in_specs=s...]
    ppermute x7 -> x9, starting transfers between devices: 13.7 us -> 17 us  [hop(): lax.ppermute(value, AXES, [(device, far(device, mask, False)) for device...]
  transfers between devices with their start and end apart: 11 -> 12, of which waited for: 5 -> 8; matrix products, arithmetic and copies ran while one was open for 2% -> 1% of each run, Pallas kernels for 12% -> 11%
where the time goes in v2:
time: 76.9 us; the launch traced here: 76.6 us
  starting transfers between devices  24.1 us (31%)
  waiting for transfers between devices  20 us (26%)
  blocking collectives  15.9 us (21%)
  Pallas kernels  13.5 us (18%)
  local copies, waits for them, and re-layouts  3 us (4%)
    ppermute x9, starting transfers between devices, hop(): lax.ppermute(value, AXES, [(device, far(device, mask, False)) for device...  17 us
    all_to_all x1, blocking collectives, per_device(): lax.all_to_all(blocks, AXES, 0, 0, axis_index_groups=CORE_GROUPS, tiled=T...  15.9 us
    ppermute x9, waiting for transfers between devices, hop(): lax.ppermute(value, AXES, [(device, far(device, mask, False)) for device...  12.8 us
    all_to_all x1, waiting for transfers between devices, per_device(): lax.all_to_all(wide, AXES, 0, 0, axis_index_groups=NEAR_GROUPS, tiled=True)  6.18 us
    all_to_all x1, starting transfers between devices, per_device(): lax.all_to_all(wide, AXES, 0, 0, axis_index_groups=NEAR_GROUPS, tiled=True)  5.22 us
    pallas_call x1, Pallas kernels, per_device(): pl.pallas_call(second_kernel, out_shape=shape((N_CORE, 8, 128), F32), in_...  3.67 us
    pallas_call x1, Pallas kernels, per_device(): pl.pallas_call(first_kernel, out_shape=shape((256, 128), F32), in_specs=s...  3.09 us
    unnamed x8, local copies, waits for them, and re-layouts  2.26 us
  transfers between devices with their start and end apart: 12, of which 8 were waited for; matrix products, arithmetic and copies ran while one was open for 1% of the time, Pallas kernels for 11%

profile of v2, /device:TPU:0, one launch (start us, length us, event | category | flops | bytes accessed | tf_op | source)
XLA Modules:
  0.0 76.6 jit_solution(12152784975395418714)
XLA Ops:
  0.0 0.0 collective-permute-start.3
  0.0 2.0 %widen.1 = bf16[8,32,1152]{2,1,0:T(8,128)(2,1)} custom-call(bf16[32,1024]{1,0:T(8,128)(2,1)} %queries_ref.1, s32[8,32]{1,0:T(8,128)} %bitcast.11, s32[1,128]{1,0:T(1,128)} %bitcast.13), custom_call_target="tpu_custom_call" | custom-call | tf_op jit(solution)/shard_map/widen/pallas_call | solution.py:244
  2.0 5.2 %all-to-all-start = ((bf16[8,32,1152]{2,1,0:T(8,128)(2,1)}), bf16[8,32,1152]{2,1,0:T(8,128)(2,1)S(1)}, u32[]{:S(2)}, u32[]{:S(2)}) async-start(bf16[8,32,1152]{2,1,0:T(8,128)(2,1)} %widen.1), calls=%async_computation | async-start | bytes 1179648 | tf_op jit(solution)/shard_map/all_to_all | solution.py:247
  7.3 1.9 %wanted.1 = (bf16[128,256]{1,0:T(8,128)(2,1)}, s32[8,256]{1,0:T(8,128)}) custom-call(s32[8,32]{1,0:T(8,128)} %bitcast.12, s32[1,128]{1,0:T(1,128)} %bitcast.14), custom_call_target="tpu_custom_call" | custom-call | tf_op jit(solution)/shard_map/wanted/pallas_call | solution.py:250
  9.1 0.7 dynamic-slice_bitcast_fusion.refs_10_
  9.8 6.2 %all-to-all-done = bf16[8,32,1152]{2,1,0:T(8,128)(2,1)S(1)} async-done(((bf16[8,32,1152]{2,1,0:T(8,128)(2,1)}), bf16[8,32,1152]{2,1,0:T(8,128)(2,1)S(1)}, u32[]{:S(2)}, u32[]{:S(2)}) %all-to-all-start) | async-done | bytes 589856 | tf_op jit(solution)/shard_map/all_to_all | solution.py:247
  16.0 1.8 %collective-permute-start.2 = (bf16[256,1152]{1,0:T(8,128)(2,1)S(1)}, bf16[256,1152]{1,0:T(8,128)(2,1)S(1)}, u32[]{:S(2)}, u32[]{:S(2)}) collective-permute-start(bf16[256,1152]{1,0:T(8,128)(2,1)S(1)} %bitcast.6), channel_id=1, source_target_pairs={{0,24},{1,25},{2,26},{3,27},{4,12},{5,13},{6,14},{7,15},{8,16},{9,... | collective-permute-start | bytes 1769480 | tf_op jit(solution)/shard_map/ppermute | solution.py:237
  17.8 2.1 %collective-permute-start.1 = (bf16[256,1152]{1,0:T(8,128)(2,1)S(1)}, bf16[256,1152]{1,0:T(8,128)(2,1)S(1)}, u32[]{:S(2)}, u32[]{:S(2)}) collective-permute-start(bf16[256,1152]{1,0:T(8,128)(2,1)S(1)} %bitcast.7), channel_id=1, source_target_pairs={{0,96},{1,97},{2,98},{3,99},{4,36},{5,37},{6,38},{7,39},{8,104},{9... | collective-permute-start | bytes 1769480 | tf_op jit(solution)/shard_map/ppermute | solution.py:237
  19.9 2.6 %collective-permute-start = (bf16[256,1152]{1,0:T(8,128)(2,1)S(1)}, bf16[256,1152]{1,0:T(8,128)(2,1)S(1)}, u32[]{:S(2)}, u32[]{:S(2)}) collective-permute-start(bf16[256,1152]{1,0:T(8,128)(2,1)S(1)} %bitcast.8), channel_id=1, source_target_pairs={{0,3},{1,2},{2,1},{3,0},{4,5},{5,4},{6,7},{7,6},{8,11},{9,10},{10,... | collective-permute-start | bytes 1769480 | tf_op jit(solution)/shard_map/ppermute | solution.py:237
  22.5 1.8 %collective-permute-start.4 = (s32[4]{0:T(128)}, s32[4]{0:T(128)S(1)}, u32[]{:S(2)}, u32[]{:S(2)}) collective-permute-start(s32[4]{0:T(128)} %own_valid_ref.1), channel_id=1, source_target_pairs={{0,4},{1,5},{2,6},{3,7},{4,0},{5,1},{6,2},{7,3},{8,12},{9,13},{10,... | collective-permute-start | bytes 56 | tf_op jit(solution)/shard_map/ppermute | solution.py:249
  24.3 1.0 %collective-permute-done.4.sibling_valid_ref = s32[4]{0:T(128)S(1)} collective-permute-done((s32[4]{0:T(128)}, s32[4]{0:T(128)S(1)}, u32[]{:S(2)}, u32[]{:S(2)}) %collective-permute-start.4) | collective-permute-done | bytes 48 | tf_op jit(solution)/shard_map/ppermute | solution.py:249
  25.3 0.0 collective-permute-done.3.sibling_ref.refs_5_.refs_7_
  25.3 1.6 %copy-done = bf16[4,256,1024]{2,1,0:T(8,128)(2,1)S(1)} copy-done((bf16[4,256,1024]{2,1,0:T(8,128)(2,1)S(1)}, bf16[4,256,1024]{2,1,0:T(8,128)(2,1)}, u32[]{:S(2)}) %copy-start) | copy-done | bytes 2097176
  26.9 0.7 copy-done.3
  27.5 1.5 %norms.1.refs_6_.refs_8_ = f32[256,128]{1,0:T(8,128)S(1)} custom-call(bf16[4,256,1024]{2,1,0:T(8,128)(2,1)S(1)} %copy-done, bf16[4,256,1024]{2,1,0:T(8,128)(2,1)S(1)} %collective-permute-done.3.sibling_ref.refs_5_.refs_7_, s32[4]{0:T(128)S(1)} %copy-done.3, s32[4]{0:T(128)S(1)} %collective-permute-done.4.sibling_valid_ref), custom_call_target="tpu_custom_call" | custom-call | tf_op jit(solution)/shard_map/norms/pallas_call | solution.py:260
  29.0 2.0 %collective-permute-done.refs_1_ = bf16[256,1152]{1,0:T(8,128)(2,1)S(1)} collective-permute-done((bf16[256,1152]{1,0:T(8,128)(2,1)S(1)}, bf16[256,1152]{1,0:T(8,128)(2,1)S(1)}, u32[]{:S(2)}, u32[]{:S(2)}) %collective-permute-start) | collective-permute-done | bytes 589856 | tf_op jit(solution)/shard_map/ppermute | solution.py:237
  31.0 1.1 %collective-permute-start.5 = (bf16[256,1152]{1,0:T(8,128)(2,1)S(1)}, bf16[256,1152]{1,0:T(8,128)(2,1)S(1)}, u32[]{:S(2)}, u32[]{:S(2)}) collective-permute-start(bf16[256,1152]{1,0:T(8,128)(2,1)S(1)} %collective-permute-done.refs_1_), channel_id=1, source_target_pairs={{0,96},{1,97},{2,98},{3,99},{4,36},{5,37},{6,38},{7,39},{8,104},{9... | collective-permute-start | bytes 1769480 | tf_op jit(solution)/shard_map/ppermute | solution.py:237
  32.1 1.4 %collective-permute-start.6 = (bf16[256,1152]{1,0:T(8,128)(2,1)S(1)}, bf16[256,1152]{1,0:T(8,128)(2,1)S(1)}, u32[]{:S(2)}, u32[]{:S(2)}) collective-permute-start(bf16[256,1152]{1,0:T(8,128)(2,1)S(1)} %collective-permute-done.1.refs_2_), channel_id=1, source_target_pairs={{0,24},{1,25},{2,26},{3,27},{4,12},{5,13},{6,14},{7,15},{8,16},{9,... | collective-permute-start | bytes 1769480 | tf_op jit(solution)/shard_map/ppermute | solution.py:237
  33.6 1.3 %collective-permute-start.7 = (bf16[256,1152]{1,0:T(8,128)(2,1)S(1)}, bf16[256,1152]{1,0:T(8,128)(2,1)S(1)}, u32[]{:S(2)}, u32[]{:S(2)}) collective-permute-start(bf16[256,1152]{1,0:T(8,128)(2,1)S(1)} %collective-permute-done.2.refs_3_), channel_id=1, source_target_pairs={{0,3},{1,2},{2,1},{3,0},{4,5},{5,4},{6,7},{7,6},{8,11},{9,10},{10,... | collective-permute-start | bytes 1769480 | tf_op jit(solution)/shard_map/ppermute | solution.py:237
  34.8 3.1 %score_first.1.refs_9_ = f32[256,128]{1,0:T(8,128)S(1)} custom-call(bf16[256,1152]{1,0:T(8,128)(2,1)S(1)} %bitcast.9, bf16[256,1152]{1,0:T(8,128)(2,1)S(1)} %collective-permute-done.refs_1_, bf16[256,1152]{1,0:T(8,128)(2,1)S(1)} %collective-permute-done.1.refs_2_, bf16[256,1152]{1,0:T(8,128)(2,1)S(1)} %collective-permute-done.2.refs_3_, ...), custom_call_target="tpu_custom_call" | custom-call | tf_op jit(solution)/shard_map/score_first/pallas_call | solution.py:269
  37.9 4.2 %collective-permute-done.5.refs_0_ = bf16[256,1152]{1,0:T(8,128)(2,1)S(1)} collective-permute-done((bf16[256,1152]{1,0:T(8,128)(2,1)S(1)}, bf16[256,1152]{1,0:T(8,128)(2,1)S(1)}, u32[]{:S(2)}, u32[]{:S(2)}) %collective-permute-start.5) | collective-permute-done | bytes 589856 | tf_op jit(solution)/shard_map/ppermute | solution.py:237
  42.1 1.1 %collective-permute-done.6.refs_1_ = bf16[256,1152]{1,0:T(8,128)(2,1)S(1)} collective-permute-done((bf16[256,1152]{1,0:T(8,128)(2,1)S(1)}, bf16[256,1152]{1,0:T(8,128)(2,1)S(1)}, u32[]{:S(2)}, u32[]{:S(2)}) %collective-permute-start.6) | collective-permute-done | bytes 589856 | tf_op jit(solution)/shard_map/ppermute | solution.py:237
  43.2 1.4 %collective-permute-done.7.refs_2_ = bf16[256,1152]{1,0:T(8,128)(2,1)S(1)} collective-permute-done((bf16[256,1152]{1,0:T(8,128)(2,1)S(1)}, bf16[256,1152]{1,0:T(8,128)(2,1)S(1)}, u32[]{:S(2)}, u32[]{:S(2)}) %collective-permute-start.7) | collective-permute-done | bytes 589856 | tf_op jit(solution)/shard_map/ppermute | solution.py:237
  44.7 1.9 %collective-permute-start.8 = (bf16[96,1152]{1,0:T(8,128)(2,1)S(1)}, bf16[96,1152]{1,0:T(8,128)(2,1)S(1)}, u32[]{:S(2)}, u32[]{:S(2)}) collective-permute-start(bf16[96,1152]{1,0:T(8,128)(2,1)S(1)} %slice.9), channel_id=1, source_target_pairs={{0,24},{1,25},{2,26},{3,27},{4,12},{5,13},{6,14},{7,15},{8,16},{9,... | collective-permute-start | bytes 663560 | tf_op jit(solution)/shard_map/ppermute | solution.py:237
  46.6 0.0 copy-start.2
  46.6 2.2 %collective-permute-start.10 = (bf16[80,1152]{1,0:T(8,128)(2,1)S(1)}, bf16[80,1152]{1,0:T(8,128)(2,1)S(1)}, u32[]{:S(2)}, u32[]{:S(2)}) collective-permute-start(bf16[80,1152]{1,0:T(8,128)(2,1)S(1)} %slice.11), channel_id=1, source_target_pairs={{0,96},{1,97},{2,98},{3,99},{4,36},{5,37},{6,38},{7,39},{8,104},{9... | collective-permute-start | bytes 552968 | tf_op jit(solution)/shard_map/ppermute | solution.py:237
  48.8 2.6 %collective-permute-start.9 = (bf16[80,1152]{1,0:T(8,128)(2,1)S(1)}, bf16[80,1152]{1,0:T(8,128)(2,1)S(1)}, u32[]{:S(2)}, u32[]{:S(2)}) collective-permute-start(bf16[80,1152]{1,0:T(8,128)(2,1)S(1)} %slice.10), channel_id=1, source_target_pairs={{0,3},{1,2},{2,1},{3,0},{4,5},{5,4},{6,7},{7,6},{8,11},{9,10},{10,... | collective-permute-start | bytes 552968 | tf_op jit(solution)/shard_map/ppermute | solution.py:237
  51.4 2.1 %collective-permute-done.10.refs_5_ = bf16[80,1152]{1,0:T(8,128)(2,1)S(1)} collective-permute-done((bf16[80,1152]{1,0:T(8,128)(2,1)S(1)}, bf16[80,1152]{1,0:T(8,128)(2,1)S(1)}, u32[]{:S(2)}, u32[]{:S(2)}) %collective-permute-start.10) | collective-permute-done | bytes 184352 | tf_op jit(solution)/shard_map/ppermute | solution.py:237
  53.5 2.1 %collective-permute-done.9.refs_4_ = bf16[80,1152]{1,0:T(8,128)(2,1)S(1)} collective-permute-done((bf16[80,1152]{1,0:T(8,128)(2,1)S(1)}, bf16[80,1152]{1,0:T(8,128)(2,1)S(1)}, u32[]{:S(2)}, u32[]{:S(2)}) %collective-permute-start.9) | collective-permute-done | bytes 184352 | tf_op jit(solution)/shard_map/ppermute | solution.py:237
  55.6 3.7 %score_second.1 = f32[64,8,128]{2,1,0:T(8,128)S(1)} custom-call(bf16[256,1152]{1,0:T(8,128)(2,1)S(1)} %collective-permute-done.5.refs_0_, bf16[256,1152]{1,0:T(8,128)(2,1)S(1)} %collective-permute-done.6.refs_1_, bf16[256,1152]{1,0:T(8,128)(2,1)S(1)} %collective-permute-done.7.refs_2_, bf16[96,1152]{1,0:T(8,128)(2,1)S(1)} %collective-permute-done.8.refs_3_, ...), custom_call_target="tpu_custom_call" | custom-call | tf_op jit(solution)/shard_map/score_second/pallas_call | solution.py:276
  59.2 15.9 %all_to_all.10 = f32[64,8,128]{2,1,0:T(8,128)S(1)} all-to-all(f32[64,8,128]{2,1,0:T(8,128)S(1)} %score_second.1), channel_id=1, replica_groups={{0,1,2,3,8,9,10,11,16,17,18,19,24,25,26,27,32,33,34,35,40,41,42,43,48,4..., dimensions={0} | all-to-all | bytes 524288 | tf_op jit(solution)/shard_map/all_to_all | solution.py:281
  75.2 1.4 %final.1 = f32[32,32]{1,0:T(8,128)} custom-call(f32[16,4,8,128]{3,2,1,0:T(8,128)S(1)} %bitcast.10, bf16[128,256]{1,0:T(8,128)(2,1)S(1)} %copy-done.1, s32[8,256]{1,0:T(8,128)S(1)} %copy-done.2), custom_call_target="tpu_custom_call" | custom-call | tf_op jit(solution)/shard_map/final/pallas_call | solution.py:282
  (11 shorter events, 0.1 us)
Async XLA Ops:
  0.0 25.3 %collective-permute-start.3 = (bf16[4,256,1024]{2,1,0:T(8,128)(2,1)}, bf16[4,256,1024]{2,1,0:T(8,128)(2,1)S(1)}, u32[]{:S(2)}, u32[]{:S(2)}) collective-permute-start(bf16[4,256,1024]{2,1,0:T(8,128)(2,1)} %refs_6_.1), channel_id=1, source_target_pairs={{0,4},{1,5},{2,6},{3,7},{4,0},{5,1},{6,2},{7,3},{8,12},{9,13},{10,... | collective-permute-start | bytes 6291464 | tf_op jit(solution)/shard_map/ppermute | solution.py:248
  2.0 13.9 %all-to-all-start = ((bf16[8,32,1152]{2,1,0:T(8,128)(2,1)}), bf16[8,32,1152]{2,1,0:T(8,128)(2,1)S(1)}, u32[]{:S(2)}, u32[]{:S(2)}) async-start(bf16[8,32,1152]{2,1,0:T(8,128)(2,1)} %widen.1), calls=%async_computation | async-start | bytes 1179648 | tf_op jit(solution)/shard_map/all_to_all | solution.py:247
  16.0 13.0 %collective-permute-start.2 = (bf16[256,1152]{1,0:T(8,128)(2,1)S(1)}, bf16[256,1152]{1,0:T(8,128)(2,1)S(1)}, u32[]{:S(2)}, u32[]{:S(2)}) collective-permute-start(bf16[256,1152]{1,0:T(8,128)(2,1)S(1)} %bitcast.6), channel_id=1, source_target_pairs={{0,24},{1,25},{2,26},{3,27},{4,12},{5,13},{6,14},{7,15},{8,16},{9,... | collective-permute-start | bytes 1769480 | tf_op jit(solution)/shard_map/ppermute | solution.py:237
  17.8 11.2 %collective-permute-start.1 = (bf16[256,1152]{1,0:T(8,128)(2,1)S(1)}, bf16[256,1152]{1,0:T(8,128)(2,1)S(1)}, u32[]{:S(2)}, u32[]{:S(2)}) collective-permute-start(bf16[256,1152]{1,0:T(8,128)(2,1)S(1)} %bitcast.7), channel_id=1, source_target_pairs={{0,96},{1,97},{2,98},{3,99},{4,36},{5,37},{6,38},{7,39},{8,104},{9... | collective-permute-start | bytes 1769480 | tf_op jit(solution)/shard_map/ppermute | solution.py:237
  19.9 11.1 %collective-permute-start = (bf16[256,1152]{1,0:T(8,128)(2,1)S(1)}, bf16[256,1152]{1,0:T(8,128)(2,1)S(1)}, u32[]{:S(2)}, u32[]{:S(2)}) collective-permute-start(bf16[256,1152]{1,0:T(8,128)(2,1)S(1)} %bitcast.8), channel_id=1, source_target_pairs={{0,3},{1,2},{2,1},{3,0},{4,5},{5,4},{6,7},{7,6},{8,11},{9,10},{10,... | collective-permute-start | bytes 1769480 | tf_op jit(solution)/shard_map/ppermute | solution.py:237
  22.5 2.8 %collective-permute-start.4 = (s32[4]{0:T(128)}, s32[4]{0:T(128)S(1)}, u32[]{:S(2)}, u32[]{:S(2)}) collective-permute-start(s32[4]{0:T(128)} %own_valid_ref.1), channel_id=1, source_target_pairs={{0,4},{1,5},{2,6},{3,7},{4,0},{5,1},{6,2},{7,3},{8,12},{9,13},{10,... | collective-permute-start | bytes 56 | tf_op jit(solution)/shard_map/ppermute | solution.py:249
  25.3 1.6 %copy-start = (bf16[4,256,1024]{2,1,0:T(8,128)(2,1)S(1)}, bf16[4,256,1024]{2,1,0:T(8,128)(2,1)}, u32[]{:S(2)}) copy-start(bf16[4,256,1024]{2,1,0:T(8,128)(2,1)} %refs_6_.1) | copy-start | bytes 6291460
  26.9 0.7 copy-start.3
  31.0 11.1 %collective-permute-start.5 = (bf16[256,1152]{1,0:T(8,128)(2,1)S(1)}, bf16[256,1152]{1,0:T(8,128)(2,1)S(1)}, u32[]{:S(2)}, u32[]{:S(2)}) collective-permute-start(bf16[256,1152]{1,0:T(8,128)(2,1)S(1)} %collective-permute-done.refs_1_), channel_id=1, source_target_pairs={{0,96},{1,97},{2,98},{3,99},{4,36},{5,37},{6,38},{7,39},{8,104},{9... | collective-permute-start | bytes 1769480 | tf_op jit(solution)/shard_map/ppermute | solution.py:237
  32.1 11.1 %collective-permute-start.6 = (bf16[256,1152]{1,0:T(8,128)(2,1)S(1)}, bf16[256,1152]{1,0:T(8,128)(2,1)S(1)}, u32[]{:S(2)}, u32[]{:S(2)}) collective-permute-start(bf16[256,1152]{1,0:T(8,128)(2,1)S(1)} %collective-permute-done.1.refs_2_), channel_id=1, source_target_pairs={{0,24},{1,25},{2,26},{3,27},{4,12},{5,13},{6,14},{7,15},{8,16},{9,... | collective-permute-start | bytes 1769480 | tf_op jit(solution)/shard_map/ppermute | solution.py:237
  33.6 11.1 %collective-permute-start.7 = (bf16[256,1152]{1,0:T(8,128)(2,1)S(1)}, bf16[256,1152]{1,0:T(8,128)(2,1)S(1)}, u32[]{:S(2)}, u32[]{:S(2)}) collective-permute-start(bf16[256,1152]{1,0:T(8,128)(2,1)S(1)} %collective-permute-done.2.refs_3_), channel_id=1, source_target_pairs={{0,3},{1,2},{2,1},{3,0},{4,5},{5,4},{6,7},{7,6},{8,11},{9,10},{10,... | collective-permute-start | bytes 1769480 | tf_op jit(solution)/shard_map/ppermute | solution.py:237
  44.7 10.9 %collective-permute-start.8 = (bf16[96,1152]{1,0:T(8,128)(2,1)S(1)}, bf16[96,1152]{1,0:T(8,128)(2,1)S(1)}, u32[]{:S(2)}, u32[]{:S(2)}) collective-permute-start(bf16[96,1152]{1,0:T(8,128)(2,1)S(1)} %slice.9), channel_id=1, source_target_pairs={{0,24},{1,25},{2,26},{3,27},{4,12},{5,13},{6,14},{7,15},{8,16},{9,... | collective-permute-start | bytes 663560 | tf_op jit(solution)/shard_map/ppermute | solution.py:237
  46.6 28.5 %copy-start.1 = (bf16[128,256]{1,0:T(8,128)(2,1)S(1)}, bf16[128,256]{1,0:T(8,128)(2,1)}, u32[]{:S(2)}) copy-start(bf16[128,256]{1,0:T(8,128)(2,1)} %get-tuple-element.31.pick_ref) | copy-start | bytes 196612
  46.6 28.5 %copy-start.2 = (s32[8,256]{1,0:T(8,128)S(1)}, s32[8,256]{1,0:T(8,128)}, u32[]{:S(2)}) copy-start(s32[8,256]{1,0:T(8,128)} %get-tuple-element.32.group_ref) | copy-start | bytes 24580
  46.6 6.8 %collective-permute-start.10 = (bf16[80,1152]{1,0:T(8,128)(2,1)S(1)}, bf16[80,1152]{1,0:T(8,128)(2,1)S(1)}, u32[]{:S(2)}, u32[]{:S(2)}) collective-permute-start(bf16[80,1152]{1,0:T(8,128)(2,1)S(1)} %slice.11), channel_id=1, source_target_pairs={{0,96},{1,97},{2,98},{3,99},{4,36},{5,37},{6,38},{7,39},{8,104},{9... | collective-permute-start | bytes 552968 | tf_op jit(solution)/shard_map/ppermute | solution.py:237
  48.8 6.7 %collective-permute-start.9 = (bf16[80,1152]{1,0:T(8,128)(2,1)S(1)}, bf16[80,1152]{1,0:T(8,128)(2,1)S(1)}, u32[]{:S(2)}, u32[]{:S(2)}) collective-permute-start(bf16[80,1152]{1,0:T(8,128)(2,1)S(1)} %slice.10), channel_id=1, source_target_pairs={{0,3},{1,2},{2,1},{3,0},{4,5},{5,4},{6,7},{7,6},{8,11},{9,10},{10,... | collective-permute-start | bytes 552968 | tf_op jit(solution)/shard_map/ppermute | solution.py:237

commit v3 on v2

v3 whole, which is shorter than its diff:
```python
import jax
import jax.numpy as jnp
from jax import lax
from jax.experimental import pallas as pl
from jax.experimental.pallas import tpu as pltpu
from jax.sharding import PartitionSpec as P

D = 1024
WIDE = D + 128
TOPK = 32
AXES = ("owner", "replica")
N_DEV = 128
N_CORE = 64
BIG = 1e30
F32 = jnp.float32
BF16 = jnp.bfloat16

PAIRING = {"a": (1, 0, 3, 2), "b": (3, 2, 1, 0)}
DIMS_A = ("za", "ya", "xa")
DIMS_B = ("zb", "yb", "xb")


def moved(device, dim):
    z, core, x, y = device % 4, device // 4 % 2, device // 8 % 4, device // 32
    place = {"x": x, "y": y, "z": z}
    place[dim[0]] = PAIRING[dim[1]][place[dim[0]]]
    return ((place["y"] * 4 + place["x"]) * 2 + core) * 4 + place["z"]


def core_of(device):
    return device // 4 % 2


def dims_of(core, first):
    return DIMS_A if (core == 0) == first else DIMS_B


def far(device, mask, first):
    for bit, dim in enumerate(dims_of(core_of(device), first)):
        if mask >> bit & 1:
            device = moved(device, dim)
    return device


def at_address(core, address):
    return far(far(4 * core, address >> 3, False), address & 7, True)


CORE_GROUPS = [[at_address(core, address) for address in range(N_CORE)] for core in range(2)]
NEAR_GROUPS = [group[start : start + 8] for group in CORE_GROUPS for start in range(0, N_CORE, 8)]
CORE_SWAP = [(device, device ^ 4) for device in range(N_DEV)]
FIRST_HALF = (0, 1, 2, 4)
SECOND_HALF = (3, 6, 5)


def pairing_bits(place, core):
    low, high = (place ^ (place >> 1)) & 1, place >> 1
    even = jnp.equal(core, 0)
    return jnp.where(even, low, high), jnp.where(even, high, low)


def own_group():
    owner = lax.axis_index("owner")
    bits = [pairing_bits(place, owner & 1)[1] for place in (lax.axis_index("replica"), owner >> 3, (owner >> 1) & 3)]
    return bits[0] + 2 * bits[1] + 4 * bits[2]


def sort_pairs(count):
    pairs = []
    p = 1
    while p < count:
        k = p
        while k >= 1:
            for j in range(k % p, count - k, 2 * k):
                for i in range(min(k, count - j - k)):
                    if (i + j) // (p * 2) == (i + j + k) // (p * 2):
                        pairs.append((i + j, i + j + k))
            k //= 2
        p *= 2
    return pairs


SORT_PAIRS = sort_pairs(TOPK)
MERGE_PAIRS = [(i, i + d) for d in (16, 8, 4, 2, 1) for i in range(TOPK) if not i & d]


def exchange(values, pairs):
    values = list(values)
    for i, j in pairs:
        values[i], values[j] = jnp.maximum(values[i], values[j]), jnp.minimum(values[i], values[j])
    return values


def merged(first, second):
    return exchange([jnp.maximum(first[i], second[TOPK - 1 - i]) for i in range(TOPK)], MERGE_PAIRS)


def merged_rows(first, second, shift):
    row = lax.broadcasted_iota(jnp.int32, (8, 128), 0)
    odd = (row & shift) != 0
    here = [jnp.where(odd, b, a) for a, b in zip(first, second)]
    there = [pltpu.roll(jnp.where(odd, a, b), 8 - shift, 0) for a, b in zip(first, second)]
    return merged(here, there)


def place_matrix(slot_ref):
    core = lax.rem(lax.axis_index("owner"), 2)
    places = jnp.bitwise_xor(slot_ref[...], 4 * core)
    return (places == lax.broadcasted_iota(jnp.int32, (128, 128), 0)).astype(BF16)


def rank_table(probes_ref, place):
    lists = lax.broadcasted_iota(jnp.int32, (128, 32), 0)
    named = jnp.zeros((128, 32), F32)
    for j in range(8):
        named = jnp.where(probes_ref[j : j + 1, :] == lists, 1.0, named)
    probed = jnp.dot(place, named.astype(BF16), preferred_element_type=F32)
    before = lax.broadcasted_iota(jnp.int32, (32, 32), 0) < lax.broadcasted_iota(jnp.int32, (32, 32), 1)
    rank = jnp.dot(probed.astype(BF16), before.astype(BF16), preferred_element_type=F32)
    return jnp.where(probed > 0.5, rank, -1.0)


def widen_kernel(queries_ref, probes_ref, slot_ref, out_ref):
    table = rank_table(probes_ref, place_matrix(slot_ref)).T.astype(BF16)
    for copy in range(8):
        out_ref[copy, :, :D] = queries_ref[...]
        out_ref[copy, :, D:] = table


def wanted_kernel(probes_ref, slot_ref, pick_ref, group_ref):
    place = place_matrix(slot_ref)
    rank = rank_table(probes_ref, place)
    index = lax.broadcasted_iota(jnp.int32, (128, 32), 0)
    core = lax.axis_index("owner") & 1
    for j in range(8):
        placed = jnp.dot(place, (probes_ref[j : j + 1, :] == index).astype(BF16), preferred_element_type=F32)
        where = jnp.sum(placed * index.astype(F32), 0, keepdims=True).astype(jnp.int32)
        slot = jnp.sum(placed * rank, 0, keepdims=True).astype(jnp.int32)
        chip = where >> 3
        (y_first, y_second), (x_first, x_second) = [pairing_bits(place, core) for place in (chip >> 2, chip & 3)]
        row = (x_second * 8 + y_second * 4 + x_first * 2 + y_first) * 8 + (where & 4) + slot
        pick_ref[:, 32 * j : 32 * j + 32] = (index == row).astype(BF16)
        group_ref[:, 32 * j : 32 * j + 32] = jnp.broadcast_to(where & 3, (8, 32))


def lists_kernel(own, sibling, own_valid, sibling_valid, lists, norms, sems):
    copies = []
    for t in range(8):
        copies.append(pltpu.make_async_copy(own.at[t] if t < 4 else sibling.at[t - 4], lists.at[t], sems.at[t]))
        copies[t].start()
    row = lax.axis_index("replica") * 256 + lax.broadcasted_iota(jnp.int32, (256, 1), 0)
    lane = lax.broadcasted_iota(jnp.int32, (256, 128), 1)
    total = jnp.zeros((256, 128), F32)
    for t in (4, 5, 6, 7, 0, 1, 2, 3):
        copies[t].wait()
        rows = lists[t].astype(F32)
        valid = (own_valid if t < 4 else sibling_valid)[0:1, t % 4 : t % 4 + 1]
        norm = jnp.where(row < valid, 0.5 * jnp.sum(rows * rows, 1, keepdims=True), BIG)
        total = jnp.where(lane == t, norm, total)
    norms[...] = total


def chosen_queries(wide):
    chip = lax.axis_index("owner") // 2
    column = lax.broadcasted_iota(jnp.int32, (256, 128), 0)
    wanted = (lax.broadcasted_iota(jnp.int32, (256, 128), 1) == chip * 8 + (column >> 5)).astype(BF16)
    rank = lax.dot_general(wanted, wide[:, D:], (((1,), (1,)), ((), ())), preferred_element_type=F32)
    column = lax.broadcasted_iota(jnp.int32, (256, 256), 0)
    same_block = (lax.broadcasted_iota(jnp.int32, (256, 256), 1) >> 5) == ((column >> 2) & 7)
    pick = (same_block & (rank == (column & 3).astype(F32))).astype(BF16)
    return jnp.dot(pick, wide[:, :D], preferred_element_type=F32).astype(BF16)


def score(lists, norms, t, queries):
    return lax.dot_general(lists[t], queries, (((1,), (1,)), ((), ())), preferred_element_type=F32) - norms[:, t : t + 1]


def sort_rows(scores):
    return exchange([scores[8 * i : 8 * i + 8] for i in range(TOPK)], SORT_PAIRS)


def score_kernel(*refs):
    groups, (lists, norms, out, chosen, best) = refs[:-5], refs[-5:]
    if len(groups) < 4:
        chosen[:, 32 * len(groups) :, :] = jnp.zeros((8, 128 - 32 * len(groups), D), BF16)
    for g, ref in enumerate(groups):
        picked = chosen_queries(ref[...])
        for t in range(8):
            chosen[t, 32 * g : 32 * g + 32, :] = picked[32 * t : 32 * t + 32]
    quads = []
    for quad in range(2):
        sets = [sort_rows(score(lists, norms, t, chosen[t])) for t in range(4 * quad, 4 * quad + 4)]
        quads.append(merged_rows(merged_rows(sets[0], sets[1], 1), merged_rows(sets[2], sets[3], 1), 2))
    for i, value in enumerate(merged_rows(quads[0], quads[1], 4)):
        best[8 * i : 8 * i + 8, :] = value
    for half in range(2):
        out[half] = jnp.concatenate([best[pl.ds(4 * half + t, TOPK, stride=8), :] for t in range(4)], 0).T


def last_kernel(lower, upper, lists, norms, first, second, out, best):
    picked = chosen_queries(jnp.concatenate([lower[...], upper[...]], 0))
    lane = lax.broadcasted_iota(jnp.int32, (256, 128), 1)
    sets = []
    for half in range(2):
        queries = picked[128 * half : 128 * half + 128]
        scores = score(lists, norms, 4 * half, queries)
        for t in range(1, 4):
            scores = jnp.where((lane >> 5) == t, score(lists, norms, 4 * half + t, queries), scores)
        sets.append(sort_rows(scores))
    values = merged_rows(sets[0], sets[1], 1)
    for shift in (2, 4):
        values = merged(values, [pltpu.roll(value, 8 - shift, 0) for value in values])
    for i, value in enumerate(values):
        best[8 * i : 8 * i + 8, :] = value
    own = own_group()
    for half in range(2):
        rows = best[pl.ds(half, TOPK, stride=8), :]
        turned = jnp.concatenate([rows] + [pltpu.roll(rows, 128 - 32 * t, 1) for t in range(1, 4)], 0).T
        found = [(mask, first[half, 32 * g : 32 * g + 32, :]) for g, mask in enumerate(FIRST_HALF)]
        found += [(mask, second[half, 32 * g : 32 * g + 32, :]) for g, mask in enumerate(SECOND_HALF)]
        for mask, values in found + [(7, turned[:32])]:
            place = (own ^ mask) * 8
            for b in range(8):
                out[place + b, 4 * half : 4 * half + 4, :] = values[4 * b : 4 * b + 4]


def final_kernel(back_ref, pick_ref, group_ref, out_ref, tiles, rows):
    pick = pick_ref[...]
    group = jnp.concatenate([group_ref[...]] * 4, 0)
    for z in range(4):
        left = back_ref[:, z >> 1, :, z & 1].reshape(128, 128).T
        found = jnp.zeros((128, 256), F32)
        for _ in range(3):
            piece = left.astype(BF16)
            left = left - piece.astype(F32)
            found = found + jnp.dot(piece, pick, preferred_element_type=F32)
        scores = found[:32]
        for t in range(1, 4):
            scores = jnp.where(group == t, found[32 * t : 32 * t + 32], scores)
        for half in range(2):
            tiles[pl.ds(2 * z + half, TOPK, stride=8), :] = scores[:, 128 * half : 128 * half + 128]
    values = [tiles[8 * i : 8 * i + 8, :] for i in range(TOPK)]
    for axis, shift in ((0, 4), (0, 2), (0, 1), (1, 64), (1, 32)):
        values = merged(values, [pltpu.roll(value, shift, axis) for value in values])
    for i, value in enumerate(values):
        rows[i : i + 1, :] = value[:1]
    out_ref[...] = rows[...].T[:32]


def params():
    return pltpu.CompilerParams(vmem_limit_bytes=20 * 1024 * 1024)


def spaces(text):
    kinds = {"v": pltpu.VMEM, "s": pltpu.SMEM, "h": pltpu.HBM, "a": pl.ANY}
    return [pl.BlockSpec(memory_space=kinds[kind]) for kind in text]


def hop(value, mask):
    return lax.ppermute(value, AXES, [(device, far(device, mask, False)) for device in range(N_DEV)])


def per_device(queries, probes, list_slot, valid_rows, database):
    shape = jax.ShapeDtypeStruct
    slots = list_slot.reshape(1, 128)
    probes = probes.T
    wide = pl.pallas_call(
        widen_kernel, out_shape=shape((8, 32, WIDE), BF16), in_specs=spaces("vvv"), out_specs=spaces("v")[0], name="widen"
    )(queries, probes, slots)
    near = lax.all_to_all(wide, AXES, 0, 0, axis_index_groups=NEAR_GROUPS, tiled=True).reshape(256, WIDE)
    sibling = lax.ppermute(database, AXES, CORE_SWAP)
    sibling_valid = lax.ppermute(valid_rows, AXES, CORE_SWAP)
    near, sibling, sibling_valid = lax.optimization_barrier((near, sibling, sibling_valid))

    groups = {0: near}
    for mask in (1, 2, 4):
        groups[mask] = hop(near, mask)
    lists, norms = pl.pallas_call(
        lists_kernel, out_shape=(pltpu.VMEM((8, 256, D), BF16), pltpu.VMEM((256, 128), F32)), in_specs=spaces("havv"),
        out_specs=spaces("vv"), scratch_shapes=[pltpu.SemaphoreType.DMA((8,))], compiler_params=params(), name="lists",
    )(pltpu.with_memory_space_constraint(database, pltpu.HBM), sibling, valid_rows.reshape(1, 4), sibling_valid.reshape(1, 4))
    groups[4], lists, norms = lax.optimization_barrier((groups[4], lists, norms))
    for mask, source, step in ((3, 1, 2), (6, 2, 4), (5, 4, 1)):
        groups[mask] = hop(groups[source], step)

    def scored(masks, name):
        return pl.pallas_call(
            score_kernel, out_shape=shape((2, 128, 128), F32), in_specs=spaces("v" * (len(masks) + 2)), out_specs=spaces("v")[0],
            scratch_shapes=[pltpu.VMEM((8, 128, D), BF16), pltpu.VMEM((256, 128), F32)], compiler_params=params(), name=name,
        )(*[groups[mask] for mask in masks], lists, norms)

    first = scored(FIRST_HALF, "score_first")
    groups[3], groups[6], groups[5], first = lax.optimization_barrier((groups[3], groups[6], groups[5], first))
    last = [hop(groups[3][:128], 4), hop(groups[6][128:], 1)]
    second = scored(SECOND_HALF, "score_second")
    *last, second = lax.optimization_barrier((*last, second))
    blocks = pl.pallas_call(
        last_kernel, out_shape=shape((N_CORE, 8, 128), F32), in_specs=spaces("vvvvvv"), out_specs=spaces("v")[0],
        scratch_shapes=[pltpu.VMEM((256, 128), F32)], compiler_params=params(), name="score_last",
    )(*last, lists, norms, first, second)
    pick, group = pl.pallas_call(
        wanted_kernel, out_shape=(pltpu.VMEM((128, 256), BF16), pltpu.VMEM((8, 256), jnp.int32)), in_specs=spaces("vv"),
        out_specs=spaces("vv"), name="wanted",
    )(probes, slots)
    back = lax.all_to_all(blocks, AXES, 0, 0, axis_index_groups=CORE_GROUPS, tiled=True)
    return pl.pallas_call(
        final_kernel, out_shape=shape((32, TOPK), F32), in_specs=spaces("vvv"), out_specs=spaces("v")[0],
        scratch_shapes=[pltpu.VMEM((256, 128), F32), pltpu.VMEM((32, 128), F32)], compiler_params=params(), name="final",
    )(back.reshape(4, 2, 4, 2, 8, 128), pick, group)


def solution(mesh):
    in_specs = (P(AXES, None), P(AXES, None), P(), P("owner"), P("owner", "replica", None))
    return jax.shard_map(per_device, mesh=mesh, in_specs=in_specs, out_specs=P(AXES, None), check_vma=False)
```

time: 76.9 us -> 73.3 us (0.953)
  blocking collectives: 15.9 us -> 0 us
  starting transfers between devices: 24.1 us -> 34.6 us
  local copies, waits for them, and re-layouts: 3 us -> 0.7 us
  waiting for transfers between devices: 20 us -> 22.1 us
  Pallas kernels: 13.5 us -> 15.5 us
    all_to_all x1 -> x0, blocking collectives: 15.9 us -> none  [per_device(): lax.all_to_all(blocks, AXES, 0, 0, axis_index_groups=CORE_GROUPS, tiled=T...]
    all_to_all x0 -> x1, waiting for transfers between devices: none -> 9.12 us  [per_device(): lax.all_to_all(blocks, AXES, 0, 0, axis_index_groups=CORE_GROUPS, tiled=T...]
    all_to_all x0 -> x1, starting transfers between devices: none -> 4.95 us  [per_device(): lax.all_to_all(blocks, AXES, 0, 0, axis_index_groups=CORE_GROUPS, tiled=T...]
    all_to_all x1, waiting for transfers between devices: 6.18 us -> 1.93 us  [per_device(): lax.all_to_all(wide, AXES, 0, 0, axis_index_groups=NEAR_GROUPS, tiled=True)]
    ppermute x1, starting transfers between devices: 1.83 us -> 5.05 us  [per_device(): sibling_valid = lax.ppermute(valid_rows, AXES, CORE_SWAP)]
    ppermute x9 -> x8, waiting for transfers between devices: 12.8 us -> 10.1 us  [hop(): lax.ppermute(value, AXES, [(device, far(device, mask, False)) for device...]
    ppermute x9 -> x8, starting transfers between devices: 17 us -> 19.4 us  [hop(): lax.ppermute(value, AXES, [(device, far(device, mask, False)) for device...]
    pallas_call x4 -> x5, Pallas kernels: 10.1 us -> 12.1 us  [the longest x2 5.92 us: scored(): pl.pallas_call(score_kernel, out_shape=shape((2, 128, 128), F32), in_spec...]
  transfers between devices with their start and end apart: 12 -> 12, of which waited for: 8 -> 8; matrix products, arithmetic and copies ran while one was open for 1% -> 0% of each run, Pallas kernels for 11% -> 16%
where the time goes in v3:
time: 73.3 us; the launch traced here: 73 us
  starting transfers between devices  34.6 us (47%)
  waiting for transfers between devices  22.1 us (30%)
  Pallas kernels  15.5 us (21%)
    ppermute x8, starting transfers between devices, hop(): lax.ppermute(value, AXES, [(device, far(device, mask, False)) for device...  19.4 us
    ppermute x8, waiting for transfers between devices, hop(): lax.ppermute(value, AXES, [(device, far(device, mask, False)) for device...  10.1 us
    all_to_all x1, waiting for transfers between devices, per_device(): lax.all_to_all(blocks, AXES, 0, 0, axis_index_groups=CORE_GROUPS, tiled=T...  9.12 us
    pallas_call x2, Pallas kernels, scored(): pl.pallas_call(score_kernel, out_shape=shape((2, 128, 128), F32), in_spec...  5.92 us
    all_to_all x1, starting transfers between devices, per_device(): lax.all_to_all(wide, AXES, 0, 0, axis_index_groups=NEAR_GROUPS, tiled=True)  5.22 us
    ppermute x1, starting transfers between devices, per_device(): sibling_valid = lax.ppermute(valid_rows, AXES, CORE_SWAP)  5.05 us
    all_to_all x1, starting transfers between devices, per_device(): lax.all_to_all(blocks, AXES, 0, 0, axis_index_groups=CORE_GROUPS, tiled=T...  4.95 us
    pallas_call x1, Pallas kernels, per_device(): pl.pallas_call(last_kernel, out_shape=shape((N_CORE, 8, 128), F32), in_sp...  2.54 us
  transfers between devices with their start and end apart: 12, of which 8 were waited for; matrix products, arithmetic and copies ran while one was open for 0% of the time, Pallas kernels for 16%

profile of v3, /device:TPU:0, one launch (start us, length us, event | category | flops | bytes accessed | tf_op | source)
XLA Modules:
  0.0 73.0 jit_solution(8005614184415827863)
XLA Ops:
  0.0 0.0 collective-permute-start
  0.0 2.0 %widen.1 = bf16[8,32,1152]{2,1,0:T(8,128)(2,1)} custom-call(bf16[32,1024]{1,0:T(8,128)(2,1)} %queries_ref.1, s32[8,32]{1,0:T(8,128)} %bitcast.13, s32[1,128]{1,0:T(1,128)} %bitcast.15), custom_call_target="tpu_custom_call" | custom-call | tf_op jit(solution)/shard_map/widen/pallas_call | solution.py:267
  2.0 5.2 %all-to-all-start = ((bf16[8,32,1152]{2,1,0:T(8,128)(2,1)}), bf16[8,32,1152]{2,1,0:T(8,128)(2,1)S(1)}, u32[]{:S(2)}, u32[]{:S(2)}) async-start(bf16[8,32,1152]{2,1,0:T(8,128)(2,1)} %widen.1), calls=%async_computation | async-start | bytes 1179648 | tf_op jit(solution)/shard_map/all_to_all | solution.py:270
  7.2 5.1 %collective-permute-start.1 = (s32[4]{0:T(128)}, s32[4]{0:T(128)S(1)}, u32[]{:S(2)}, u32[]{:S(2)}) collective-permute-start(s32[4]{0:T(128)} %param.8), channel_id=1, source_target_pairs={{0,4},{1,5},{2,6},{3,7},{4,0},{5,1},{6,2},{7,3},{8,12},{9,13},{10,... | collective-permute-start | bytes 56 | tf_op jit(solution)/shard_map/ppermute | solution.py:272
  12.3 1.0 %collective-permute-done.1 = s32[4]{0:T(128)S(1)} collective-permute-done((s32[4]{0:T(128)}, s32[4]{0:T(128)S(1)}, u32[]{:S(2)}, u32[]{:S(2)}) %collective-permute-start.1) | collective-permute-done | bytes 48 | tf_op jit(solution)/shard_map/ppermute | solution.py:272
  13.3 1.9 %all-to-all-done = bf16[8,32,1152]{2,1,0:T(8,128)(2,1)S(1)} async-done(((bf16[8,32,1152]{2,1,0:T(8,128)(2,1)}), bf16[8,32,1152]{2,1,0:T(8,128)(2,1)S(1)}, u32[]{:S(2)}, u32[]{:S(2)}) %all-to-all-start) | async-done | bytes 589856 | tf_op jit(solution)/shard_map/all_to_all | solution.py:270
  15.2 0.0 collective-permute-done.sibling
  15.2 2.1 %collective-permute-start.6 = (bf16[256,1152]{1,0:T(8,128)(2,1)S(1)}, bf16[256,1152]{1,0:T(8,128)(2,1)S(1)}, u32[]{:S(2)}, u32[]{:S(2)}) collective-permute-start(bf16[256,1152]{1,0:T(8,128)(2,1)S(1)} %bitcast.6), channel_id=1, source_target_pairs={{0,24},{1,25},{2,26},{3,27},{4,12},{5,13},{6,14},{7,15},{8,16},{9,... | collective-permute-start | bytes 1769480 | tf_op jit(solution)/shard_map/ppermute | solution.py:260
  17.3 3.0 %collective-permute-start.2 = (bf16[256,1152]{1,0:T(8,128)(2,1)S(1)}, bf16[256,1152]{1,0:T(8,128)(2,1)S(1)}, u32[]{:S(2)}, u32[]{:S(2)}) collective-permute-start(bf16[256,1152]{1,0:T(8,128)(2,1)S(1)} %bitcast.7), channel_id=1, source_target_pairs={{0,3},{1,2},{2,1},{3,0},{4,5},{5,4},{6,7},{7,6},{8,11},{9,10},{10,... | collective-permute-start | bytes 1769480 | tf_op jit(solution)/shard_map/ppermute | solution.py:260
  20.3 3.0 %collective-permute-start.4 = (bf16[256,1152]{1,0:T(8,128)(2,1)S(1)}, bf16[256,1152]{1,0:T(8,128)(2,1)S(1)}, u32[]{:S(2)}, u32[]{:S(2)}) collective-permute-start(bf16[256,1152]{1,0:T(8,128)(2,1)S(1)} %bitcast.8), channel_id=1, source_target_pairs={{0,96},{1,97},{2,98},{3,99},{4,36},{5,37},{6,38},{7,39},{8,104},{9... | collective-permute-start | bytes 1769480 | tf_op jit(solution)/shard_map/ppermute | solution.py:260
  23.3 0.7 copy-done
  24.0 2.3 %lists.1 = (bf16[8,256,1024]{2,1,0:T(8,128)(2,1)S(1)}, f32[256,128]{1,0:T(8,128)S(1)}) custom-call(bf16[4,256,1024]{2,1,0:T(8,128)(2,1)} %own.1, bf16[4,256,1024]{2,1,0:T(8,128)(2,1)S(1)} %collective-permute-done.sibling, s32[1,4]{1,0:T(1,128)S(1)} %bitcast.11, s32[1,4]{1,0:T(1,128)S(1)} %bitcast.12), custom_call_target="tpu_custom_call" | custom-call | tf_op jit(solution)/shard_map/lists/pallas_call | solution.py:278
  26.4 0.0 collective-permute-done.6.refs_3_
  26.4 2.6 %collective-permute-start.7 = (bf16[256,1152]{1,0:T(8,128)(2,1)S(1)}, bf16[256,1152]{1,0:T(8,128)(2,1)S(1)}, u32[]{:S(2)}, u32[]{:S(2)}) collective-permute-start(bf16[256,1152]{1,0:T(8,128)(2,1)S(1)} %collective-permute-done.6.refs_3_), channel_id=1, source_target_pairs={{0,3},{1,2},{2,1},{3,0},{4,5},{5,4},{6,7},{7,6},{8,11},{9,10},{10,... | collective-permute-start | bytes 1769480 | tf_op jit(solution)/shard_map/ppermute | solution.py:260
  29.0 0.2 collective-permute-done.2.refs_1_
  29.2 2.5 %collective-permute-start.3 = (bf16[256,1152]{1,0:T(8,128)(2,1)S(1)}, bf16[256,1152]{1,0:T(8,128)(2,1)S(1)}, u32[]{:S(2)}, u32[]{:S(2)}) collective-permute-start(bf16[256,1152]{1,0:T(8,128)(2,1)S(1)} %collective-permute-done.2.refs_1_), channel_id=1, source_target_pairs={{0,96},{1,97},{2,98},{3,99},{4,36},{5,37},{6,38},{7,39},{8,104},{9... | collective-permute-start | bytes 1769480 | tf_op jit(solution)/shard_map/ppermute | solution.py:260
  31.7 0.0 collective-permute-done.4.refs_2_
  31.7 2.8 %collective-permute-start.5 = (bf16[256,1152]{1,0:T(8,128)(2,1)S(1)}, bf16[256,1152]{1,0:T(8,128)(2,1)S(1)}, u32[]{:S(2)}, u32[]{:S(2)}) collective-permute-start(bf16[256,1152]{1,0:T(8,128)(2,1)S(1)} %collective-permute-done.4.refs_2_), channel_id=1, source_target_pairs={{0,24},{1,25},{2,26},{3,27},{4,12},{5,13},{6,14},{7,15},{8,16},{9,... | collective-permute-start | bytes 1769480 | tf_op jit(solution)/shard_map/ppermute | solution.py:260
  34.4 3.1 %score_first.1.first = f32[2,128,128]{2,1,0:T(8,128)S(1)} custom-call(bf16[256,1152]{1,0:T(8,128)(2,1)S(1)} %bitcast.9, bf16[256,1152]{1,0:T(8,128)(2,1)S(1)} %collective-permute-done.2.refs_1_, bf16[256,1152]{1,0:T(8,128)(2,1)S(1)} %collective-permute-done.4.refs_2_, bf16[256,1152]{1,0:T(8,128)(2,1)S(1)} %collective-permute-done.6.refs_3_, ...), custom_call_target="tpu_custom_call" | custom-call | tf_op jit(solution)/shard_map/score_first/pallas_call | solution.py:287
  37.5 0.0 collective-permute-done.7.refs_2_
  37.6 2.7 %collective-permute-done.3.refs_0_ = bf16[256,1152]{1,0:T(8,128)(2,1)S(1)} collective-permute-done((bf16[256,1152]{1,0:T(8,128)(2,1)S(1)}, bf16[256,1152]{1,0:T(8,128)(2,1)S(1)}, u32[]{:S(2)}, u32[]{:S(2)}) %collective-permute-start.3) | collective-permute-done | bytes 589856 | tf_op jit(solution)/shard_map/ppermute | solution.py:260
  40.3 2.5 %collective-permute-done.5.refs_1_ = bf16[256,1152]{1,0:T(8,128)(2,1)S(1)} collective-permute-done((bf16[256,1152]{1,0:T(8,128)(2,1)S(1)}, bf16[256,1152]{1,0:T(8,128)(2,1)S(1)}, u32[]{:S(2)}, u32[]{:S(2)}) %collective-permute-start.5) | collective-permute-done | bytes 589856 | tf_op jit(solution)/shard_map/ppermute | solution.py:260
  42.8 2.8 %collective-permute-start.8 = (bf16[128,1152]{1,0:T(8,128)(2,1)S(1)}, bf16[128,1152]{1,0:T(8,128)(2,1)S(1)}, u32[]{:S(2)}, u32[]{:S(2)}) collective-permute-start(bf16[128,1152]{1,0:T(8,128)(2,1)S(1)} %slice.6), channel_id=1, source_target_pairs={{0,24},{1,25},{2,26},{3,27},{4,12},{5,13},{6,14},{7,15},{8,16},{9,... | collective-permute-start | bytes 884744 | tf_op jit(solution)/shard_map/ppermute | solution.py:260
  45.7 0.6 collective-permute-start.9
  46.2 2.8 %score_second.1.second = f32[2,128,128]{2,1,0:T(8,128)S(1)} custom-call(bf16[256,1152]{1,0:T(8,128)(2,1)S(1)} %collective-permute-done.3.refs_0_, bf16[256,1152]{1,0:T(8,128)(2,1)S(1)} %collective-permute-done.5.refs_1_, bf16[256,1152]{1,0:T(8,128)(2,1)S(1)} %collective-permute-done.7.refs_2_, ...), custom_call_target="tpu_custom_call" | custom-call | tf_op jit(solution)/shard_map/score_second/pallas_call | solution.py:287
  49.1 1.8 %collective-permute-done.8.lower = bf16[128,1152]{1,0:T(8,128)(2,1)S(1)} collective-permute-done((bf16[128,1152]{1,0:T(8,128)(2,1)S(1)}, bf16[128,1152]{1,0:T(8,128)(2,1)S(1)}, u32[]{:S(2)}, u32[]{:S(2)}) %collective-permute-start.8) | collective-permute-done | bytes 294944 | tf_op jit(solution)/shard_map/ppermute | solution.py:260
  50.8 2.9 %collective-permute-done.9.upper = bf16[128,1152]{1,0:T(8,128)(2,1)S(1)} collective-permute-done((bf16[128,1152]{1,0:T(8,128)(2,1)S(1)}, bf16[128,1152]{1,0:T(8,128)(2,1)S(1)}, u32[]{:S(2)}, u32[]{:S(2)}) %collective-permute-start.9) | collective-permute-done | bytes 294944 | tf_op jit(solution)/shard_map/ppermute | solution.py:260
  53.7 2.5 %score_last.1 = f32[64,8,128]{2,1,0:T(8,128)} custom-call(bf16[128,1152]{1,0:T(8,128)(2,1)S(1)} %collective-permute-done.8.lower, bf16[128,1152]{1,0:T(8,128)(2,1)S(1)} %collective-permute-done.9.upper, bf16[8,256,1024]{2,1,0:T(8,128)(2,1)S(1)} %get-tuple-element.28.refs_4_.refs_3_.lists, f32[256,128]{1,0:T(8,128)S(1)} %get-tuple-element.29.refs_5_.refs_4_.norms, ...), custom_call_target="tpu_custom_call" | custom-call | tf_op jit(solution)/shard_map/score_last/pallas_call | solution.py:297
  56.2 5.0 %all-to-all-start.1 = ((f32[64,8,128]{2,1,0:T(8,128)}), f32[64,8,128]{2,1,0:T(8,128)S(1)}, u32[]{:S(2)}, u32[]{:S(2)}) async-start(f32[64,8,128]{2,1,0:T(8,128)} %score_last.1), calls=%async_computation.1 | async-start | bytes 524288 | tf_op jit(solution)/shard_map/all_to_all | solution.py:305
  61.2 1.2 %wanted.1 = (bf16[128,256]{1,0:T(8,128)(2,1)S(1)}, s32[8,256]{1,0:T(8,128)S(1)}) custom-call(s32[8,32]{1,0:T(8,128)} %bitcast.14, s32[1,128]{1,0:T(1,128)} %bitcast.16), custom_call_target="tpu_custom_call" | custom-call | tf_op jit(solution)/shard_map/wanted/pallas_call | solution.py:301
  62.4 9.1 %all-to-all-done.1 = f32[64,8,128]{2,1,0:T(8,128)S(1)} async-done(((f32[64,8,128]{2,1,0:T(8,128)}), f32[64,8,128]{2,1,0:T(8,128)S(1)}, u32[]{:S(2)}, u32[]{:S(2)}) %all-to-all-start.1) | async-done | bytes 262176 | tf_op jit(solution)/shard_map/all_to_all | solution.py:305
  71.6 1.4 %final.1 = f32[32,32]{1,0:T(8,128)} custom-call(f32[4,2,4,2,8,128]{5,4,3,2,1,0:T(8,128)S(1)} %bitcast.10, bf16[128,256]{1,0:T(8,128)(2,1)S(1)} %get-tuple-element.37.pick_ref, s32[8,256]{1,0:T(8,128)S(1)} %get-tuple-element.38.group_ref), custom_call_target="tpu_custom_call" | custom-call | tf_op jit(solution)/shard_map/final/pallas_call | solution.py:306
  (3 shorter events, 0.0 us)
Async XLA Ops:
  0.0 15.2 %collective-permute-start = (bf16[4,256,1024]{2,1,0:T(8,128)(2,1)}, bf16[4,256,1024]{2,1,0:T(8,128)(2,1)S(1)}, u32[]{:S(2)}, u32[]{:S(2)}) collective-permute-start(bf16[4,256,1024]{2,1,0:T(8,128)(2,1)} %own.1), channel_id=1, source_target_pairs={{0,4},{1,5},{2,6},{3,7},{4,0},{5,1},{6,2},{7,3},{8,12},{9,13},{10,... | collective-permute-start | bytes 6291464 | tf_op jit(solution)/shard_map/ppermute | solution.py:271
  2.0 13.2 %all-to-all-start = ((bf16[8,32,1152]{2,1,0:T(8,128)(2,1)}), bf16[8,32,1152]{2,1,0:T(8,128)(2,1)S(1)}, u32[]{:S(2)}, u32[]{:S(2)}) async-start(bf16[8,32,1152]{2,1,0:T(8,128)(2,1)} %widen.1), calls=%async_computation | async-start | bytes 1179648 | tf_op jit(solution)/shard_map/all_to_all | solution.py:270
  7.2 6.0 %collective-permute-start.1 = (s32[4]{0:T(128)}, s32[4]{0:T(128)S(1)}, u32[]{:S(2)}, u32[]{:S(2)}) collective-permute-start(s32[4]{0:T(128)} %param.8), channel_id=1, source_target_pairs={{0,4},{1,5},{2,6},{3,7},{4,0},{5,1},{6,2},{7,3},{8,12},{9,13},{10,... | collective-permute-start | bytes 56 | tf_op jit(solution)/shard_map/ppermute | solution.py:272
  15.2 11.2 %collective-permute-start.6 = (bf16[256,1152]{1,0:T(8,128)(2,1)S(1)}, bf16[256,1152]{1,0:T(8,128)(2,1)S(1)}, u32[]{:S(2)}, u32[]{:S(2)}) collective-permute-start(bf16[256,1152]{1,0:T(8,128)(2,1)S(1)} %bitcast.6), channel_id=1, source_target_pairs={{0,24},{1,25},{2,26},{3,27},{4,12},{5,13},{6,14},{7,15},{8,16},{9,... | collective-permute-start | bytes 1769480 | tf_op jit(solution)/shard_map/ppermute | solution.py:260
  17.3 11.9 %collective-permute-start.2 = (bf16[256,1152]{1,0:T(8,128)(2,1)S(1)}, bf16[256,1152]{1,0:T(8,128)(2,1)S(1)}, u32[]{:S(2)}, u32[]{:S(2)}) collective-permute-start(bf16[256,1152]{1,0:T(8,128)(2,1)S(1)} %bitcast.7), channel_id=1, source_target_pairs={{0,3},{1,2},{2,1},{3,0},{4,5},{5,4},{6,7},{7,6},{8,11},{9,10},{10,... | collective-permute-start | bytes 1769480 | tf_op jit(solution)/shard_map/ppermute | solution.py:260
  20.3 11.4 %collective-permute-start.4 = (bf16[256,1152]{1,0:T(8,128)(2,1)S(1)}, bf16[256,1152]{1,0:T(8,128)(2,1)S(1)}, u32[]{:S(2)}, u32[]{:S(2)}) collective-permute-start(bf16[256,1152]{1,0:T(8,128)(2,1)S(1)} %bitcast.8), channel_id=1, source_target_pairs={{0,96},{1,97},{2,98},{3,99},{4,36},{5,37},{6,38},{7,39},{8,104},{9... | collective-permute-start | bytes 1769480 | tf_op jit(solution)/shard_map/ppermute | solution.py:260
  23.3 0.7 copy-start
  26.4 11.2 %collective-permute-start.7 = (bf16[256,1152]{1,0:T(8,128)(2,1)S(1)}, bf16[256,1152]{1,0:T(8,128)(2,1)S(1)}, u32[]{:S(2)}, u32[]{:S(2)}) collective-permute-start(bf16[256,1152]{1,0:T(8,128)(2,1)S(1)} %collective-permute-done.6.refs_3_), channel_id=1, source_target_pairs={{0,3},{1,2},{2,1},{3,0},{4,5},{5,4},{6,7},{7,6},{8,11},{9,10},{10,... | collective-permute-start | bytes 1769480 | tf_op jit(solution)/shard_map/ppermute | solution.py:260
  29.2 11.1 %collective-permute-start.3 = (bf16[256,1152]{1,0:T(8,128)(2,1)S(1)}, bf16[256,1152]{1,0:T(8,128)(2,1)S(1)}, u32[]{:S(2)}, u32[]{:S(2)}) collective-permute-start(bf16[256,1152]{1,0:T(8,128)(2,1)S(1)} %collective-permute-done.2.refs_1_), channel_id=1, source_target_pairs={{0,96},{1,97},{2,98},{3,99},{4,36},{5,37},{6,38},{7,39},{8,104},{9... | collective-permute-start | bytes 1769480 | tf_op jit(solution)/shard_map/ppermute | solution.py:260
  31.7 11.1 %collective-permute-start.5 = (bf16[256,1152]{1,0:T(8,128)(2,1)S(1)}, bf16[256,1152]{1,0:T(8,128)(2,1)S(1)}, u32[]{:S(2)}, u32[]{:S(2)}) collective-permute-start(bf16[256,1152]{1,0:T(8,128)(2,1)S(1)} %collective-permute-done.4.refs_2_), channel_id=1, source_target_pairs={{0,24},{1,25},{2,26},{3,27},{4,12},{5,13},{6,14},{7,15},{8,16},{9,... | collective-permute-start | bytes 1769480 | tf_op jit(solution)/shard_map/ppermute | solution.py:260
  42.8 8.0 %collective-permute-start.8 = (bf16[128,1152]{1,0:T(8,128)(2,1)S(1)}, bf16[128,1152]{1,0:T(8,128)(2,1)S(1)}, u32[]{:S(2)}, u32[]{:S(2)}) collective-permute-start(bf16[128,1152]{1,0:T(8,128)(2,1)S(1)} %slice.6), channel_id=1, source_target_pairs={{0,24},{1,25},{2,26},{3,27},{4,12},{5,13},{6,14},{7,15},{8,16},{9,... | collective-permute-start | bytes 884744 | tf_op jit(solution)/shard_map/ppermute | solution.py:260
  45.7 8.0 %collective-permute-start.9 = (bf16[128,1152]{1,0:T(8,128)(2,1)S(1)}, bf16[128,1152]{1,0:T(8,128)(2,1)S(1)}, u32[]{:S(2)}, u32[]{:S(2)}) collective-permute-start(bf16[128,1152]{1,0:T(8,128)(2,1)S(1)} %slice.7), channel_id=1, source_target_pairs={{0,3},{1,2},{2,1},{3,0},{4,5},{5,4},{6,7},{7,6},{8,11},{9,10},{10,... | collective-permute-start | bytes 884744 | tf_op jit(solution)/shard_map/ppermute | solution.py:260
  56.2 15.3 %all-to-all-start.1 = ((f32[64,8,128]{2,1,0:T(8,128)}), f32[64,8,128]{2,1,0:T(8,128)S(1)}, u32[]{:S(2)}, u32[]{:S(2)}) async-start(f32[64,8,128]{2,1,0:T(8,128)} %score_last.1), calls=%async_computation.1 | async-start | bytes 524288 | tf_op jit(solution)/shard_map/all_to_all | solution.py:305

commit v4 on v3

--- a/solution.py
+++ b/solution.py
@@ -16,8 +16,8 @@
 BF16 = jnp.bfloat16
 
 PAIRING = {"a": (1, 0, 3, 2), "b": (3, 2, 1, 0)}
-DIMS_A = ("za", "ya", "xa")
-DIMS_B = ("zb", "yb", "xb")
+DIMS_A = ("za", "ya", "xb")
+DIMS_B = ("zb", "yb", "xa")
 
 
 def moved(device, dim):
@@ -50,19 +50,20 @@
 NEAR_GROUPS = [group[start : start + 8] for group in CORE_GROUPS for start in range(0, N_CORE, 8)]
 CORE_SWAP = [(device, device ^ 4) for device in range(N_DEV)]
 FIRST_HALF = (0, 1, 2, 4)
-SECOND_HALF = (3, 6, 5)
-
-
-def pairing_bits(place, core):
+SECOND_HALF = (5, 3, 6)
+
+
+def pairing_bits(place, core, axis):
     low, high = (place ^ (place >> 1)) & 1, place >> 1
-    even = jnp.equal(core, 0)
-    return jnp.where(even, low, high), jnp.where(even, high, low)
+    low_first = jnp.equal(core, 0 if axis + "a" in DIMS_A else 1)
+    return jnp.where(low_first, low, high), jnp.where(low_first, high, low)
 
 
 def own_group():
     owner = lax.axis_index("owner")
-    bits = [pairing_bits(place, owner & 1)[1] for place in (lax.axis_index("replica"), owner >> 3, (owner >> 1) & 3)]
-    return bits[0] + 2 * bits[1] + 4 * bits[2]
+    places = {"z": lax.axis_index("replica"), "y": owner >> 3, "x": (owner >> 1) & 3}
+    z, y, x = [pairing_bits(place, owner & 1, axis)[1] for axis, place in places.items()]
+    return z + 2 * y + 4 * x
 
 
 def sort_pairs(count):
@@ -137,7 +138,8 @@
         where = jnp.sum(placed * index.astype(F32), 0, keepdims=True).astype(jnp.int32)
         slot = jnp.sum(placed * rank, 0, keepdims=True).astype(jnp.int32)
         chip = where >> 3
-        (y_first, y_second), (x_first, x_second) = [pairing_bits(place, core) for place in (chip >> 2, chip & 3)]
+        y_first, y_second = pairing_bits(chip >> 2, core, "y")
+        x_first, x_second = pairing_bits(chip & 3, core, "x")
         row = (x_second * 8 + y_second * 4 + x_first * 2 + y_first) * 8 + (where & 4) + slot
         pick_ref[:, 32 * j : 32 * j + 32] = (index == row).astype(BF16)
         group_ref[:, 32 * j : 32 * j + 32] = jnp.broadcast_to(where & 3, (8, 32))
@@ -290,8 +292,8 @@
         )(*[groups[mask] for mask in masks], lists, norms)
 
     first = scored(FIRST_HALF, "score_first")
-    groups[3], groups[6], groups[5], first = lax.optimization_barrier((groups[3], groups[6], groups[5], first))
-    last = [hop(groups[3][:128], 4), hop(groups[6][128:], 1)]
+    groups[5], first = lax.optimization_barrier((groups[5], first))
+    last = [hop(groups[5][:128], 2), hop(groups[3][128:], 4)]
     second = scored(SECOND_HALF, "score_second")
     *last, second = lax.optimization_barrier((*last, second))
     blocks = pl.pallas_call(

time: 73.3 us -> 70.1 us (0.956)
  starting transfers between devices: 34.6 us -> 30 us
  waiting for transfers between devices: 22.1 us -> 23.4 us
    ppermute x8, starting transfers between devices: 19.4 us -> 13.7 us  [hop(): lax.ppermute(value, AXES, [(device, far(device, mask, False)) for device...]
    all_to_all x1, waiting for transfers between devices: 1.93 us -> 5.68 us  [per_device(): lax.all_to_all(wide, AXES, 0, 0, axis_index_groups=NEAR_GROUPS, tiled=True)]
    ppermute x1, starting transfers between devices: 5.05 us -> 2.52 us  [per_device(): sibling_valid = lax.ppermute(valid_rows, AXES, CORE_SWAP)]
    all_to_all x1, starting transfers between devices: 4.95 us -> 7.36 us  [per_device(): lax.all_to_all(blocks, AXES, 0, 0, axis_index_groups=CORE_GROUPS, tiled=T...]
    ppermute x8, waiting for transfers between devices: 10.1 us -> 7.81 us  [hop(): lax.ppermute(value, AXES, [(device, far(device, mask, False)) for device...]
    all_to_all x1, starting transfers between devices: 5.22 us -> 6.48 us  [per_device(): lax.all_to_all(wide, AXES, 0, 0, axis_index_groups=NEAR_GROUPS, tiled=True)]
  transfers between devices with their start and end apart: 12 -> 12, of which waited for: 8 -> 9; matrix products, arithmetic and copies ran while one was open for 0% -> 0% of each run, Pallas kernels for 16% -> 17%
where the time goes in v4:
time: 70.1 us; the launch traced here: 69.7 us
  starting transfers between devices  30 us (43%)
  waiting for transfers between devices  23.4 us (33%)
  Pallas kernels  15.5 us (22%)
    ppermute x8, starting transfers between devices, hop(): lax.ppermute(value, AXES, [(device, far(device, mask, False)) for device...  13.7 us
    all_to_all x1, waiting for transfers between devices, per_device(): lax.all_to_all(blocks, AXES, 0, 0, axis_index_groups=CORE_GROUPS, tiled=T...  8.98 us
    ppermute x8, waiting for transfers between devices, hop(): lax.ppermute(value, AXES, [(device, far(device, mask, False)) for device...  7.81 us
    all_to_all x1, starting transfers between devices, per_device(): lax.all_to_all(blocks, AXES, 0, 0, axis_index_groups=CORE_GROUPS, tiled=T...  7.36 us
    all_to_all x1, starting transfers between devices, per_device(): lax.all_to_all(wide, AXES, 0, 0, axis_index_groups=NEAR_GROUPS, tiled=True)  6.48 us
    pallas_call x2, Pallas kernels, scored(): pl.pallas_call(score_kernel, out_shape=shape((2, 128, 128), F32), in_spec...  5.92 us
    all_to_all x1, waiting for transfers between devices, per_device(): lax.all_to_all(wide, AXES, 0, 0, axis_index_groups=NEAR_GROUPS, tiled=True)  5.68 us
    pallas_call x1, Pallas kernels, per_device(): pl.pallas_call(last_kernel, out_shape=shape((N_CORE, 8, 128), F32), in_sp...  2.54 us
  transfers between devices with their start and end apart: 12, of which 9 were waited for; matrix products, arithmetic and copies ran while one was open for 0% of the time, Pallas kernels for 17%

profile of v4, /device:TPU:0, one launch (start us, length us, event | category | flops | bytes accessed | tf_op | source)
XLA Modules:
  0.0 69.7 jit_solution(8497568166185077960)
XLA Ops:
  0.0 0.0 collective-permute-start
  0.0 2.0 %widen.1 = bf16[8,32,1152]{2,1,0:T(8,128)(2,1)} custom-call(bf16[32,1024]{1,0:T(8,128)(2,1)} %queries_ref.1, s32[8,32]{1,0:T(8,128)} %bitcast.13, s32[1,128]{1,0:T(1,128)} %bitcast.15), custom_call_target="tpu_custom_call" | custom-call | tf_op jit(solution)/shard_map/widen/pallas_call | solution.py:269
  2.0 6.5 %all-to-all-start = ((bf16[8,32,1152]{2,1,0:T(8,128)(2,1)}), bf16[8,32,1152]{2,1,0:T(8,128)(2,1)S(1)}, u32[]{:S(2)}, u32[]{:S(2)}) async-start(bf16[8,32,1152]{2,1,0:T(8,128)(2,1)} %widen.1), calls=%async_computation | async-start | bytes 1179648 | tf_op jit(solution)/shard_map/all_to_all | solution.py:272
  8.5 2.5 %collective-permute-start.1 = (s32[4]{0:T(128)}, s32[4]{0:T(128)S(1)}, u32[]{:S(2)}, u32[]{:S(2)}) collective-permute-start(s32[4]{0:T(128)} %param.8), channel_id=1, source_target_pairs={{0,4},{1,5},{2,6},{3,7},{4,0},{5,1},{6,2},{7,3},{8,12},{9,13},{10,... | collective-permute-start | bytes 56 | tf_op jit(solution)/shard_map/ppermute | solution.py:274
  11.0 1.0 %collective-permute-done.1 = s32[4]{0:T(128)S(1)} collective-permute-done((s32[4]{0:T(128)}, s32[4]{0:T(128)S(1)}, u32[]{:S(2)}, u32[]{:S(2)}) %collective-permute-start.1) | collective-permute-done | bytes 48 | tf_op jit(solution)/shard_map/ppermute | solution.py:274
  12.0 5.7 %all-to-all-done = bf16[8,32,1152]{2,1,0:T(8,128)(2,1)S(1)} async-done(((bf16[8,32,1152]{2,1,0:T(8,128)(2,1)}), bf16[8,32,1152]{2,1,0:T(8,128)(2,1)S(1)}, u32[]{:S(2)}, u32[]{:S(2)}) %all-to-all-start) | async-done | bytes 589856 | tf_op jit(solution)/shard_map/all_to_all | solution.py:272
  17.7 0.0 collective-permute-done.sibling
  17.7 0.0 collective-permute-start.2
  17.7 2.7 %collective-permute-start.4 = (bf16[256,1152]{1,0:T(8,128)(2,1)S(1)}, bf16[256,1152]{1,0:T(8,128)(2,1)S(1)}, u32[]{:S(2)}, u32[]{:S(2)}) collective-permute-start(bf16[256,1152]{1,0:T(8,128)(2,1)S(1)} %bitcast.7), channel_id=1, source_target_pairs={{0,3},{1,2},{2,1},{3,0},{4,5},{5,4},{6,7},{7,6},{8,11},{9,10},{10,... | collective-permute-start | bytes 1769480 | tf_op jit(solution)/shard_map/ppermute | solution.py:262
  20.4 2.2 %collective-permute-start.5 = (bf16[256,1152]{1,0:T(8,128)(2,1)S(1)}, bf16[256,1152]{1,0:T(8,128)(2,1)S(1)}, u32[]{:S(2)}, u32[]{:S(2)}) collective-permute-start(bf16[256,1152]{1,0:T(8,128)(2,1)S(1)} %bitcast.8), channel_id=1, source_target_pairs={{0,96},{1,97},{2,98},{3,99},{4,36},{5,37},{6,38},{7,39},{8,104},{9... | collective-permute-start | bytes 1769480 | tf_op jit(solution)/shard_map/ppermute | solution.py:262
  22.5 0.7 copy-done
  23.2 2.3 %lists.1 = (bf16[8,256,1024]{2,1,0:T(8,128)(2,1)S(1)}, f32[256,128]{1,0:T(8,128)S(1)}) custom-call(bf16[4,256,1024]{2,1,0:T(8,128)(2,1)} %own.1, bf16[4,256,1024]{2,1,0:T(8,128)(2,1)S(1)} %collective-permute-done.sibling, s32[1,4]{1,0:T(1,128)S(1)} %bitcast.11, s32[1,4]{1,0:T(1,128)S(1)} %bitcast.12), custom_call_target="tpu_custom_call" | custom-call | tf_op jit(solution)/shard_map/lists/pallas_call | solution.py:280
  25.5 2.0 %collective-permute-done.2.refs_3_ = bf16[256,1152]{1,0:T(8,128)(2,1)S(1)} collective-permute-done((bf16[256,1152]{1,0:T(8,128)(2,1)S(1)}, bf16[256,1152]{1,0:T(8,128)(2,1)S(1)}, u32[]{:S(2)}, u32[]{:S(2)}) %collective-permute-start.2) | collective-permute-done | bytes 589856 | tf_op jit(solution)/shard_map/ppermute | solution.py:262
  27.5 2.7 %collective-permute-start.3 = (bf16[256,1152]{1,0:T(8,128)(2,1)S(1)}, bf16[256,1152]{1,0:T(8,128)(2,1)S(1)}, u32[]{:S(2)}, u32[]{:S(2)}) collective-permute-start(bf16[256,1152]{1,0:T(8,128)(2,1)S(1)} %collective-permute-done.2.refs_3_), channel_id=1, source_target_pairs={{0,3},{1,2},{2,1},{3,0},{4,5},{5,4},{6,7},{7,6},{8,11},{9,10},{10,... | collective-permute-start | bytes 1769480 | tf_op jit(solution)/shard_map/ppermute | solution.py:262
  30.2 0.0 collective-permute-done.4.refs_1_
  30.2 2.2 %collective-permute-start.7 = (bf16[256,1152]{1,0:T(8,128)(2,1)S(1)}, bf16[256,1152]{1,0:T(8,128)(2,1)S(1)}, u32[]{:S(2)}, u32[]{:S(2)}) collective-permute-start(bf16[256,1152]{1,0:T(8,128)(2,1)S(1)} %collective-permute-done.4.refs_1_), channel_id=1, source_target_pairs={{0,96},{1,97},{2,98},{3,99},{4,36},{5,37},{6,38},{7,39},{8,104},{9... | collective-permute-start | bytes 1769480 | tf_op jit(solution)/shard_map/ppermute | solution.py:262
  32.4 0.0 collective-permute-done.5.refs_2_
  32.4 1.0 %collective-permute-start.9 = (bf16[256,1152]{1,0:T(8,128)(2,1)S(1)}, bf16[256,1152]{1,0:T(8,128)(2,1)S(1)}, u32[]{:S(2)}, u32[]{:S(2)}) collective-permute-start(bf16[256,1152]{1,0:T(8,128)(2,1)S(1)} %collective-permute-done.5.refs_2_), channel_id=1, source_target_pairs={{0,8},{1,9},{2,10},{3,11},{4,28},{5,29},{6,30},{7,31},{8,0},{9,1},... | collective-permute-start | bytes 1769480 | tf_op jit(solution)/shard_map/ppermute | solution.py:262
  33.5 3.1 %score_first.1.first = f32[2,128,128]{2,1,0:T(8,128)S(1)} custom-call(bf16[256,1152]{1,0:T(8,128)(2,1)S(1)} %bitcast.9, bf16[256,1152]{1,0:T(8,128)(2,1)S(1)} %collective-permute-done.4.refs_1_, bf16[256,1152]{1,0:T(8,128)(2,1)S(1)} %collective-permute-done.5.refs_2_, bf16[256,1152]{1,0:T(8,128)(2,1)S(1)} %collective-permute-done.2.refs_3_, ...), custom_call_target="tpu_custom_call" | custom-call | tf_op jit(solution)/shard_map/score_first/pallas_call | solution.py:289
  36.6 2.1 %collective-permute-done.3.refs_0_ = bf16[256,1152]{1,0:T(8,128)(2,1)S(1)} collective-permute-done((bf16[256,1152]{1,0:T(8,128)(2,1)S(1)}, bf16[256,1152]{1,0:T(8,128)(2,1)S(1)}, u32[]{:S(2)}, u32[]{:S(2)}) %collective-permute-start.3) | collective-permute-done | bytes 589856 | tf_op jit(solution)/shard_map/ppermute | solution.py:262
  38.7 2.3 %collective-permute-start.6 = (bf16[128,1152]{1,0:T(8,128)(2,1)S(1)}, bf16[128,1152]{1,0:T(8,128)(2,1)S(1)}, u32[]{:S(2)}, u32[]{:S(2)}) collective-permute-start(bf16[128,1152]{1,0:T(8,128)(2,1)S(1)} %slice.6), channel_id=1, source_target_pairs={{0,96},{1,97},{2,98},{3,99},{4,36},{5,37},{6,38},{7,39},{8,104},{9... | collective-permute-start | bytes 884744 | tf_op jit(solution)/shard_map/ppermute | solution.py:262
  40.9 0.4 collective-permute-done.7.refs_1_
  41.4 0.6 collective-permute-start.8
  42.0 0.3 collective-permute-done.9.refs_2_
  42.3 2.8 %score_second.1.second = f32[2,128,128]{2,1,0:T(8,128)S(1)} custom-call(bf16[256,1152]{1,0:T(8,128)(2,1)S(1)} %collective-permute-done.3.refs_0_, bf16[256,1152]{1,0:T(8,128)(2,1)S(1)} %collective-permute-done.7.refs_1_, bf16[256,1152]{1,0:T(8,128)(2,1)S(1)} %collective-permute-done.9.refs_2_, ...), custom_call_target="tpu_custom_call" | custom-call | tf_op jit(solution)/shard_map/score_second/pallas_call | solution.py:289
  45.1 1.5 %collective-permute-done.6.lower = bf16[128,1152]{1,0:T(8,128)(2,1)S(1)} collective-permute-done((bf16[128,1152]{1,0:T(8,128)(2,1)S(1)}, bf16[128,1152]{1,0:T(8,128)(2,1)S(1)}, u32[]{:S(2)}, u32[]{:S(2)}) %collective-permute-start.6) | collective-permute-done | bytes 294944 | tf_op jit(solution)/shard_map/ppermute | solution.py:262
  46.7 1.5 %collective-permute-done.8.upper = bf16[128,1152]{1,0:T(8,128)(2,1)S(1)} collective-permute-done((bf16[128,1152]{1,0:T(8,128)(2,1)S(1)}, bf16[128,1152]{1,0:T(8,128)(2,1)S(1)}, u32[]{:S(2)}, u32[]{:S(2)}) %collective-permute-start.8) | collective-permute-done | bytes 294944 | tf_op jit(solution)/shard_map/ppermute | solution.py:262
  48.2 2.5 %score_last.1 = f32[64,8,128]{2,1,0:T(8,128)} custom-call(bf16[128,1152]{1,0:T(8,128)(2,1)S(1)} %collective-permute-done.6.lower, bf16[128,1152]{1,0:T(8,128)(2,1)S(1)} %collective-permute-done.8.upper, bf16[8,256,1024]{2,1,0:T(8,128)(2,1)S(1)} %get-tuple-element.26.refs_4_.refs_3_.lists, f32[256,128]{1,0:T(8,128)S(1)} %get-tuple-element.27.refs_5_.refs_4_.norms, ...), custom_call_target="tpu_custom_call" | custom-call | tf_op jit(solution)/shard_map/score_last/pallas_call | solution.py:299
  50.7 7.4 %all-to-all-start.1 = ((f32[64,8,128]{2,1,0:T(8,128)}), f32[64,8,128]{2,1,0:T(8,128)S(1)}, u32[]{:S(2)}, u32[]{:S(2)}) async-start(f32[64,8,128]{2,1,0:T(8,128)} %score_last.1), calls=%async_computation.1 | async-start | bytes 524288 | tf_op jit(solution)/shard_map/all_to_all | solution.py:307
  58.1 1.2 %wanted.1 = (bf16[128,256]{1,0:T(8,128)(2,1)S(1)}, s32[8,256]{1,0:T(8,128)S(1)}) custom-call(s32[8,32]{1,0:T(8,128)} %bitcast.14, s32[1,128]{1,0:T(1,128)} %bitcast.16), custom_call_target="tpu_custom_call" | custom-call | tf_op jit(solution)/shard_map/wanted/pallas_call | solution.py:303
  59.3 9.0 %all-to-all-done.1 = f32[64,8,128]{2,1,0:T(8,128)S(1)} async-done(((f32[64,8,128]{2,1,0:T(8,128)}), f32[64,8,128]{2,1,0:T(8,128)S(1)}, u32[]{:S(2)}, u32[]{:S(2)}) %all-to-all-start.1) | async-done | bytes 262176 | tf_op jit(solution)/shard_map/all_to_all | solution.py:307
  68.3 1.4 %final.1 = f32[32,32]{1,0:T(8,128)} custom-call(f32[4,2,4,2,8,128]{5,4,3,2,1,0:T(8,128)S(1)} %bitcast.10, bf16[128,256]{1,0:T(8,128)(2,1)S(1)} %get-tuple-element.33.pick_ref, s32[8,256]{1,0:T(8,128)S(1)} %get-tuple-element.34.group_ref), custom_call_target="tpu_custom_call" | custom-call | tf_op jit(solution)/shard_map/final/pallas_call | solution.py:308
  (3 shorter events, 0.0 us)
Async XLA Ops:
  0.0 17.7 %collective-permute-start = (bf16[4,256,1024]{2,1,0:T(8,128)(2,1)}, bf16[4,256,1024]{2,1,0:T(8,128)(2,1)S(1)}, u32[]{:S(2)}, u32[]{:S(2)}) collective-permute-start(bf16[4,256,1024]{2,1,0:T(8,128)(2,1)} %own.1), channel_id=1, source_target_pairs={{0,4},{1,5},{2,6},{3,7},{4,0},{5,1},{6,2},{7,3},{8,12},{9,13},{10,... | collective-permute-start | bytes 6291464 | tf_op jit(solution)/shard_map/ppermute | solution.py:273
  2.0 15.6 %all-to-all-start = ((bf16[8,32,1152]{2,1,0:T(8,128)(2,1)}), bf16[8,32,1152]{2,1,0:T(8,128)(2,1)S(1)}, u32[]{:S(2)}, u32[]{:S(2)}) async-start(bf16[8,32,1152]{2,1,0:T(8,128)(2,1)} %widen.1), calls=%async_computation | async-start | bytes 1179648 | tf_op jit(solution)/shard_map/all_to_all | solution.py:272
  8.5 3.5 %collective-permute-start.1 = (s32[4]{0:T(128)}, s32[4]{0:T(128)S(1)}, u32[]{:S(2)}, u32[]{:S(2)}) collective-permute-start(s32[4]{0:T(128)} %param.8), channel_id=1, source_target_pairs={{0,4},{1,5},{2,6},{3,7},{4,0},{5,1},{6,2},{7,3},{8,12},{9,13},{10,... | collective-permute-start | bytes 56 | tf_op jit(solution)/shard_map/ppermute | solution.py:274
  17.7 9.9 %collective-permute-start.2 = (bf16[256,1152]{1,0:T(8,128)(2,1)S(1)}, bf16[256,1152]{1,0:T(8,128)(2,1)S(1)}, u32[]{:S(2)}, u32[]{:S(2)}) collective-permute-start(bf16[256,1152]{1,0:T(8,128)(2,1)S(1)} %bitcast.6), channel_id=1, source_target_pairs={{0,8},{1,9},{2,10},{3,11},{4,28},{5,29},{6,30},{7,31},{8,0},{9,1},... | collective-permute-start | bytes 1769480 | tf_op jit(solution)/shard_map/ppermute | solution.py:262
  17.7 12.6 %collective-permute-start.4 = (bf16[256,1152]{1,0:T(8,128)(2,1)S(1)}, bf16[256,1152]{1,0:T(8,128)(2,1)S(1)}, u32[]{:S(2)}, u32[]{:S(2)}) collective-permute-start(bf16[256,1152]{1,0:T(8,128)(2,1)S(1)} %bitcast.7), channel_id=1, source_target_pairs={{0,3},{1,2},{2,1},{3,0},{4,5},{5,4},{6,7},{7,6},{8,11},{9,10},{10,... | collective-permute-start | bytes 1769480 | tf_op jit(solution)/shard_map/ppermute | solution.py:262
  20.4 12.1 %collective-permute-start.5 = (bf16[256,1152]{1,0:T(8,128)(2,1)S(1)}, bf16[256,1152]{1,0:T(8,128)(2,1)S(1)}, u32[]{:S(2)}, u32[]{:S(2)}) collective-permute-start(bf16[256,1152]{1,0:T(8,128)(2,1)S(1)} %bitcast.8), channel_id=1, source_target_pairs={{0,96},{1,97},{2,98},{3,99},{4,36},{5,37},{6,38},{7,39},{8,104},{9... | collective-permute-start | bytes 1769480 | tf_op jit(solution)/shard_map/ppermute | solution.py:262
  22.5 0.7 copy-start
  27.5 11.1 %collective-permute-start.3 = (bf16[256,1152]{1,0:T(8,128)(2,1)S(1)}, bf16[256,1152]{1,0:T(8,128)(2,1)S(1)}, u32[]{:S(2)}, u32[]{:S(2)}) collective-permute-start(bf16[256,1152]{1,0:T(8,128)(2,1)S(1)} %collective-permute-done.2.refs_3_), channel_id=1, source_target_pairs={{0,3},{1,2},{2,1},{3,0},{4,5},{5,4},{6,7},{7,6},{8,11},{9,10},{10,... | collective-permute-start | bytes 1769480 | tf_op jit(solution)/shard_map/ppermute | solution.py:262
  30.2 11.1 %collective-permute-start.7 = (bf16[256,1152]{1,0:T(8,128)(2,1)S(1)}, bf16[256,1152]{1,0:T(8,128)(2,1)S(1)}, u32[]{:S(2)}, u32[]{:S(2)}) collective-permute-start(bf16[256,1152]{1,0:T(8,128)(2,1)S(1)} %collective-permute-done.4.refs_1_), channel_id=1, source_target_pairs={{0,96},{1,97},{2,98},{3,99},{4,36},{5,37},{6,38},{7,39},{8,104},{9... | collective-permute-start | bytes 1769480 | tf_op jit(solution)/shard_map/ppermute | solution.py:262
  32.4 9.9 %collective-permute-start.9 = (bf16[256,1152]{1,0:T(8,128)(2,1)S(1)}, bf16[256,1152]{1,0:T(8,128)(2,1)S(1)}, u32[]{:S(2)}, u32[]{:S(2)}) collective-permute-start(bf16[256,1152]{1,0:T(8,128)(2,1)S(1)} %collective-permute-done.5.refs_2_), channel_id=1, source_target_pairs={{0,8},{1,9},{2,10},{3,11},{4,28},{5,29},{6,30},{7,31},{8,0},{9,1},... | collective-permute-start | bytes 1769480 | tf_op jit(solution)/shard_map/ppermute | solution.py:262
  38.7 8.0 %collective-permute-start.6 = (bf16[128,1152]{1,0:T(8,128)(2,1)S(1)}, bf16[128,1152]{1,0:T(8,128)(2,1)S(1)}, u32[]{:S(2)}, u32[]{:S(2)}) collective-permute-start(bf16[128,1152]{1,0:T(8,128)(2,1)S(1)} %slice.6), channel_id=1, source_target_pairs={{0,96},{1,97},{2,98},{3,99},{4,36},{5,37},{6,38},{7,39},{8,104},{9... | collective-permute-start | bytes 884744 | tf_op jit(solution)/shard_map/ppermute | solution.py:262
  41.4 6.8 %collective-permute-start.8 = (bf16[128,1152]{1,0:T(8,128)(2,1)S(1)}, bf16[128,1152]{1,0:T(8,128)(2,1)S(1)}, u32[]{:S(2)}, u32[]{:S(2)}) collective-permute-start(bf16[128,1152]{1,0:T(8,128)(2,1)S(1)} %slice.8), channel_id=1, source_target_pairs={{0,8},{1,9},{2,10},{3,11},{4,28},{5,29},{6,30},{7,31},{8,0},{9,1},... | collective-permute-start | bytes 884744 | tf_op jit(solution)/shard_map/ppermute | solution.py:262
  50.7 17.6 %all-to-all-start.1 = ((f32[64,8,128]{2,1,0:T(8,128)}), f32[64,8,128]{2,1,0:T(8,128)S(1)}, u32[]{:S(2)}, u32[]{:S(2)}) async-start(f32[64,8,128]{2,1,0:T(8,128)} %score_last.1), calls=%async_computation.1 | async-start | bytes 524288 | tf_op jit(solution)/shard_map/all_to_all | solution.py:307

commit v5 on v4

--- a/solution.py
+++ b/solution.py
@@ -51,6 +51,7 @@
 CORE_SWAP = [(device, device ^ 4) for device in range(N_DEV)]
 FIRST_HALF = (0, 1, 2, 4)
 SECOND_HALF = (5, 3, 6)
+SPLIT = 160
 
 
 def pairing_bits(place, core, axis):
@@ -271,8 +272,12 @@
     )(queries, probes, slots)
     near = lax.all_to_all(wide, AXES, 0, 0, axis_index_groups=NEAR_GROUPS, tiled=True).reshape(256, WIDE)
     sibling = lax.ppermute(database, AXES, CORE_SWAP)
+    pick, group = pl.pallas_call(
+        wanted_kernel, out_shape=(pltpu.VMEM((128, 256), BF16), pltpu.VMEM((8, 256), jnp.int32)), in_specs=spaces("vv"),
+        out_specs=spaces("vv"), name="wanted",
+    )(probes, slots)
+    near, valid_rows, pick, group = lax.optimization_barrier((near, valid_rows, pick, group))
     sibling_valid = lax.ppermute(valid_rows, AXES, CORE_SWAP)
-    near, sibling, sibling_valid = lax.optimization_barrier((near, sibling, sibling_valid))
 
     groups = {0: near}
     for mask in (1, 2, 4):
@@ -293,17 +298,13 @@
 
     first = scored(FIRST_HALF, "score_first")
     groups[5], first = lax.optimization_barrier((groups[5], first))
-    last = [hop(groups[5][:128], 2), hop(groups[3][128:], 4)]
+    last = [hop(groups[5][:SPLIT], 2), hop(groups[3][SPLIT:], 4)]
     second = scored(SECOND_HALF, "score_second")
     *last, second = lax.optimization_barrier((*last, second))
     blocks = pl.pallas_call(
         last_kernel, out_shape=shape((N_CORE, 8, 128), F32), in_specs=spaces("vvvvvv"), out_specs=spaces("v")[0],
         scratch_shapes=[pltpu.VMEM((256, 128), F32)], compiler_params=params(), name="score_last",
     )(*last, lists, norms, first, second)
-    pick, group = pl.pallas_call(
-        wanted_kernel, out_shape=(pltpu.VMEM((128, 256), BF16), pltpu.VMEM((8, 256), jnp.int32)), in_specs=spaces("vv"),
-        out_specs=spaces("vv"), name="wanted",
-    )(probes, slots)
     back = lax.all_to_all(blocks, AXES, 0, 0, axis_index_groups=CORE_GROUPS, tiled=True)
     return pl.pallas_call(
         final_kernel, out_shape=shape((32, TOPK), F32), in_specs=spaces("vvv"), out_specs=spaces("v")[0],

time: 70.1 us -> 68.5 us (0.977)
  blocking collectives: 0 us -> 17.4 us
  starting transfers between devices: 30 us -> 20.2 us
  waiting for transfers between devices: 23.4 us -> 15 us
    all_to_all x0 -> x1, blocking collectives: none -> 17.4 us  [per_device(): lax.all_to_all(blocks, AXES, 0, 0, axis_index_groups=CORE_GROUPS, tiled=T...]
    all_to_all x1 -> x0, waiting for transfers between devices: 8.98 us -> none  [per_device(): lax.all_to_all(blocks, AXES, 0, 0, axis_index_groups=CORE_GROUPS, tiled=T...]
    all_to_all x1 -> x0, starting transfers between devices: 7.36 us -> none  [per_device(): lax.all_to_all(blocks, AXES, 0, 0, axis_index_groups=CORE_GROUPS, tiled=T...]
    ppermute x1, starting transfers between devices: 2.52 us -> 0.01 us  [per_device(): sibling_valid = lax.ppermute(valid_rows, AXES, CORE_SWAP)]
    all_to_all x1, waiting for transfers between devices: 5.68 us -> 7.9 us  [per_device(): lax.all_to_all(wide, AXES, 0, 0, axis_index_groups=NEAR_GROUPS, tiled=True)]
    ppermute x8, waiting for transfers between devices: 7.81 us -> 5.87 us  [hop(): lax.ppermute(value, AXES, [(device, far(device, mask, False)) for device...]
    pallas_call x1, Pallas kernels: 2.54 us -> 1.84 us  [per_device(): pl.pallas_call(last_kernel, out_shape=shape((N_CORE, 8, 128), F32), in_sp...]
  transfers between devices with their start and end apart: 12 -> 11, of which waited for: 9 -> 8; matrix products, arithmetic and copies ran while one was open for 0% -> 0% of each run, Pallas kernels for 17% -> 17%
where the time goes in v5:
time: 68.5 us; the launch traced here: 68.2 us
  starting transfers between devices  20.2 us (29%)
  blocking collectives  17.4 us (25%)
  waiting for transfers between devices  15 us (22%)
  Pallas kernels  14.8 us (22%)
  local copies, waits for them, and re-layouts  0.7 us (1%)
    all_to_all x1, blocking collectives, per_device(): lax.all_to_all(blocks, AXES, 0, 0, axis_index_groups=CORE_GROUPS, tiled=T...  17.4 us
    ppermute x8, starting transfers between devices, hop(): lax.ppermute(value, AXES, [(device, far(device, mask, False)) for device...  13.7 us
    all_to_all x1, waiting for transfers between devices, per_device(): lax.all_to_all(wide, AXES, 0, 0, axis_index_groups=NEAR_GROUPS, tiled=True)  7.9 us
    all_to_all x1, starting transfers between devices, per_device(): lax.all_to_all(wide, AXES, 0, 0, axis_index_groups=NEAR_GROUPS, tiled=True)  6.48 us
    pallas_call x2, Pallas kernels, scored(): pl.pallas_call(score_kernel, out_shape=shape((2, 128, 128), F32), in_spec...  5.93 us
    ppermute x8, waiting for transfers between devices, hop(): lax.ppermute(value, AXES, [(device, far(device, mask, False)) for device...  5.87 us
    pallas_call x1, Pallas kernels, per_device(): pl.pallas_call(lists_kernel, out_shape=(pltpu.VMEM((8, 256, D), BF16), pl...  2.35 us
    pallas_call x1, Pallas kernels, per_device(): pl.pallas_call(widen_kernel, out_shape=shape((8, 32, WIDE), BF16), in_spe...  2.03 us
  transfers between devices with their start and end apart: 11, of which 8 were waited for; matrix products, arithmetic and copies ran while one was open for 0% of the time, Pallas kernels for 17%

profile of v5, /device:TPU:0, one launch (start us, length us, event | category | flops | bytes accessed | tf_op | source)
XLA Modules:
  0.0 68.2 jit_solution(7793336688193422349)
XLA Ops:
  0.0 0.0 collective-permute-start.1
  0.0 2.0 %widen.1 = bf16[8,32,1152]{2,1,0:T(8,128)(2,1)} custom-call(bf16[32,1024]{1,0:T(8,128)(2,1)} %queries_ref.1, s32[8,32]{1,0:T(8,128)} %bitcast.13, s32[1,128]{1,0:T(1,128)} %bitcast.15), custom_call_target="tpu_custom_call" | custom-call | tf_op jit(solution)/shard_map/widen/pallas_call | solution.py:270
  2.0 6.5 %all-to-all-start = ((bf16[8,32,1152]{2,1,0:T(8,128)(2,1)}), bf16[8,32,1152]{2,1,0:T(8,128)(2,1)S(1)}, u32[]{:S(2)}, u32[]{:S(2)}) async-start(bf16[8,32,1152]{2,1,0:T(8,128)(2,1)} %widen.1), calls=%async_computation | async-start | bytes 1179648 | tf_op jit(solution)/shard_map/all_to_all | solution.py:273
  8.5 1.2 %wanted.1 = (bf16[128,256]{1,0:T(8,128)(2,1)S(1)}, s32[8,256]{1,0:T(8,128)S(1)}) custom-call(s32[8,32]{1,0:T(8,128)} %bitcast.14, s32[1,128]{1,0:T(1,128)} %bitcast.16), custom_call_target="tpu_custom_call" | custom-call | tf_op jit(solution)/shard_map/wanted/pallas_call | solution.py:275
  9.8 7.9 %all-to-all-done = bf16[8,32,1152]{2,1,0:T(8,128)(2,1)S(1)} async-done(((bf16[8,32,1152]{2,1,0:T(8,128)(2,1)}), bf16[8,32,1152]{2,1,0:T(8,128)(2,1)S(1)}, u32[]{:S(2)}, u32[]{:S(2)}) %all-to-all-start) | async-done | bytes 589856 | tf_op jit(solution)/shard_map/all_to_all | solution.py:273
  17.7 0.0 collective-permute-start
  17.7 2.7 %collective-permute-start.4 = (bf16[256,1152]{1,0:T(8,128)(2,1)S(1)}, bf16[256,1152]{1,0:T(8,128)(2,1)S(1)}, u32[]{:S(2)}, u32[]{:S(2)}) collective-permute-start(bf16[256,1152]{1,0:T(8,128)(2,1)S(1)} %bitcast.7), channel_id=1, source_target_pairs={{0,3},{1,2},{2,1},{3,0},{4,5},{5,4},{6,7},{7,6},{8,11},{9,10},{10,... | collective-permute-start | bytes 1769480 | tf_op jit(solution)/shard_map/ppermute | solution.py:263
  20.4 2.2 %collective-permute-start.5 = (bf16[256,1152]{1,0:T(8,128)(2,1)S(1)}, bf16[256,1152]{1,0:T(8,128)(2,1)S(1)}, u32[]{:S(2)}, u32[]{:S(2)}) collective-permute-start(bf16[256,1152]{1,0:T(8,128)(2,1)S(1)} %bitcast.8), channel_id=1, source_target_pairs={{0,96},{1,97},{2,98},{3,99},{4,36},{5,37},{6,38},{7,39},{8,104},{9... | collective-permute-start | bytes 1769480 | tf_op jit(solution)/shard_map/ppermute | solution.py:263
  22.5 0.0 collective-permute-start.2
  22.5 1.3 %collective-permute-done.2 = s32[4]{0:T(128)S(1)} collective-permute-done((s32[4]{0:T(128)}, s32[4]{0:T(128)S(1)}, u32[]{:S(2)}, u32[]{:S(2)}) %collective-permute-start.2) | collective-permute-done | bytes 48 | tf_op jit(solution)/shard_map/ppermute | solution.py:280
  23.8 0.0 collective-permute-done.1.sibling
  23.8 0.0 copy-start
  23.8 0.7 copy-done
  24.5 2.3 %lists.1 = (bf16[8,256,1024]{2,1,0:T(8,128)(2,1)S(1)}, f32[256,128]{1,0:T(8,128)S(1)}) custom-call(bf16[4,256,1024]{2,1,0:T(8,128)(2,1)} %own.1, bf16[4,256,1024]{2,1,0:T(8,128)(2,1)S(1)} %collective-permute-done.1.sibling, s32[1,4]{1,0:T(1,128)S(1)} %bitcast.11, s32[1,4]{1,0:T(1,128)S(1)} %bitcast.12), custom_call_target="tpu_custom_call" | custom-call | tf_op jit(solution)/shard_map/lists/pallas_call | solution.py:285
  26.8 0.7 %collective-permute-done.refs_3_ = bf16[256,1152]{1,0:T(8,128)(2,1)S(1)} collective-permute-done((bf16[256,1152]{1,0:T(8,128)(2,1)S(1)}, bf16[256,1152]{1,0:T(8,128)(2,1)S(1)}, u32[]{:S(2)}, u32[]{:S(2)}) %collective-permute-start) | collective-permute-done | bytes 589856 | tf_op jit(solution)/shard_map/ppermute | solution.py:263
  27.6 2.7 %collective-permute-start.3 = (bf16[256,1152]{1,0:T(8,128)(2,1)S(1)}, bf16[256,1152]{1,0:T(8,128)(2,1)S(1)}, u32[]{:S(2)}, u32[]{:S(2)}) collective-permute-start(bf16[256,1152]{1,0:T(8,128)(2,1)S(1)} %collective-permute-done.refs_3_), channel_id=1, source_target_pairs={{0,3},{1,2},{2,1},{3,0},{4,5},{5,4},{6,7},{7,6},{8,11},{9,10},{10,... | collective-permute-start | bytes 1769480 | tf_op jit(solution)/shard_map/ppermute | solution.py:263
  30.2 0.0 collective-permute-done.4.refs_1_
  30.2 2.2 %collective-permute-start.7 = (bf16[256,1152]{1,0:T(8,128)(2,1)S(1)}, bf16[256,1152]{1,0:T(8,128)(2,1)S(1)}, u32[]{:S(2)}, u32[]{:S(2)}) collective-permute-start(bf16[256,1152]{1,0:T(8,128)(2,1)S(1)} %collective-permute-done.4.refs_1_), channel_id=1, source_target_pairs={{0,96},{1,97},{2,98},{3,99},{4,36},{5,37},{6,38},{7,39},{8,104},{9... | collective-permute-start | bytes 1769480 | tf_op jit(solution)/shard_map/ppermute | solution.py:263
  32.4 0.0 collective-permute-done.5.refs_2_
  32.4 1.0 %collective-permute-start.9 = (bf16[256,1152]{1,0:T(8,128)(2,1)S(1)}, bf16[256,1152]{1,0:T(8,128)(2,1)S(1)}, u32[]{:S(2)}, u32[]{:S(2)}) collective-permute-start(bf16[256,1152]{1,0:T(8,128)(2,1)S(1)} %collective-permute-done.5.refs_2_), channel_id=1, source_target_pairs={{0,8},{1,9},{2,10},{3,11},{4,28},{5,29},{6,30},{7,31},{8,0},{9,1},... | collective-permute-start | bytes 1769480 | tf_op jit(solution)/shard_map/ppermute | solution.py:263
  33.5 3.1 %score_first.1.first = f32[2,128,128]{2,1,0:T(8,128)S(1)} custom-call(bf16[256,1152]{1,0:T(8,128)(2,1)S(1)} %bitcast.9, bf16[256,1152]{1,0:T(8,128)(2,1)S(1)} %collective-permute-done.4.refs_1_, bf16[256,1152]{1,0:T(8,128)(2,1)S(1)} %collective-permute-done.5.refs_2_, bf16[256,1152]{1,0:T(8,128)(2,1)S(1)} %collective-permute-done.refs_3_, ...), custom_call_target="tpu_custom_call" | custom-call | tf_op jit(solution)/shard_map/score_first/pallas_call | solution.py:294
  36.6 2.1 %collective-permute-done.3.refs_0_ = bf16[256,1152]{1,0:T(8,128)(2,1)S(1)} collective-permute-done((bf16[256,1152]{1,0:T(8,128)(2,1)S(1)}, bf16[256,1152]{1,0:T(8,128)(2,1)S(1)}, u32[]{:S(2)}, u32[]{:S(2)}) %collective-permute-start.3) | collective-permute-done | bytes 589856 | tf_op jit(solution)/shard_map/ppermute | solution.py:263
  38.7 2.3 %collective-permute-start.6 = (bf16[160,1152]{1,0:T(8,128)(2,1)S(1)}, bf16[160,1152]{1,0:T(8,128)(2,1)S(1)}, u32[]{:S(2)}, u32[]{:S(2)}) collective-permute-start(bf16[160,1152]{1,0:T(8,128)(2,1)S(1)} %slice.6), channel_id=1, source_target_pairs={{0,96},{1,97},{2,98},{3,99},{4,36},{5,37},{6,38},{7,39},{8,104},{9... | collective-permute-start | bytes 1105928 | tf_op jit(solution)/shard_map/ppermute | solution.py:263
  40.9 0.4 collective-permute-done.7.refs_1_
  41.4 0.6 collective-permute-start.8
  42.0 0.3 collective-permute-done.9.refs_2_
  42.3 2.8 %score_second.1.second = f32[2,128,128]{2,1,0:T(8,128)S(1)} custom-call(bf16[256,1152]{1,0:T(8,128)(2,1)S(1)} %collective-permute-done.3.refs_0_, bf16[256,1152]{1,0:T(8,128)(2,1)S(1)} %collective-permute-done.7.refs_1_, bf16[256,1152]{1,0:T(8,128)(2,1)S(1)} %collective-permute-done.9.refs_2_, ...), custom_call_target="tpu_custom_call" | custom-call | tf_op jit(solution)/shard_map/score_second/pallas_call | solution.py:294
  45.1 2.2 %collective-permute-done.8.upper = bf16[96,1152]{1,0:T(8,128)(2,1)S(1)} collective-permute-done((bf16[96,1152]{1,0:T(8,128)(2,1)S(1)}, bf16[96,1152]{1,0:T(8,128)(2,1)S(1)}, u32[]{:S(2)}, u32[]{:S(2)}) %collective-permute-start.8) | collective-permute-done | bytes 221216 | tf_op jit(solution)/shard_map/ppermute | solution.py:263
  47.4 0.1 collective-permute-done.6.lower
  47.5 1.8 %score_last.1 = f32[64,8,128]{2,1,0:T(8,128)S(1)} custom-call(bf16[160,1152]{1,0:T(8,128)(2,1)S(1)} %collective-permute-done.6.lower, bf16[96,1152]{1,0:T(8,128)(2,1)S(1)} %collective-permute-done.8.upper, bf16[8,256,1024]{2,1,0:T(8,128)(2,1)S(1)} %get-tuple-element.28.refs_4_.refs_3_.lists, f32[256,128]{1,0:T(8,128)S(1)} %get-tuple-element.29.refs_5_.refs_4_.norms, ...), custom_call_target="tpu_custom_call" | custom-call | tf_op jit(solution)/shard_map/score_last/pallas_call | solution.py:304
  49.3 17.4 %all_to_all.10 = f32[64,8,128]{2,1,0:T(8,128)S(1)} all-to-all(f32[64,8,128]{2,1,0:T(8,128)S(1)} %score_last.1), channel_id=1, replica_groups={{0,1,32,33,24,25,56,57,3,2,35,34,27,26,59,58,96,97,64,65,120,121,88,89,..., dimensions={0} | all-to-all | bytes 524288 | tf_op jit(solution)/shard_map/all_to_all | solution.py:308
  66.8 1.4 %final.1 = f32[32,32]{1,0:T(8,128)} custom-call(f32[4,2,4,2,8,128]{5,4,3,2,1,0:T(8,128)S(1)} %bitcast.10, bf16[128,256]{1,0:T(8,128)(2,1)S(1)} %get-tuple-element.35.pick_ref, s32[8,256]{1,0:T(8,128)S(1)} %get-tuple-element.36.group_ref), custom_call_target="tpu_custom_call" | custom-call | tf_op jit(solution)/shard_map/final/pallas_call | solution.py:309
  (2 shorter events, 0.0 us)
Async XLA Ops:
  0.0 23.8 %collective-permute-start.1 = (bf16[4,256,1024]{2,1,0:T(8,128)(2,1)}, bf16[4,256,1024]{2,1,0:T(8,128)(2,1)S(1)}, u32[]{:S(2)}, u32[]{:S(2)}) collective-permute-start(bf16[4,256,1024]{2,1,0:T(8,128)(2,1)} %own.1), channel_id=1, source_target_pairs={{0,4},{1,5},{2,6},{3,7},{4,0},{5,1},{6,2},{7,3},{8,12},{9,13},{10,... | collective-permute-start | bytes 6291464 | tf_op jit(solution)/shard_map/ppermute | solution.py:274
  2.0 15.6 %all-to-all-start = ((bf16[8,32,1152]{2,1,0:T(8,128)(2,1)}), bf16[8,32,1152]{2,1,0:T(8,128)(2,1)S(1)}, u32[]{:S(2)}, u32[]{:S(2)}) async-start(bf16[8,32,1152]{2,1,0:T(8,128)(2,1)} %widen.1), calls=%async_computation | async-start | bytes 1179648 | tf_op jit(solution)/shard_map/all_to_all | solution.py:273
  17.7 9.9 %collective-permute-start = (bf16[256,1152]{1,0:T(8,128)(2,1)S(1)}, bf16[256,1152]{1,0:T(8,128)(2,1)S(1)}, u32[]{:S(2)}, u32[]{:S(2)}) collective-permute-start(bf16[256,1152]{1,0:T(8,128)(2,1)S(1)} %bitcast.6), channel_id=1, source_target_pairs={{0,8},{1,9},{2,10},{3,11},{4,28},{5,29},{6,30},{7,31},{8,0},{9,1},... | collective-permute-start | bytes 1769480 | tf_op jit(solution)/shard_map/ppermute | solution.py:263
  17.7 12.6 %collective-permute-start.4 = (bf16[256,1152]{1,0:T(8,128)(2,1)S(1)}, bf16[256,1152]{1,0:T(8,128)(2,1)S(1)}, u32[]{:S(2)}, u32[]{:S(2)}) collective-permute-start(bf16[256,1152]{1,0:T(8,128)(2,1)S(1)} %bitcast.7), channel_id=1, source_target_pairs={{0,3},{1,2},{2,1},{3,0},{4,5},{5,4},{6,7},{7,6},{8,11},{9,10},{10,... | collective-permute-start | bytes 1769480 | tf_op jit(solution)/shard_map/ppermute | solution.py:263
  20.4 12.1 %collective-permute-start.5 = (bf16[256,1152]{1,0:T(8,128)(2,1)S(1)}, bf16[256,1152]{1,0:T(8,128)(2,1)S(1)}, u32[]{:S(2)}, u32[]{:S(2)}) collective-permute-start(bf16[256,1152]{1,0:T(8,128)(2,1)S(1)} %bitcast.8), channel_id=1, source_target_pairs={{0,96},{1,97},{2,98},{3,99},{4,36},{5,37},{6,38},{7,39},{8,104},{9... | collective-permute-start | bytes 1769480 | tf_op jit(solution)/shard_map/ppermute | solution.py:263
  22.5 1.3 %collective-permute-start.2 = (s32[4]{0:T(128)}, s32[4]{0:T(128)S(1)}, u32[]{:S(2)}, u32[]{:S(2)}) collective-permute-start(s32[4]{0:T(128)} %param.8), channel_id=1, source_target_pairs={{0,4},{1,5},{2,6},{3,7},{4,0},{5,1},{6,2},{7,3},{8,12},{9,13},{10,... | collective-permute-start | bytes 56 | tf_op jit(solution)/shard_map/ppermute | solution.py:280
  23.8 0.7 copy-start
  27.6 11.1 %collective-permute-start.3 = (bf16[256,1152]{1,0:T(8,128)(2,1)S(1)}, bf16[256,1152]{1,0:T(8,128)(2,1)S(1)}, u32[]{:S(2)}, u32[]{:S(2)}) collective-permute-start(bf16[256,1152]{1,0:T(8,128)(2,1)S(1)} %collective-permute-done.refs_3_), channel_id=1, source_target_pairs={{0,3},{1,2},{2,1},{3,0},{4,5},{5,4},{6,7},{7,6},{8,11},{9,10},{10,... | collective-permute-start | bytes 1769480 | tf_op jit(solution)/shard_map/ppermute | solution.py:263
  30.2 11.1 %collective-permute-start.7 = (bf16[256,1152]{1,0:T(8,128)(2,1)S(1)}, bf16[256,1152]{1,0:T(8,128)(2,1)S(1)}, u32[]{:S(2)}, u32[]{:S(2)}) collective-permute-start(bf16[256,1152]{1,0:T(8,128)(2,1)S(1)} %collective-permute-done.4.refs_1_), channel_id=1, source_target_pairs={{0,96},{1,97},{2,98},{3,99},{4,36},{5,37},{6,38},{7,39},{8,104},{9... | collective-permute-start | bytes 1769480 | tf_op jit(solution)/shard_map/ppermute | solution.py:263
  32.4 9.9 %collective-permute-start.9 = (bf16[256,1152]{1,0:T(8,128)(2,1)S(1)}, bf16[256,1152]{1,0:T(8,128)(2,1)S(1)}, u32[]{:S(2)}, u32[]{:S(2)}) collective-permute-start(bf16[256,1152]{1,0:T(8,128)(2,1)S(1)} %collective-permute-done.5.refs_2_), channel_id=1, source_target_pairs={{0,8},{1,9},{2,10},{3,11},{4,28},{5,29},{6,30},{7,31},{8,0},{9,1},... | collective-permute-start | bytes 1769480 | tf_op jit(solution)/shard_map/ppermute | solution.py:263
  38.7 8.8 %collective-permute-start.6 = (bf16[160,1152]{1,0:T(8,128)(2,1)S(1)}, bf16[160,1152]{1,0:T(8,128)(2,1)S(1)}, u32[]{:S(2)}, u32[]{:S(2)}) collective-permute-start(bf16[160,1152]{1,0:T(8,128)(2,1)S(1)} %slice.6), channel_id=1, source_target_pairs={{0,96},{1,97},{2,98},{3,99},{4,36},{5,37},{6,38},{7,39},{8,104},{9... | collective-permute-start | bytes 1105928 | tf_op jit(solution)/shard_map/ppermute | solution.py:263
  41.4 6.0 %collective-permute-start.8 = (bf16[96,1152]{1,0:T(8,128)(2,1)S(1)}, bf16[96,1152]{1,0:T(8,128)(2,1)S(1)}, u32[]{:S(2)}, u32[]{:S(2)}) collective-permute-start(bf16[96,1152]{1,0:T(8,128)(2,1)S(1)} %slice.8), channel_id=1, source_target_pairs={{0,8},{1,9},{2,10},{3,11},{4,28},{5,29},{6,30},{7,31},{8,0},{9,1},... | collective-permute-start | bytes 663560 | tf_op jit(solution)/shard_map/ppermute | solution.py:263

commit v6 on v5

--- a/solution.py
+++ b/solution.py
@@ -129,7 +129,7 @@
         out_ref[copy, :, D:] = table
 
 
-def wanted_kernel(probes_ref, slot_ref, pick_ref, group_ref):
+def find_wanted(probes_ref, slot_ref, pick_ref, group_ref):
     place = place_matrix(slot_ref)
     rank = rank_table(probes_ref, place)
     index = lax.broadcasted_iota(jnp.int32, (128, 32), 0)
@@ -182,8 +182,7 @@
     return exchange([scores[8 * i : 8 * i + 8] for i in range(TOPK)], SORT_PAIRS)
 
 
-def score_kernel(*refs):
-    groups, (lists, norms, out, chosen, best) = refs[:-5], refs[-5:]
+def score_groups(groups, lists, norms, out, chosen, best):
     if len(groups) < 4:
         chosen[:, 32 * len(groups) :, :] = jnp.zeros((8, 128 - 32 * len(groups), D), BF16)
     for g, ref in enumerate(groups):
@@ -198,6 +197,16 @@
         best[8 * i : 8 * i + 8, :] = value
     for half in range(2):
         out[half] = jnp.concatenate([best[pl.ds(4 * half + t, TOPK, stride=8), :] for t in range(4)], 0).T
+
+
+def first_kernel(*refs):
+    score_groups(refs[:4], *refs[4:])
+
+
+def second_kernel(*refs):
+    groups, (lists, norms, probes, slots, out, pick, group, chosen, best) = refs[:3], refs[3:]
+    score_groups(groups, lists, norms, out, chosen, best)
+    find_wanted(probes, slots, pick, group)
 
 
 def last_kernel(lower, upper, lists, norms, first, second, out, best):
@@ -268,15 +277,11 @@
     slots = list_slot.reshape(1, 128)
     probes = probes.T
     wide = pl.pallas_call(
-        widen_kernel, out_shape=shape((8, 32, WIDE), BF16), in_specs=spaces("vvv"), out_specs=spaces("v")[0], name="widen"
+        widen_kernel, out_shape=pltpu.VMEM((8, 32, WIDE), BF16), in_specs=spaces("vvv"), out_specs=spaces("v")[0], name="widen"
     )(queries, probes, slots)
     near = lax.all_to_all(wide, AXES, 0, 0, axis_index_groups=NEAR_GROUPS, tiled=True).reshape(256, WIDE)
     sibling = lax.ppermute(database, AXES, CORE_SWAP)
-    pick, group = pl.pallas_call(
-        wanted_kernel, out_shape=(pltpu.VMEM((128, 256), BF16), pltpu.VMEM((8, 256), jnp.int32)), in_specs=spaces("vv"),
-        out_specs=spaces("vv"), name="wanted",
-    )(probes, slots)
-    near, valid_rows, pick, group = lax.optimization_barrier((near, valid_rows, pick, group))
+    near, valid_rows = lax.optimization_barrier((near, valid_rows))
     sibling_valid = lax.ppermute(valid_rows, AXES, CORE_SWAP)
 
     groups = {0: near}
@@ -290,16 +295,18 @@
     for mask, source, step in ((3, 1, 2), (6, 2, 4), (5, 4, 1)):
         groups[mask] = hop(groups[source], step)
 
-    def scored(masks, name):
+    def scored(kernel, masks, more, out_shape, name):
         return pl.pallas_call(
-            score_kernel, out_shape=shape((2, 128, 128), F32), in_specs=spaces("v" * (len(masks) + 2)), out_specs=spaces("v")[0],
+            kernel, out_shape=out_shape, in_specs=spaces("v" * (len(masks) + 2 + len(more))), out_specs=spaces("v" * len(out_shape)),
             scratch_shapes=[pltpu.VMEM((8, 128, D), BF16), pltpu.VMEM((256, 128), F32)], compiler_params=params(), name=name,
-        )(*[groups[mask] for mask in masks], lists, norms)
-
-    first = scored(FIRST_HALF, "score_first")
+        )(*[groups[mask] for mask in masks], lists, norms, *more)
+
+    best_shape = pltpu.VMEM((2, 128, 128), F32)
+    first, = scored(first_kernel, FIRST_HALF, (), (best_shape,), "score_first")
     groups[5], first = lax.optimization_barrier((groups[5], first))
     last = [hop(groups[5][:SPLIT], 2), hop(groups[3][SPLIT:], 4)]
-    second = scored(SECOND_HALF, "score_second")
+    wanted_shapes = (pltpu.VMEM((128, 256), BF16), pltpu.VMEM((8, 256), jnp.int32))
+    second, pick, group = scored(second_kernel, SECOND_HALF, (probes, slots), (best_shape, *wanted_shapes), "score_second")
     *last, second = lax.optimization_barrier((*last, second))
     blocks = pl.pallas_call(
         last_kernel, out_shape=shape((N_CORE, 8, 128), F32), in_specs=spaces("vvvvvv"), out_specs=spaces("v")[0],

time: 68.5 us -> 67.4 us (0.984)
  blocking collectives: 17.4 us -> 32.8 us
  waiting for transfers between devices: 15 us -> 6.79 us
  starting transfers between devices: 20.2 us -> 13.7 us
  Pallas kernels: 14.8 us -> 13.1 us
    all_to_all x0 -> x1, blocking collectives: none -> 16.1 us  [per_device(): lax.all_to_all(wide, AXES, 0, 0, axis_index_groups=NEAR_GROUPS, tiled=True)]
    all_to_all x1 -> x0, waiting for transfers between devices: 7.9 us -> none  [per_device(): lax.all_to_all(wide, AXES, 0, 0, axis_index_groups=NEAR_GROUPS, tiled=True)]
    all_to_all x1 -> x0, starting transfers between devices: 6.48 us -> none  [per_device(): lax.all_to_all(wide, AXES, 0, 0, axis_index_groups=NEAR_GROUPS, tiled=True)]
    pallas_call x4 -> x3, Pallas kernels: 9.2 us -> 7.48 us  [the longest x2 6.26 us: scored(): pl.pallas_call(kernel, out_shape=out_shape, in_specs=spaces('v' * (len(ma...]
    all_to_all x1, blocking collectives: 17.4 us -> 16.7 us  [per_device(): lax.all_to_all(blocks, AXES, 0, 0, axis_index_groups=CORE_GROUPS, tiled=T...]
  transfers between devices with their start and end apart: 11 -> 10, of which waited for: 8 -> 7; matrix products, arithmetic and copies ran while one was open for 0% -> 0% of each run, Pallas kernels for 17% -> 15%
where the time goes in v6:
time: 67.4 us; the launch traced here: 67.2 us
  blocking collectives  32.8 us (49%)
  starting transfers between devices  13.7 us (20%)
  Pallas kernels  13.1 us (19%)
  waiting for transfers between devices  6.79 us (10%)
  local copies, waits for them, and re-layouts  0.71 us (1%)
    all_to_all x1, blocking collectives, per_device(): lax.all_to_all(blocks, AXES, 0, 0, axis_index_groups=CORE_GROUPS, tiled=T...  16.7 us
    all_to_all x1, blocking collectives, per_device(): lax.all_to_all(wide, AXES, 0, 0, axis_index_groups=NEAR_GROUPS, tiled=True)  16.1 us
    ppermute x8, starting transfers between devices, hop(): lax.ppermute(value, AXES, [(device, far(device, mask, False)) for device...  13.7 us
    pallas_call x2, Pallas kernels, scored(): pl.pallas_call(kernel, out_shape=out_shape, in_specs=spaces('v' * (len(ma...  6.26 us
    ppermute x8, waiting for transfers between devices, hop(): lax.ppermute(value, AXES, [(device, far(device, mask, False)) for device...  5.54 us
    pallas_call x1, Pallas kernels, per_device(): pl.pallas_call(lists_kernel, out_shape=(pltpu.VMEM((8, 256, D), BF16), pl...  2.35 us
    pallas_call x1, Pallas kernels, per_device(): pl.pallas_call(last_kernel, out_shape=shape((N_CORE, 8, 128), F32), in_sp...  1.85 us
    pallas_call x1, Pallas kernels, per_device(): pl.pallas_call(final_kernel, out_shape=shape((32, TOPK), F32), in_specs=s...  1.41 us
  transfers between devices with their start and end apart: 10, of which 7 were waited for; matrix products, arithmetic and copies ran while one was open for 0% of the time, Pallas kernels for 15%

profile of v6, /device:TPU:0, one launch (start us, length us, event | category | flops | bytes accessed | tf_op | source)
XLA Modules:
  0.0 67.2 jit_solution(17775655994927921822)
XLA Ops:
  0.0 0.0 collective-permute-start.1
  0.0 1.2 %widen.1 = bf16[8,32,1152]{2,1,0:T(8,128)(2,1)S(1)} custom-call(bf16[32,1024]{1,0:T(8,128)(2,1)} %queries_ref.1, s32[8,32]{1,0:T(8,128)} %bitcast.11, s32[1,128]{1,0:T(1,128)} %bitcast.13), custom_call_target="tpu_custom_call" | custom-call | tf_op jit(solution)/shard_map/widen/pallas_call | solution.py:279
  1.2 16.1 %all_to_all.10 = bf16[8,32,1152]{2,1,0:T(8,128)(2,1)S(1)} all-to-all(bf16[8,32,1152]{2,1,0:T(8,128)(2,1)S(1)} %widen.1), channel_id=1, replica_groups={{0,1,32,33,24,25,56,57},{3,2,35,34,27,26,59,58},{96,97,64,65,120,121,88..., dimensions={0} | all-to-all | bytes 1179648 | tf_op jit(solution)/shard_map/all_to_all | solution.py:282
  17.4 0.0 collective-permute-start
  17.4 2.7 %collective-permute-start.4 = (bf16[256,1152]{1,0:T(8,128)(2,1)S(1)}, bf16[256,1152]{1,0:T(8,128)(2,1)S(1)}, u32[]{:S(2)}, u32[]{:S(2)}) collective-permute-start(bf16[256,1152]{1,0:T(8,128)(2,1)S(1)} %bitcast.7), channel_id=1, source_target_pairs={{0,3},{1,2},{2,1},{3,0},{4,5},{5,4},{6,7},{7,6},{8,11},{9,10},{10,... | collective-permute-start | bytes 1769480 | tf_op jit(solution)/shard_map/ppermute | solution.py:272
  20.1 2.2 %collective-permute-start.5 = (bf16[256,1152]{1,0:T(8,128)(2,1)S(1)}, bf16[256,1152]{1,0:T(8,128)(2,1)S(1)}, u32[]{:S(2)}, u32[]{:S(2)}) collective-permute-start(bf16[256,1152]{1,0:T(8,128)(2,1)S(1)} %bitcast.8), channel_id=1, source_target_pairs={{0,96},{1,97},{2,98},{3,99},{4,36},{5,37},{6,38},{7,39},{8,104},{9... | collective-permute-start | bytes 1769480 | tf_op jit(solution)/shard_map/ppermute | solution.py:272
  22.2 0.0 collective-permute-start.2
  22.2 1.3 %collective-permute-done.2 = s32[4]{0:T(128)S(1)} collective-permute-done((s32[4]{0:T(128)}, s32[4]{0:T(128)S(1)}, u32[]{:S(2)}, u32[]{:S(2)}) %collective-permute-start.2) | collective-permute-done | bytes 48 | tf_op jit(solution)/shard_map/ppermute | solution.py:285
  23.5 0.0 collective-permute-done.1.sibling
  23.5 0.0 copy-start.2
  23.5 0.7 copy-done.2
  24.2 2.3 %lists.1 = (bf16[8,256,1024]{2,1,0:T(8,128)(2,1)S(1)}, f32[256,128]{1,0:T(8,128)S(1)}) custom-call(bf16[4,256,1024]{2,1,0:T(8,128)(2,1)} %own.1, bf16[4,256,1024]{2,1,0:T(8,128)(2,1)S(1)} %collective-permute-done.1.sibling, s32[1,4]{1,0:T(1,128)S(1)} %bitcast.15, s32[1,4]{1,0:T(1,128)S(1)} %bitcast.16), custom_call_target="tpu_custom_call" | custom-call | tf_op jit(solution)/shard_map/lists/pallas_call | solution.py:290
  26.5 0.7 %collective-permute-done.refs_3_ = bf16[256,1152]{1,0:T(8,128)(2,1)S(1)} collective-permute-done((bf16[256,1152]{1,0:T(8,128)(2,1)S(1)}, bf16[256,1152]{1,0:T(8,128)(2,1)S(1)}, u32[]{:S(2)}, u32[]{:S(2)}) %collective-permute-start) | collective-permute-done | bytes 589856 | tf_op jit(solution)/shard_map/ppermute | solution.py:272
  27.3 2.7 %collective-permute-start.3 = (bf16[256,1152]{1,0:T(8,128)(2,1)S(1)}, bf16[256,1152]{1,0:T(8,128)(2,1)S(1)}, u32[]{:S(2)}, u32[]{:S(2)}) collective-permute-start(bf16[256,1152]{1,0:T(8,128)(2,1)S(1)} %collective-permute-done.refs_3_), channel_id=1, source_target_pairs={{0,3},{1,2},{2,1},{3,0},{4,5},{5,4},{6,7},{7,6},{8,11},{9,10},{10,... | collective-permute-start | bytes 1769480 | tf_op jit(solution)/shard_map/ppermute | solution.py:272
  29.9 0.0 collective-permute-done.4.refs_1_
  29.9 2.2 %collective-permute-start.7 = (bf16[256,1152]{1,0:T(8,128)(2,1)S(1)}, bf16[256,1152]{1,0:T(8,128)(2,1)S(1)}, u32[]{:S(2)}, u32[]{:S(2)}) collective-permute-start(bf16[256,1152]{1,0:T(8,128)(2,1)S(1)} %collective-permute-done.4.refs_1_), channel_id=1, source_target_pairs={{0,96},{1,97},{2,98},{3,99},{4,36},{5,37},{6,38},{7,39},{8,104},{9... | collective-permute-start | bytes 1769480 | tf_op jit(solution)/shard_map/ppermute | solution.py:272
  32.1 0.0 collective-permute-done.5.refs_2_
  32.1 1.0 %collective-permute-start.9 = (bf16[256,1152]{1,0:T(8,128)(2,1)S(1)}, bf16[256,1152]{1,0:T(8,128)(2,1)S(1)}, u32[]{:S(2)}, u32[]{:S(2)}) collective-permute-start(bf16[256,1152]{1,0:T(8,128)(2,1)S(1)} %collective-permute-done.5.refs_2_), channel_id=1, source_target_pairs={{0,8},{1,9},{2,10},{3,11},{4,28},{5,29},{6,30},{7,31},{8,0},{9,1},... | collective-permute-start | bytes 1769480 | tf_op jit(solution)/shard_map/ppermute | solution.py:272
  33.2 3.1 %score_first.1.first = f32[2,128,128]{2,1,0:T(8,128)S(1)} custom-call(bf16[256,1152]{1,0:T(8,128)(2,1)S(1)} %bitcast.9, bf16[256,1152]{1,0:T(8,128)(2,1)S(1)} %collective-permute-done.4.refs_1_, bf16[256,1152]{1,0:T(8,128)(2,1)S(1)} %collective-permute-done.5.refs_2_, bf16[256,1152]{1,0:T(8,128)(2,1)S(1)} %collective-permute-done.refs_3_, ...), custom_call_target="tpu_custom_call" | custom-call | tf_op jit(solution)/shard_map/score_first/pallas_call | solution.py:299
  36.3 2.1 %collective-permute-done.3.refs_0_ = bf16[256,1152]{1,0:T(8,128)(2,1)S(1)} collective-permute-done((bf16[256,1152]{1,0:T(8,128)(2,1)S(1)}, bf16[256,1152]{1,0:T(8,128)(2,1)S(1)}, u32[]{:S(2)}, u32[]{:S(2)}) %collective-permute-start.3) | collective-permute-done | bytes 589856 | tf_op jit(solution)/shard_map/ppermute | solution.py:272
  38.4 2.3 %collective-permute-start.6 = (bf16[160,1152]{1,0:T(8,128)(2,1)S(1)}, bf16[160,1152]{1,0:T(8,128)(2,1)S(1)}, u32[]{:S(2)}, u32[]{:S(2)}) collective-permute-start(bf16[160,1152]{1,0:T(8,128)(2,1)S(1)} %slice.6), channel_id=1, source_target_pairs={{0,96},{1,97},{2,98},{3,99},{4,36},{5,37},{6,38},{7,39},{8,104},{9... | collective-permute-start | bytes 1105928 | tf_op jit(solution)/shard_map/ppermute | solution.py:272
  40.6 0.4 collective-permute-done.7.refs_1_
  41.1 0.6 collective-permute-start.8
  41.7 0.3 collective-permute-done.9.refs_2_
  42.0 0.0 copy-done
  42.0 0.0 copy-done.1
  42.0 3.1 %score_second.1 = (f32[2,128,128]{2,1,0:T(8,128)S(1)}, bf16[128,256]{1,0:T(8,128)(2,1)S(1)}, s32[8,256]{1,0:T(8,128)S(1)}) custom-call(bf16[256,1152]{1,0:T(8,128)(2,1)S(1)} %collective-permute-done.3.refs_0_, bf16[256,1152]{1,0:T(8,128)(2,1)S(1)} %collective-permute-done.7.refs_1_, bf16[256,1152]{1,0:T(8,128)(2,1)S(1)} %collective-permute-done.9.refs_2_, ...), custom_call_target="tpu_custom_call" | custom-call | tf_op jit(solution)/shard_map/score_second/pallas_call | solution.py:299
  45.2 1.9 %collective-permute-done.8.upper = bf16[96,1152]{1,0:T(8,128)(2,1)S(1)} collective-permute-done((bf16[96,1152]{1,0:T(8,128)(2,1)S(1)}, bf16[96,1152]{1,0:T(8,128)(2,1)S(1)}, u32[]{:S(2)}, u32[]{:S(2)}) %collective-permute-start.8) | collective-permute-done | bytes 221216 | tf_op jit(solution)/shard_map/ppermute | solution.py:272
  47.1 0.1 collective-permute-done.6.lower
  47.2 1.8 %score_last.1 = f32[64,8,128]{2,1,0:T(8,128)S(1)} custom-call(bf16[160,1152]{1,0:T(8,128)(2,1)S(1)} %collective-permute-done.6.lower, bf16[96,1152]{1,0:T(8,128)(2,1)S(1)} %collective-permute-done.8.upper, bf16[8,256,1024]{2,1,0:T(8,128)(2,1)S(1)} %get-tuple-element.25.refs_4_.refs_3_.lists, f32[256,128]{1,0:T(8,128)S(1)} %get-tuple-element.26.refs_5_.refs_4_.norms, ...), custom_call_target="tpu_custom_call" | custom-call | tf_op jit(solution)/shard_map/score_last/pallas_call | solution.py:311
  49.0 16.7 %all_to_all.11 = f32[64,8,128]{2,1,0:T(8,128)S(1)} all-to-all(f32[64,8,128]{2,1,0:T(8,128)S(1)} %score_last.1), channel_id=1, replica_groups={{0,1,32,33,24,25,56,57,3,2,35,34,27,26,59,58,96,97,64,65,120,121,88,89,..., dimensions={0} | all-to-all | bytes 524288 | tf_op jit(solution)/shard_map/all_to_all | solution.py:315
  65.8 1.4 %final.1 = f32[32,32]{1,0:T(8,128)} custom-call(f32[4,2,4,2,8,128]{5,4,3,2,1,0:T(8,128)S(1)} %bitcast.10, bf16[128,256]{1,0:T(8,128)(2,1)S(1)} %get-tuple-element.33.pick_ref, s32[8,256]{1,0:T(8,128)S(1)} %get-tuple-element.34.group_ref), custom_call_target="tpu_custom_call" | custom-call | tf_op jit(solution)/shard_map/final/pallas_call | solution.py:316
  (4 shorter events, 0.1 us)
Async XLA Ops:
  0.0 23.5 %collective-permute-start.1 = (bf16[4,256,1024]{2,1,0:T(8,128)(2,1)}, bf16[4,256,1024]{2,1,0:T(8,128)(2,1)S(1)}, u32[]{:S(2)}, u32[]{:S(2)}) collective-permute-start(bf16[4,256,1024]{2,1,0:T(8,128)(2,1)} %own.1), channel_id=1, source_target_pairs={{0,4},{1,5},{2,6},{3,7},{4,0},{5,1},{6,2},{7,3},{8,12},{9,13},{10,... | collective-permute-start | bytes 6291464 | tf_op jit(solution)/shard_map/ppermute | solution.py:283
  17.4 9.9 %collective-permute-start = (bf16[256,1152]{1,0:T(8,128)(2,1)S(1)}, bf16[256,1152]{1,0:T(8,128)(2,1)S(1)}, u32[]{:S(2)}, u32[]{:S(2)}) collective-permute-start(bf16[256,1152]{1,0:T(8,128)(2,1)S(1)} %bitcast.6), channel_id=1, source_target_pairs={{0,8},{1,9},{2,10},{3,11},{4,28},{5,29},{6,30},{7,31},{8,0},{9,1},... | collective-permute-start | bytes 1769480 | tf_op jit(solution)/shard_map/ppermute | solution.py:272
  17.4 12.6 %collective-permute-start.4 = (bf16[256,1152]{1,0:T(8,128)(2,1)S(1)}, bf16[256,1152]{1,0:T(8,128)(2,1)S(1)}, u32[]{:S(2)}, u32[]{:S(2)}) collective-permute-start(bf16[256,1152]{1,0:T(8,128)(2,1)S(1)} %bitcast.7), channel_id=1, source_target_pairs={{0,3},{1,2},{2,1},{3,0},{4,5},{5,4},{6,7},{7,6},{8,11},{9,10},{10,... | collective-permute-start | bytes 1769480 | tf_op jit(solution)/shard_map/ppermute | solution.py:272
  20.1 12.1 %collective-permute-start.5 = (bf16[256,1152]{1,0:T(8,128)(2,1)S(1)}, bf16[256,1152]{1,0:T(8,128)(2,1)S(1)}, u32[]{:S(2)}, u32[]{:S(2)}) collective-permute-start(bf16[256,1152]{1,0:T(8,128)(2,1)S(1)} %bitcast.8), channel_id=1, source_target_pairs={{0,96},{1,97},{2,98},{3,99},{4,36},{5,37},{6,38},{7,39},{8,104},{9... | collective-permute-start | bytes 1769480 | tf_op jit(solution)/shard_map/ppermute | solution.py:272
  22.2 1.3 %collective-permute-start.2 = (s32[4]{0:T(128)}, s32[4]{0:T(128)S(1)}, u32[]{:S(2)}, u32[]{:S(2)}) collective-permute-start(s32[4]{0:T(128)} %param.8), channel_id=1, source_target_pairs={{0,4},{1,5},{2,6},{3,7},{4,0},{5,1},{6,2},{7,3},{8,12},{9,13},{10,... | collective-permute-start | bytes 56 | tf_op jit(solution)/shard_map/ppermute | solution.py:285
  23.5 0.7 copy-start.2
  27.3 14.8 %copy-start = (s32[32,8]{0,1:T(8,128)S(1)}, s32[32,8]{0,1:T(8,128)}, u32[]{:S(2)}) copy-start(s32[32,8]{0,1:T(8,128)} %param.6) | copy-start | bytes 3076
  27.3 14.8 %copy-start.1 = (s32[128]{0:T(128)S(1)}, s32[128]{0:T(128)}, u32[]{:S(2)}) copy-start(s32[128]{0:T(128)} %param.7) | copy-start | bytes 1540
  27.3 11.1 %collective-permute-start.3 = (bf16[256,1152]{1,0:T(8,128)(2,1)S(1)}, bf16[256,1152]{1,0:T(8,128)(2,1)S(1)}, u32[]{:S(2)}, u32[]{:S(2)}) collective-permute-start(bf16[256,1152]{1,0:T(8,128)(2,1)S(1)} %collective-permute-done.refs_3_), channel_id=1, source_target_pairs={{0,3},{1,2},{2,1},{3,0},{4,5},{5,4},{6,7},{7,6},{8,11},{9,10},{10,... | collective-permute-start | bytes 1769480 | tf_op jit(solution)/shard_map/ppermute | solution.py:272
  29.9 11.1 %collective-permute-start.7 = (bf16[256,1152]{1,0:T(8,128)(2,1)S(1)}, bf16[256,1152]{1,0:T(8,128)(2,1)S(1)}, u32[]{:S(2)}, u32[]{:S(2)}) collective-permute-start(bf16[256,1152]{1,0:T(8,128)(2,1)S(1)} %collective-permute-done.4.refs_1_), channel_id=1, source_target_pairs={{0,96},{1,97},{2,98},{3,99},{4,36},{5,37},{6,38},{7,39},{8,104},{9... | collective-permute-start | bytes 1769480 | tf_op jit(solution)/shard_map/ppermute | solution.py:272
  32.1 9.9 %collective-permute-start.9 = (bf16[256,1152]{1,0:T(8,128)(2,1)S(1)}, bf16[256,1152]{1,0:T(8,128)(2,1)S(1)}, u32[]{:S(2)}, u32[]{:S(2)}) collective-permute-start(bf16[256,1152]{1,0:T(8,128)(2,1)S(1)} %collective-permute-done.5.refs_2_), channel_id=1, source_target_pairs={{0,8},{1,9},{2,10},{3,11},{4,28},{5,29},{6,30},{7,31},{8,0},{9,1},... | collective-permute-start | bytes 1769480 | tf_op jit(solution)/shard_map/ppermute | solution.py:272
  38.4 8.8 %collective-permute-start.6 = (bf16[160,1152]{1,0:T(8,128)(2,1)S(1)}, bf16[160,1152]{1,0:T(8,128)(2,1)S(1)}, u32[]{:S(2)}, u32[]{:S(2)}) collective-permute-start(bf16[160,1152]{1,0:T(8,128)(2,1)S(1)} %slice.6), channel_id=1, source_target_pairs={{0,96},{1,97},{2,98},{3,99},{4,36},{5,37},{6,38},{7,39},{8,104},{9... | collective-permute-start | bytes 1105928 | tf_op jit(solution)/shard_map/ppermute | solution.py:272
  41.1 6.0 %collective-permute-start.8 = (bf16[96,1152]{1,0:T(8,128)(2,1)S(1)}, bf16[96,1152]{1,0:T(8,128)(2,1)S(1)}, u32[]{:S(2)}, u32[]{:S(2)}) collective-permute-start(bf16[96,1152]{1,0:T(8,128)(2,1)S(1)} %slice.8), channel_id=1, source_target_pairs={{0,8},{1,9},{2,10},{3,11},{4,28},{5,29},{6,30},{7,31},{8,0},{9,1},... | collective-permute-start | bytes 663560 | tf_op jit(solution)/shard_map/ppermute | solution.py:272

commit v7 on v6

--- a/solution.py
+++ b/solution.py
@@ -236,7 +236,7 @@
                 out[place + b, 4 * half : 4 * half + 4, :] = values[4 * b : 4 * b + 4]
 
 
-def final_kernel(back_ref, pick_ref, group_ref, out_ref, tiles, rows):
+def final_kernel(back_ref, pick_ref, group_ref, out_ref, tiles):
     pick = pick_ref[...]
     group = jnp.concatenate([group_ref[...]] * 4, 0)
     for z in range(4):
@@ -254,9 +254,14 @@
     values = [tiles[8 * i : 8 * i + 8, :] for i in range(TOPK)]
     for axis, shift in ((0, 4), (0, 2), (0, 1), (1, 64), (1, 32)):
         values = merged(values, [pltpu.roll(value, shift, axis) for value in values])
-    for i, value in enumerate(values):
-        rows[i : i + 1, :] = value[:1]
-    out_ref[...] = rows[...].T[:32]
+    row = lax.broadcasted_iota(jnp.int32, (8, 128), 0)
+    ranked = []
+    for first in range(0, TOPK, 8):
+        rows = values[first]
+        for i in range(1, 8):
+            rows = jnp.where(row == i, values[first + i], rows)
+        ranked.append(rows)
+    out_ref[...] = jnp.concatenate(ranked, 0).T[:32]
 
 
 def params():
@@ -298,7 +303,7 @@
     def scored(kernel, masks, more, out_shape, name):
         return pl.pallas_call(
             kernel, out_shape=out_shape, in_specs=spaces("v" * (len(masks) + 2 + len(more))), out_specs=spaces("v" * len(out_shape)),
-            scratch_shapes=[pltpu.VMEM((8, 128, D), BF16), pltpu.VMEM((256, 128), F32)], compiler_params=params(), name=name,
+            scratch_shapes=[pltpu.VMEM((8, 128, D), BF16), pltpu.VMEM((264, 128), F32)], compiler_params=params(), name=name,
         )(*[groups[mask] for mask in masks], lists, norms, *more)
 
     best_shape = pltpu.VMEM((2, 128, 128), F32)
@@ -310,12 +315,12 @@
     *last, second = lax.optimization_barrier((*last, second))
     blocks = pl.pallas_call(
         last_kernel, out_shape=shape((N_CORE, 8, 128), F32), in_specs=spaces("vvvvvv"), out_specs=spaces("v")[0],
-        scratch_shapes=[pltpu.VMEM((256, 128), F32)], compiler_params=params(), name="score_last",
+        scratch_shapes=[pltpu.VMEM((264, 128), F32)], compiler_params=params(), name="score_last",
     )(*last, lists, norms, first, second)
     back = lax.all_to_all(blocks, AXES, 0, 0, axis_index_groups=CORE_GROUPS, tiled=True)
     return pl.pallas_call(
         final_kernel, out_shape=shape((32, TOPK), F32), in_specs=spaces("vvv"), out_specs=spaces("v")[0],
-        scratch_shapes=[pltpu.VMEM((256, 128), F32), pltpu.VMEM((32, 128), F32)], compiler_params=params(), name="final",
+        scratch_shapes=[pltpu.VMEM((264, 128), F32)], compiler_params=params(), name="final",
     )(back.reshape(4, 2, 4, 2, 8, 128), pick, group)
 
 

time: 67.4 us -> 67.4 us (level)
  no operation moved by 1% of the time
where the time goes in v7:
time: 67.4 us; the launch traced here: 67.2 us
  blocking collectives  32.8 us (49%)
  starting transfers between devices  13.7 us (20%)
  Pallas kernels  13.1 us (19%)
  waiting for transfers between devices  6.82 us (10%)
  local copies, waits for them, and re-layouts  0.71 us (1%)
    all_to_all x1, blocking collectives, per_device(): lax.all_to_all(blocks, AXES, 0, 0, axis_index_groups=CORE_GROUPS, tiled=T...  16.7 us
    all_to_all x1, blocking collectives, per_device(): lax.all_to_all(wide, AXES, 0, 0, axis_index_groups=NEAR_GROUPS, tiled=True)  16.1 us
    ppermute x8, starting transfers between devices, hop(): lax.ppermute(value, AXES, [(device, far(device, mask, False)) for device...  13.7 us
    pallas_call x2, Pallas kernels, scored(): pl.pallas_call(kernel, out_shape=out_shape, in_specs=spaces('v' * (len(ma...  6.24 us
    ppermute x8, waiting for transfers between devices, hop(): lax.ppermute(value, AXES, [(device, far(device, mask, False)) for device...  5.56 us
    pallas_call x1, Pallas kernels, per_device(): pl.pallas_call(lists_kernel, out_shape=(pltpu.VMEM((8, 256, D), BF16), pl...  2.35 us
    pallas_call x1, Pallas kernels, per_device(): pl.pallas_call(last_kernel, out_shape=shape((N_CORE, 8, 128), F32), in_sp...  1.85 us
    pallas_call x1, Pallas kernels, per_device(): pl.pallas_call(final_kernel, out_shape=shape((32, TOPK), F32), in_specs=s...  1.41 us
  transfers between devices with their start and end apart: 10, of which 7 were waited for; matrix products, arithmetic and copies ran while one was open for 0% of the time, Pallas kernels for 15%

profile of v7, /device:TPU:0, one launch (start us, length us, event | category | flops | bytes accessed | tf_op | source)
XLA Modules:
  0.0 67.2 jit_solution(3496207087279863772)
XLA Ops:
  0.0 0.0 collective-permute-start.1
  0.0 1.2 %widen.1 = bf16[8,32,1152]{2,1,0:T(8,128)(2,1)S(1)} custom-call(bf16[32,1024]{1,0:T(8,128)(2,1)} %queries_ref.1, s32[8,32]{1,0:T(8,128)} %bitcast.11, s32[1,128]{1,0:T(1,128)} %bitcast.13), custom_call_target="tpu_custom_call" | custom-call | tf_op jit(solution)/shard_map/widen/pallas_call | solution.py:284
  1.2 16.1 %all_to_all.10 = bf16[8,32,1152]{2,1,0:T(8,128)(2,1)S(1)} all-to-all(bf16[8,32,1152]{2,1,0:T(8,128)(2,1)S(1)} %widen.1), channel_id=1, replica_groups={{0,1,32,33,24,25,56,57},{3,2,35,34,27,26,59,58},{96,97,64,65,120,121,88..., dimensions={0} | all-to-all | bytes 1179648 | tf_op jit(solution)/shard_map/all_to_all | solution.py:287
  17.4 0.0 collective-permute-start
  17.4 2.7 %collective-permute-start.4 = (bf16[256,1152]{1,0:T(8,128)(2,1)S(1)}, bf16[256,1152]{1,0:T(8,128)(2,1)S(1)}, u32[]{:S(2)}, u32[]{:S(2)}) collective-permute-start(bf16[256,1152]{1,0:T(8,128)(2,1)S(1)} %bitcast.7), channel_id=1, source_target_pairs={{0,3},{1,2},{2,1},{3,0},{4,5},{5,4},{6,7},{7,6},{8,11},{9,10},{10,... | collective-permute-start | bytes 1769480 | tf_op jit(solution)/shard_map/ppermute | solution.py:277
  20.1 2.2 %collective-permute-start.5 = (bf16[256,1152]{1,0:T(8,128)(2,1)S(1)}, bf16[256,1152]{1,0:T(8,128)(2,1)S(1)}, u32[]{:S(2)}, u32[]{:S(2)}) collective-permute-start(bf16[256,1152]{1,0:T(8,128)(2,1)S(1)} %bitcast.8), channel_id=1, source_target_pairs={{0,96},{1,97},{2,98},{3,99},{4,36},{5,37},{6,38},{7,39},{8,104},{9... | collective-permute-start | bytes 1769480 | tf_op jit(solution)/shard_map/ppermute | solution.py:277
  22.2 0.0 collective-permute-start.2
  22.2 1.3 %collective-permute-done.2 = s32[4]{0:T(128)S(1)} collective-permute-done((s32[4]{0:T(128)}, s32[4]{0:T(128)S(1)}, u32[]{:S(2)}, u32[]{:S(2)}) %collective-permute-start.2) | collective-permute-done | bytes 48 | tf_op jit(solution)/shard_map/ppermute | solution.py:290
  23.5 0.0 collective-permute-done.1.sibling
  23.5 0.0 copy-start.2
  23.5 0.7 copy-done.2
  24.2 2.3 %lists.1 = (bf16[8,256,1024]{2,1,0:T(8,128)(2,1)S(1)}, f32[256,128]{1,0:T(8,128)S(1)}) custom-call(bf16[4,256,1024]{2,1,0:T(8,128)(2,1)} %own.1, bf16[4,256,1024]{2,1,0:T(8,128)(2,1)S(1)} %collective-permute-done.1.sibling, s32[1,4]{1,0:T(1,128)S(1)} %bitcast.15, s32[1,4]{1,0:T(1,128)S(1)} %bitcast.16), custom_call_target="tpu_custom_call" | custom-call | tf_op jit(solution)/shard_map/lists/pallas_call | solution.py:295
  26.5 0.7 %collective-permute-done.refs_3_ = bf16[256,1152]{1,0:T(8,128)(2,1)S(1)} collective-permute-done((bf16[256,1152]{1,0:T(8,128)(2,1)S(1)}, bf16[256,1152]{1,0:T(8,128)(2,1)S(1)}, u32[]{:S(2)}, u32[]{:S(2)}) %collective-permute-start) | collective-permute-done | bytes 589856 | tf_op jit(solution)/shard_map/ppermute | solution.py:277
  27.3 2.7 %collective-permute-start.3 = (bf16[256,1152]{1,0:T(8,128)(2,1)S(1)}, bf16[256,1152]{1,0:T(8,128)(2,1)S(1)}, u32[]{:S(2)}, u32[]{:S(2)}) collective-permute-start(bf16[256,1152]{1,0:T(8,128)(2,1)S(1)} %collective-permute-done.refs_3_), channel_id=1, source_target_pairs={{0,3},{1,2},{2,1},{3,0},{4,5},{5,4},{6,7},{7,6},{8,11},{9,10},{10,... | collective-permute-start | bytes 1769480 | tf_op jit(solution)/shard_map/ppermute | solution.py:277
  29.9 0.0 collective-permute-done.4.refs_1_
  29.9 2.2 %collective-permute-start.7 = (bf16[256,1152]{1,0:T(8,128)(2,1)S(1)}, bf16[256,1152]{1,0:T(8,128)(2,1)S(1)}, u32[]{:S(2)}, u32[]{:S(2)}) collective-permute-start(bf16[256,1152]{1,0:T(8,128)(2,1)S(1)} %collective-permute-done.4.refs_1_), channel_id=1, source_target_pairs={{0,96},{1,97},{2,98},{3,99},{4,36},{5,37},{6,38},{7,39},{8,104},{9... | collective-permute-start | bytes 1769480 | tf_op jit(solution)/shard_map/ppermute | solution.py:277
  32.1 0.0 collective-permute-done.5.refs_2_
  32.1 1.0 %collective-permute-start.9 = (bf16[256,1152]{1,0:T(8,128)(2,1)S(1)}, bf16[256,1152]{1,0:T(8,128)(2,1)S(1)}, u32[]{:S(2)}, u32[]{:S(2)}) collective-permute-start(bf16[256,1152]{1,0:T(8,128)(2,1)S(1)} %collective-permute-done.5.refs_2_), channel_id=1, source_target_pairs={{0,8},{1,9},{2,10},{3,11},{4,28},{5,29},{6,30},{7,31},{8,0},{9,1},... | collective-permute-start | bytes 1769480 | tf_op jit(solution)/shard_map/ppermute | solution.py:277
  33.2 3.1 %score_first.1.first = f32[2,128,128]{2,1,0:T(8,128)S(1)} custom-call(bf16[256,1152]{1,0:T(8,128)(2,1)S(1)} %bitcast.9, bf16[256,1152]{1,0:T(8,128)(2,1)S(1)} %collective-permute-done.4.refs_1_, bf16[256,1152]{1,0:T(8,128)(2,1)S(1)} %collective-permute-done.5.refs_2_, bf16[256,1152]{1,0:T(8,128)(2,1)S(1)} %collective-permute-done.refs_3_, ...), custom_call_target="tpu_custom_call" | custom-call | tf_op jit(solution)/shard_map/score_first/pallas_call | solution.py:304
  36.3 2.0 %collective-permute-done.3.refs_0_ = bf16[256,1152]{1,0:T(8,128)(2,1)S(1)} collective-permute-done((bf16[256,1152]{1,0:T(8,128)(2,1)S(1)}, bf16[256,1152]{1,0:T(8,128)(2,1)S(1)}, u32[]{:S(2)}, u32[]{:S(2)}) %collective-permute-start.3) | collective-permute-done | bytes 589856 | tf_op jit(solution)/shard_map/ppermute | solution.py:277
  38.4 2.3 %collective-permute-start.6 = (bf16[160,1152]{1,0:T(8,128)(2,1)S(1)}, bf16[160,1152]{1,0:T(8,128)(2,1)S(1)}, u32[]{:S(2)}, u32[]{:S(2)}) collective-permute-start(bf16[160,1152]{1,0:T(8,128)(2,1)S(1)} %slice.6), channel_id=1, source_target_pairs={{0,96},{1,97},{2,98},{3,99},{4,36},{5,37},{6,38},{7,39},{8,104},{9... | collective-permute-start | bytes 1105928 | tf_op jit(solution)/shard_map/ppermute | solution.py:277
  40.6 0.4 collective-permute-done.7.refs_1_
  41.1 0.6 collective-permute-start.8
  41.7 0.3 collective-permute-done.9.refs_2_
  42.0 0.0 copy-done
  42.0 0.0 copy-done.1
  42.0 3.1 %score_second.1 = (f32[2,128,128]{2,1,0:T(8,128)S(1)}, bf16[128,256]{1,0:T(8,128)(2,1)S(1)}, s32[8,256]{1,0:T(8,128)S(1)}) custom-call(bf16[256,1152]{1,0:T(8,128)(2,1)S(1)} %collective-permute-done.3.refs_0_, bf16[256,1152]{1,0:T(8,128)(2,1)S(1)} %collective-permute-done.7.refs_1_, bf16[256,1152]{1,0:T(8,128)(2,1)S(1)} %collective-permute-done.9.refs_2_, ...), custom_call_target="tpu_custom_call" | custom-call | tf_op jit(solution)/shard_map/score_second/pallas_call | solution.py:304
  45.1 1.9 %collective-permute-done.8.upper = bf16[96,1152]{1,0:T(8,128)(2,1)S(1)} collective-permute-done((bf16[96,1152]{1,0:T(8,128)(2,1)S(1)}, bf16[96,1152]{1,0:T(8,128)(2,1)S(1)}, u32[]{:S(2)}, u32[]{:S(2)}) %collective-permute-start.8) | collective-permute-done | bytes 221216 | tf_op jit(solution)/shard_map/ppermute | solution.py:277
  47.1 0.1 collective-permute-done.6.lower
  47.2 1.9 %score_last.1 = f32[64,8,128]{2,1,0:T(8,128)S(1)} custom-call(bf16[160,1152]{1,0:T(8,128)(2,1)S(1)} %collective-permute-done.6.lower, bf16[96,1152]{1,0:T(8,128)(2,1)S(1)} %collective-permute-done.8.upper, bf16[8,256,1024]{2,1,0:T(8,128)(2,1)S(1)} %get-tuple-element.25.refs_4_.refs_3_.lists, f32[256,128]{1,0:T(8,128)S(1)} %get-tuple-element.26.refs_5_.refs_4_.norms, ...), custom_call_target="tpu_custom_call" | custom-call | tf_op jit(solution)/shard_map/score_last/pallas_call | solution.py:316
  49.1 16.7 %all_to_all.11 = f32[64,8,128]{2,1,0:T(8,128)S(1)} all-to-all(f32[64,8,128]{2,1,0:T(8,128)S(1)} %score_last.1), channel_id=1, replica_groups={{0,1,32,33,24,25,56,57,3,2,35,34,27,26,59,58,96,97,64,65,120,121,88,89,..., dimensions={0} | all-to-all | bytes 524288 | tf_op jit(solution)/shard_map/all_to_all | solution.py:320
  65.8 1.4 %final.1 = f32[32,32]{1,0:T(8,128)} custom-call(f32[4,2,4,2,8,128]{5,4,3,2,1,0:T(8,128)S(1)} %bitcast.10, bf16[128,256]{1,0:T(8,128)(2,1)S(1)} %get-tuple-element.33.pick_ref, s32[8,256]{1,0:T(8,128)S(1)} %get-tuple-element.34.group_ref), custom_call_target="tpu_custom_call" | custom-call | tf_op jit(solution)/shard_map/final/pallas_call | solution.py:321
  (4 shorter events, 0.1 us)
Async XLA Ops:
  0.0 23.5 %collective-permute-start.1 = (bf16[4,256,1024]{2,1,0:T(8,128)(2,1)}, bf16[4,256,1024]{2,1,0:T(8,128)(2,1)S(1)}, u32[]{:S(2)}, u32[]{:S(2)}) collective-permute-start(bf16[4,256,1024]{2,1,0:T(8,128)(2,1)} %own.1), channel_id=1, source_target_pairs={{0,4},{1,5},{2,6},{3,7},{4,0},{5,1},{6,2},{7,3},{8,12},{9,13},{10,... | collective-permute-start | bytes 6291464 | tf_op jit(solution)/shard_map/ppermute | solution.py:288
  17.4 9.9 %collective-permute-start = (bf16[256,1152]{1,0:T(8,128)(2,1)S(1)}, bf16[256,1152]{1,0:T(8,128)(2,1)S(1)}, u32[]{:S(2)}, u32[]{:S(2)}) collective-permute-start(bf16[256,1152]{1,0:T(8,128)(2,1)S(1)} %bitcast.6), channel_id=1, source_target_pairs={{0,8},{1,9},{2,10},{3,11},{4,28},{5,29},{6,30},{7,31},{8,0},{9,1},... | collective-permute-start | bytes 1769480 | tf_op jit(solution)/shard_map/ppermute | solution.py:277
  17.4 12.6 %collective-permute-start.4 = (bf16[256,1152]{1,0:T(8,128)(2,1)S(1)}, bf16[256,1152]{1,0:T(8,128)(2,1)S(1)}, u32[]{:S(2)}, u32[]{:S(2)}) collective-permute-start(bf16[256,1152]{1,0:T(8,128)(2,1)S(1)} %bitcast.7), channel_id=1, source_target_pairs={{0,3},{1,2},{2,1},{3,0},{4,5},{5,4},{6,7},{7,6},{8,11},{9,10},{10,... | collective-permute-start | bytes 1769480 | tf_op jit(solution)/shard_map/ppermute | solution.py:277
  20.1 12.1 %collective-permute-start.5 = (bf16[256,1152]{1,0:T(8,128)(2,1)S(1)}, bf16[256,1152]{1,0:T(8,128)(2,1)S(1)}, u32[]{:S(2)}, u32[]{:S(2)}) collective-permute-start(bf16[256,1152]{1,0:T(8,128)(2,1)S(1)} %bitcast.8), channel_id=1, source_target_pairs={{0,96},{1,97},{2,98},{3,99},{4,36},{5,37},{6,38},{7,39},{8,104},{9... | collective-permute-start | bytes 1769480 | tf_op jit(solution)/shard_map/ppermute | solution.py:277
  22.2 1.3 %collective-permute-start.2 = (s32[4]{0:T(128)}, s32[4]{0:T(128)S(1)}, u32[]{:S(2)}, u32[]{:S(2)}) collective-permute-start(s32[4]{0:T(128)} %param.8), channel_id=1, source_target_pairs={{0,4},{1,5},{2,6},{3,7},{4,0},{5,1},{6,2},{7,3},{8,12},{9,13},{10,... | collective-permute-start | bytes 56 | tf_op jit(solution)/shard_map/ppermute | solution.py:290
  23.5 0.7 copy-start.2
  27.3 14.8 %copy-start = (s32[32,8]{0,1:T(8,128)S(1)}, s32[32,8]{0,1:T(8,128)}, u32[]{:S(2)}) copy-start(s32[32,8]{0,1:T(8,128)} %param.6) | copy-start | bytes 3076
  27.3 14.8 %copy-start.1 = (s32[128]{0:T(128)S(1)}, s32[128]{0:T(128)}, u32[]{:S(2)}) copy-start(s32[128]{0:T(128)} %param.7) | copy-start | bytes 1540
  27.3 11.1 %collective-permute-start.3 = (bf16[256,1152]{1,0:T(8,128)(2,1)S(1)}, bf16[256,1152]{1,0:T(8,128)(2,1)S(1)}, u32[]{:S(2)}, u32[]{:S(2)}) collective-permute-start(bf16[256,1152]{1,0:T(8,128)(2,1)S(1)} %collective-permute-done.refs_3_), channel_id=1, source_target_pairs={{0,3},{1,2},{2,1},{3,0},{4,5},{5,4},{6,7},{7,6},{8,11},{9,10},{10,... | collective-permute-start | bytes 1769480 | tf_op jit(solution)/shard_map/ppermute | solution.py:277
  29.9 11.1 %collective-permute-start.7 = (bf16[256,1152]{1,0:T(8,128)(2,1)S(1)}, bf16[256,1152]{1,0:T(8,128)(2,1)S(1)}, u32[]{:S(2)}, u32[]{:S(2)}) collective-permute-start(bf16[256,1152]{1,0:T(8,128)(2,1)S(1)} %collective-permute-done.4.refs_1_), channel_id=1, source_target_pairs={{0,96},{1,97},{2,98},{3,99},{4,36},{5,37},{6,38},{7,39},{8,104},{9... | collective-permute-start | bytes 1769480 | tf_op jit(solution)/shard_map/ppermute | solution.py:277
  32.1 9.9 %collective-permute-start.9 = (bf16[256,1152]{1,0:T(8,128)(2,1)S(1)}, bf16[256,1152]{1,0:T(8,128)(2,1)S(1)}, u32[]{:S(2)}, u32[]{:S(2)}) collective-permute-start(bf16[256,1152]{1,0:T(8,128)(2,1)S(1)} %collective-permute-done.5.refs_2_), channel_id=1, source_target_pairs={{0,8},{1,9},{2,10},{3,11},{4,28},{5,29},{6,30},{7,31},{8,0},{9,1},... | collective-permute-start | bytes 1769480 | tf_op jit(solution)/shard_map/ppermute | solution.py:277
  38.4 8.8 %collective-permute-start.6 = (bf16[160,1152]{1,0:T(8,128)(2,1)S(1)}, bf16[160,1152]{1,0:T(8,128)(2,1)S(1)}, u32[]{:S(2)}, u32[]{:S(2)}) collective-permute-start(bf16[160,1152]{1,0:T(8,128)(2,1)S(1)} %slice.6), channel_id=1, source_target_pairs={{0,96},{1,97},{2,98},{3,99},{4,36},{5,37},{6,38},{7,39},{8,104},{9... | collective-permute-start | bytes 1105928 | tf_op jit(solution)/shard_map/ppermute | solution.py:277
  41.1 6.0 %collective-permute-start.8 = (bf16[96,1152]{1,0:T(8,128)(2,1)S(1)}, bf16[96,1152]{1,0:T(8,128)(2,1)S(1)}, u32[]{:S(2)}, u32[]{:S(2)}) collective-permute-start(bf16[96,1152]{1,0:T(8,128)(2,1)S(1)} %slice.8), channel_id=1, source_target_pairs={{0,8},{1,9},{2,10},{3,11},{4,28},{5,29},{6,30},{7,31},{8,0},{9,1},... | collective-permute-start | bytes 663560 | tf_op jit(solution)/shard_map/ppermute | solution.py:277

commit v8 on v7

--- a/solution.py
+++ b/solution.py
@@ -146,15 +146,19 @@
         group_ref[:, 32 * j : 32 * j + 32] = jnp.broadcast_to(where & 3, (8, 32))
 
 
-def lists_kernel(own, sibling, own_valid, sibling_valid, lists, norms, sems):
+def lists_kernel(own, sibling, own_rows, sibling_valid, lists, norms, own_valid, sems):
     copies = []
     for t in range(8):
         copies.append(pltpu.make_async_copy(own.at[t] if t < 4 else sibling.at[t - 4], lists.at[t], sems.at[t]))
         copies[t].start()
+    valid_copy = pltpu.make_async_copy(own_rows, own_valid, sems.at[8])
+    valid_copy.start()
     row = lax.axis_index("replica") * 256 + lax.broadcasted_iota(jnp.int32, (256, 1), 0)
     lane = lax.broadcasted_iota(jnp.int32, (256, 128), 1)
     total = jnp.zeros((256, 128), F32)
     for t in (4, 5, 6, 7, 0, 1, 2, 3):
+        if t == 0:
+            valid_copy.wait()
         copies[t].wait()
         rows = lists[t].astype(F32)
         valid = (own_valid if t < 4 else sibling_valid)[0:1, t % 4 : t % 4 + 1]
@@ -214,10 +218,13 @@
     lane = lax.broadcasted_iota(jnp.int32, (256, 128), 1)
     sets = []
     for half in range(2):
+        four = lists[4 * half : 4 * half + 4].reshape(1024, D)
         queries = picked[128 * half : 128 * half + 128]
-        scores = score(lists, norms, 4 * half, queries)
+        dots = lax.dot_general(four, queries, (((1,), (1,)), ((), ())), preferred_element_type=F32)
+        scores = dots[:256] - norms[:, 4 * half : 4 * half + 1]
         for t in range(1, 4):
-            scores = jnp.where((lane >> 5) == t, score(lists, norms, 4 * half + t, queries), scores)
+            other = dots[256 * t : 256 * t + 256] - norms[:, 4 * half + t : 4 * half + t + 1]
+            scores = jnp.where((lane >> 5) == t, other, scores)
         sets.append(sort_rows(scores))
     values = merged_rows(sets[0], sets[1], 1)
     for shift in (2, 4):
@@ -239,13 +246,16 @@
 def final_kernel(back_ref, pick_ref, group_ref, out_ref, tiles):
     pick = pick_ref[...]
     group = jnp.concatenate([group_ref[...]] * 4, 0)
+    pieces = []
     for z in range(4):
         left = back_ref[:, z >> 1, :, z & 1].reshape(128, 128).T
-        found = jnp.zeros((128, 256), F32)
         for _ in range(3):
-            piece = left.astype(BF16)
-            left = left - piece.astype(F32)
-            found = found + jnp.dot(piece, pick, preferred_element_type=F32)
+            pieces.append(left.astype(BF16))
+            left = left - pieces[-1].astype(F32)
+    products = jnp.dot(jnp.concatenate(pieces, 0), pick, preferred_element_type=F32)
+    for z in range(4):
+        high, middle, low = [products[128 * i : 128 * i + 128] for i in range(3 * z, 3 * z + 3)]
+        found = high + middle + low
         scores = found[:32]
         for t in range(1, 4):
             scores = jnp.where(group == t, found[32 * t : 32 * t + 32], scores)
@@ -293,9 +303,9 @@
     for mask in (1, 2, 4):
         groups[mask] = hop(near, mask)
     lists, norms = pl.pallas_call(
-        lists_kernel, out_shape=(pltpu.VMEM((8, 256, D), BF16), pltpu.VMEM((256, 128), F32)), in_specs=spaces("havv"),
-        out_specs=spaces("vv"), scratch_shapes=[pltpu.SemaphoreType.DMA((8,))], compiler_params=params(), name="lists",
-    )(pltpu.with_memory_space_constraint(database, pltpu.HBM), sibling, valid_rows.reshape(1, 4), sibling_valid.reshape(1, 4))
+        lists_kernel, out_shape=(pltpu.VMEM((8, 256, D), BF16), pltpu.VMEM((256, 128), F32)), in_specs=spaces("hahv"),
+        out_specs=spaces("vv"), scratch_shapes=[pltpu.VMEM((1, 4), jnp.int32), pltpu.SemaphoreType.DMA((9,))], compiler_params=params(), name="lists",
+    )(pltpu.with_memory_space_constraint(database, pltpu.HBM), sibling, pltpu.with_memory_space_constraint(valid_rows.reshape(1, 4), pltpu.HBM), sibling_valid.reshape(1, 4))
     groups[4], lists, norms = lax.optimization_barrier((groups[4], lists, norms))
     for mask, source, step in ((3, 1, 2), (6, 2, 4), (5, 4, 1)):
         groups[mask] = hop(groups[source], step)

time: 67.4 us -> 67.4 us (level)
  no operation moved by 1% of the time
where the time goes in v8:
time: 67.4 us; the launch traced here: 67.2 us
  blocking collectives  32.8 us (49%)
  starting transfers between devices  13.7 us (20%)
  Pallas kernels  13.1 us (19%)
  waiting for transfers between devices  7.44 us (11%)
    all_to_all x1, blocking collectives, per_device(): lax.all_to_all(blocks, AXES, 0, 0, axis_index_groups=CORE_GROUPS, tiled=T...  16.7 us
    all_to_all x1, blocking collectives, per_device(): lax.all_to_all(wide, AXES, 0, 0, axis_index_groups=NEAR_GROUPS, tiled=True)  16.1 us
    ppermute x8, starting transfers between devices, hop(): lax.ppermute(value, AXES, [(device, far(device, mask, False)) for device...  13.7 us
    pallas_call x2, Pallas kernels, scored(): pl.pallas_call(kernel, out_shape=out_shape, in_specs=spaces('v' * (len(ma...  6.22 us
    ppermute x8, waiting for transfers between devices, hop(): lax.ppermute(value, AXES, [(device, far(device, mask, False)) for device...  6.18 us
    pallas_call x1, Pallas kernels, per_device(): pl.pallas_call(lists_kernel, out_shape=(pltpu.VMEM((8, 256, D), BF16), pl...  2.39 us
    pallas_call x1, Pallas kernels, per_device(): pl.pallas_call(last_kernel, out_shape=shape((N_CORE, 8, 128), F32), in_sp...  1.88 us
    pallas_call x1, Pallas kernels, per_device(): pl.pallas_call(final_kernel, out_shape=shape((32, TOPK), F32), in_specs=s...  1.4 us
  transfers between devices with their start and end apart: 10, of which 7 were waited for; matrix products, arithmetic and copies ran while one was open for 0% of the time, Pallas kernels for 15%

profile of v8, /device:TPU:0, one launch (start us, length us, event | category | flops | bytes accessed | tf_op | source)
XLA Modules:
  0.0 67.2 jit_solution(10432424082134213011)
XLA Ops:
  0.0 0.0 collective-permute-start.1
  0.0 1.2 %widen.1 = bf16[8,32,1152]{2,1,0:T(8,128)(2,1)S(1)} custom-call(bf16[32,1024]{1,0:T(8,128)(2,1)} %queries_ref.1, s32[8,32]{1,0:T(8,128)} %bitcast.11, s32[1,128]{1,0:T(1,128)} %bitcast.13), custom_call_target="tpu_custom_call" | custom-call | tf_op jit(solution)/shard_map/widen/pallas_call | solution.py:294
  1.2 16.1 %all_to_all.10 = bf16[8,32,1152]{2,1,0:T(8,128)(2,1)S(1)} all-to-all(bf16[8,32,1152]{2,1,0:T(8,128)(2,1)S(1)} %widen.1), channel_id=1, replica_groups={{0,1,32,33,24,25,56,57},{3,2,35,34,27,26,59,58},{96,97,64,65,120,121,88..., dimensions={0} | all-to-all | bytes 1179648 | tf_op jit(solution)/shard_map/all_to_all | solution.py:297
  17.4 0.0 collective-permute-start
  17.4 2.7 %collective-permute-start.4 = (bf16[256,1152]{1,0:T(8,128)(2,1)S(1)}, bf16[256,1152]{1,0:T(8,128)(2,1)S(1)}, u32[]{:S(2)}, u32[]{:S(2)}) collective-permute-start(bf16[256,1152]{1,0:T(8,128)(2,1)S(1)} %bitcast.7), channel_id=1, source_target_pairs={{0,3},{1,2},{2,1},{3,0},{4,5},{5,4},{6,7},{7,6},{8,11},{9,10},{10,... | collective-permute-start | bytes 1769480 | tf_op jit(solution)/shard_map/ppermute | solution.py:287
  20.1 2.2 %collective-permute-start.5 = (bf16[256,1152]{1,0:T(8,128)(2,1)S(1)}, bf16[256,1152]{1,0:T(8,128)(2,1)S(1)}, u32[]{:S(2)}, u32[]{:S(2)}) collective-permute-start(bf16[256,1152]{1,0:T(8,128)(2,1)S(1)} %bitcast.8), channel_id=1, source_target_pairs={{0,96},{1,97},{2,98},{3,99},{4,36},{5,37},{6,38},{7,39},{8,104},{9... | collective-permute-start | bytes 1769480 | tf_op jit(solution)/shard_map/ppermute | solution.py:287
  22.2 0.0 collective-permute-start.2
  22.2 1.3 %collective-permute-done.2 = s32[4]{0:T(128)S(1)} collective-permute-done((s32[4]{0:T(128)}, s32[4]{0:T(128)S(1)}, u32[]{:S(2)}, u32[]{:S(2)}) %collective-permute-start.2) | collective-permute-done | bytes 48 | tf_op jit(solution)/shard_map/ppermute | solution.py:300
  23.5 0.0 collective-permute-done.1.sibling
  23.5 2.4 %lists.1 = (bf16[8,256,1024]{2,1,0:T(8,128)(2,1)S(1)}, f32[256,128]{1,0:T(8,128)S(1)}) custom-call(bf16[4,256,1024]{2,1,0:T(8,128)(2,1)} %own.1, bf16[4,256,1024]{2,1,0:T(8,128)(2,1)S(1)} %collective-permute-done.1.sibling, s32[1,4]{1,0:T(1,128)} %bitcast.16, s32[1,4]{1,0:T(1,128)S(1)} %bitcast.15), custom_call_target="tpu_custom_call" | custom-call | tf_op jit(solution)/shard_map/lists/pallas_call | solution.py:305
  25.9 1.4 %collective-permute-done.refs_3_ = bf16[256,1152]{1,0:T(8,128)(2,1)S(1)} collective-permute-done((bf16[256,1152]{1,0:T(8,128)(2,1)S(1)}, bf16[256,1152]{1,0:T(8,128)(2,1)S(1)}, u32[]{:S(2)}, u32[]{:S(2)}) %collective-permute-start) | collective-permute-done | bytes 589856 | tf_op jit(solution)/shard_map/ppermute | solution.py:287
  27.3 0.0 copy-start
  27.3 0.0 copy-start.1
  27.3 2.7 %collective-permute-start.3 = (bf16[256,1152]{1,0:T(8,128)(2,1)S(1)}, bf16[256,1152]{1,0:T(8,128)(2,1)S(1)}, u32[]{:S(2)}, u32[]{:S(2)}) collective-permute-start(bf16[256,1152]{1,0:T(8,128)(2,1)S(1)} %collective-permute-done.refs_3_), channel_id=1, source_target_pairs={{0,3},{1,2},{2,1},{3,0},{4,5},{5,4},{6,7},{7,6},{8,11},{9,10},{10,... | collective-permute-start | bytes 1769480 | tf_op jit(solution)/shard_map/ppermute | solution.py:287
  29.9 0.0 collective-permute-done.4.refs_1_
  29.9 2.2 %collective-permute-start.7 = (bf16[256,1152]{1,0:T(8,128)(2,1)S(1)}, bf16[256,1152]{1,0:T(8,128)(2,1)S(1)}, u32[]{:S(2)}, u32[]{:S(2)}) collective-permute-start(bf16[256,1152]{1,0:T(8,128)(2,1)S(1)} %collective-permute-done.4.refs_1_), channel_id=1, source_target_pairs={{0,96},{1,97},{2,98},{3,99},{4,36},{5,37},{6,38},{7,39},{8,104},{9... | collective-permute-start | bytes 1769480 | tf_op jit(solution)/shard_map/ppermute | solution.py:287
  32.1 0.0 collective-permute-done.5.refs_2_
  32.1 1.0 %collective-permute-start.9 = (bf16[256,1152]{1,0:T(8,128)(2,1)S(1)}, bf16[256,1152]{1,0:T(8,128)(2,1)S(1)}, u32[]{:S(2)}, u32[]{:S(2)}) collective-permute-start(bf16[256,1152]{1,0:T(8,128)(2,1)S(1)} %collective-permute-done.5.refs_2_), channel_id=1, source_target_pairs={{0,8},{1,9},{2,10},{3,11},{4,28},{5,29},{6,30},{7,31},{8,0},{9,1},... | collective-permute-start | bytes 1769480 | tf_op jit(solution)/shard_map/ppermute | solution.py:287
  33.2 3.1 %score_first.1.first = f32[2,128,128]{2,1,0:T(8,128)S(1)} custom-call(bf16[256,1152]{1,0:T(8,128)(2,1)S(1)} %bitcast.9, bf16[256,1152]{1,0:T(8,128)(2,1)S(1)} %collective-permute-done.4.refs_1_, bf16[256,1152]{1,0:T(8,128)(2,1)S(1)} %collective-permute-done.5.refs_2_, bf16[256,1152]{1,0:T(8,128)(2,1)S(1)} %collective-permute-done.refs_3_, ...), custom_call_target="tpu_custom_call" | custom-call | tf_op jit(solution)/shard_map/score_first/pallas_call | solution.py:314
  36.3 2.0 %collective-permute-done.3.refs_0_ = bf16[256,1152]{1,0:T(8,128)(2,1)S(1)} collective-permute-done((bf16[256,1152]{1,0:T(8,128)(2,1)S(1)}, bf16[256,1152]{1,0:T(8,128)(2,1)S(1)}, u32[]{:S(2)}, u32[]{:S(2)}) %collective-permute-start.3) | collective-permute-done | bytes 589856 | tf_op jit(solution)/shard_map/ppermute | solution.py:287
  38.4 2.3 %collective-permute-start.6 = (bf16[160,1152]{1,0:T(8,128)(2,1)S(1)}, bf16[160,1152]{1,0:T(8,128)(2,1)S(1)}, u32[]{:S(2)}, u32[]{:S(2)}) collective-permute-start(bf16[160,1152]{1,0:T(8,128)(2,1)S(1)} %slice.6), channel_id=1, source_target_pairs={{0,96},{1,97},{2,98},{3,99},{4,36},{5,37},{6,38},{7,39},{8,104},{9... | collective-permute-start | bytes 1105928 | tf_op jit(solution)/shard_map/ppermute | solution.py:287
  40.6 0.4 collective-permute-done.7.refs_1_
  41.1 0.6 collective-permute-start.8
  41.7 0.3 collective-permute-done.9.refs_2_
  42.0 0.0 copy-done
  42.0 0.0 copy-done.1
  42.0 3.1 %score_second.1 = (f32[2,128,128]{2,1,0:T(8,128)S(1)}, bf16[128,256]{1,0:T(8,128)(2,1)S(1)}, s32[8,256]{1,0:T(8,128)S(1)}) custom-call(bf16[256,1152]{1,0:T(8,128)(2,1)S(1)} %collective-permute-done.3.refs_0_, bf16[256,1152]{1,0:T(8,128)(2,1)S(1)} %collective-permute-done.7.refs_1_, bf16[256,1152]{1,0:T(8,128)(2,1)S(1)} %collective-permute-done.9.refs_2_, ...), custom_call_target="tpu_custom_call" | custom-call | tf_op jit(solution)/shard_map/score_second/pallas_call | solution.py:314
  45.1 2.0 %collective-permute-done.8.upper = bf16[96,1152]{1,0:T(8,128)(2,1)S(1)} collective-permute-done((bf16[96,1152]{1,0:T(8,128)(2,1)S(1)}, bf16[96,1152]{1,0:T(8,128)(2,1)S(1)}, u32[]{:S(2)}, u32[]{:S(2)}) %collective-permute-start.8) | collective-permute-done | bytes 221216 | tf_op jit(solution)/shard_map/ppermute | solution.py:287
  47.1 0.1 collective-permute-done.6.lower
  47.2 1.9 %score_last.1 = f32[64,8,128]{2,1,0:T(8,128)S(1)} custom-call(bf16[160,1152]{1,0:T(8,128)(2,1)S(1)} %collective-permute-done.6.lower, bf16[96,1152]{1,0:T(8,128)(2,1)S(1)} %collective-permute-done.8.upper, bf16[8,256,1024]{2,1,0:T(8,128)(2,1)S(1)} %get-tuple-element.25.refs_4_.refs_3_.lists, f32[256,128]{1,0:T(8,128)S(1)} %get-tuple-element.26.refs_5_.refs_4_.norms, ...), custom_call_target="tpu_custom_call" | custom-call | tf_op jit(solution)/shard_map/score_last/pallas_call | solution.py:326
  49.1 16.7 %all_to_all.11 = f32[64,8,128]{2,1,0:T(8,128)S(1)} all-to-all(f32[64,8,128]{2,1,0:T(8,128)S(1)} %score_last.1), channel_id=1, replica_groups={{0,1,32,33,24,25,56,57,3,2,35,34,27,26,59,58,96,97,64,65,120,121,88,89,..., dimensions={0} | all-to-all | bytes 524288 | tf_op jit(solution)/shard_map/all_to_all | solution.py:330
  65.8 1.4 %final.1 = f32[32,32]{1,0:T(8,128)} custom-call(f32[4,2,4,2,8,128]{5,4,3,2,1,0:T(8,128)S(1)} %bitcast.10, bf16[128,256]{1,0:T(8,128)(2,1)S(1)} %get-tuple-element.33.pick_ref, s32[8,256]{1,0:T(8,128)S(1)} %get-tuple-element.34.group_ref), custom_call_target="tpu_custom_call" | custom-call | tf_op jit(solution)/shard_map/final/pallas_call | solution.py:331
  (2 shorter events, 0.0 us)
Async XLA Ops:
  0.0 23.5 %collective-permute-start.1 = (bf16[4,256,1024]{2,1,0:T(8,128)(2,1)}, bf16[4,256,1024]{2,1,0:T(8,128)(2,1)S(1)}, u32[]{:S(2)}, u32[]{:S(2)}) collective-permute-start(bf16[4,256,1024]{2,1,0:T(8,128)(2,1)} %own.1), channel_id=1, source_target_pairs={{0,4},{1,5},{2,6},{3,7},{4,0},{5,1},{6,2},{7,3},{8,12},{9,13},{10,... | collective-permute-start | bytes 6291464 | tf_op jit(solution)/shard_map/ppermute | solution.py:298
  17.4 9.9 %collective-permute-start = (bf16[256,1152]{1,0:T(8,128)(2,1)S(1)}, bf16[256,1152]{1,0:T(8,128)(2,1)S(1)}, u32[]{:S(2)}, u32[]{:S(2)}) collective-permute-start(bf16[256,1152]{1,0:T(8,128)(2,1)S(1)} %bitcast.6), channel_id=1, source_target_pairs={{0,8},{1,9},{2,10},{3,11},{4,28},{5,29},{6,30},{7,31},{8,0},{9,1},... | collective-permute-start | bytes 1769480 | tf_op jit(solution)/shard_map/ppermute | solution.py:287
  17.4 12.6 %collective-permute-start.4 = (bf16[256,1152]{1,0:T(8,128)(2,1)S(1)}, bf16[256,1152]{1,0:T(8,128)(2,1)S(1)}, u32[]{:S(2)}, u32[]{:S(2)}) collective-permute-start(bf16[256,1152]{1,0:T(8,128)(2,1)S(1)} %bitcast.7), channel_id=1, source_target_pairs={{0,3},{1,2},{2,1},{3,0},{4,5},{5,4},{6,7},{7,6},{8,11},{9,10},{10,... | collective-permute-start | bytes 1769480 | tf_op jit(solution)/shard_map/ppermute | solution.py:287
  20.1 12.1 %collective-permute-start.5 = (bf16[256,1152]{1,0:T(8,128)(2,1)S(1)}, bf16[256,1152]{1,0:T(8,128)(2,1)S(1)}, u32[]{:S(2)}, u32[]{:S(2)}) collective-permute-start(bf16[256,1152]{1,0:T(8,128)(2,1)S(1)} %bitcast.8), channel_id=1, source_target_pairs={{0,96},{1,97},{2,98},{3,99},{4,36},{5,37},{6,38},{7,39},{8,104},{9... | collective-permute-start | bytes 1769480 | tf_op jit(solution)/shard_map/ppermute | solution.py:287
  22.2 1.3 %collective-permute-start.2 = (s32[4]{0:T(128)}, s32[4]{0:T(128)S(1)}, u32[]{:S(2)}, u32[]{:S(2)}) collective-permute-start(s32[4]{0:T(128)} %param.8), channel_id=1, source_target_pairs={{0,4},{1,5},{2,6},{3,7},{4,0},{5,1},{6,2},{7,3},{8,12},{9,13},{10,... | collective-permute-start | bytes 56 | tf_op jit(solution)/shard_map/ppermute | solution.py:300
  27.3 14.8 %copy-start = (s32[32,8]{0,1:T(8,128)S(1)}, s32[32,8]{0,1:T(8,128)}, u32[]{:S(2)}) copy-start(s32[32,8]{0,1:T(8,128)} %param.6) | copy-start | bytes 3076
  27.3 14.8 %copy-start.1 = (s32[128]{0:T(128)S(1)}, s32[128]{0:T(128)}, u32[]{:S(2)}) copy-start(s32[128]{0:T(128)} %param.7) | copy-start | bytes 1540
  27.3 11.1 %collective-permute-start.3 = (bf16[256,1152]{1,0:T(8,128)(2,1)S(1)}, bf16[256,1152]{1,0:T(8,128)(2,1)S(1)}, u32[]{:S(2)}, u32[]{:S(2)}) collective-permute-start(bf16[256,1152]{1,0:T(8,128)(2,1)S(1)} %collective-permute-done.refs_3_), channel_id=1, source_target_pairs={{0,3},{1,2},{2,1},{3,0},{4,5},{5,4},{6,7},{7,6},{8,11},{9,10},{10,... | collective-permute-start | bytes 1769480 | tf_op jit(solution)/shard_map/ppermute | solution.py:287
  29.9 11.1 %collective-permute-start.7 = (bf16[256,1152]{1,0:T(8,128)(2,1)S(1)}, bf16[256,1152]{1,0:T(8,128)(2,1)S(1)}, u32[]{:S(2)}, u32[]{:S(2)}) collective-permute-start(bf16[256,1152]{1,0:T(8,128)(2,1)S(1)} %collective-permute-done.4.refs_1_), channel_id=1, source_target_pairs={{0,96},{1,97},{2,98},{3,99},{4,36},{5,37},{6,38},{7,39},{8,104},{9... | collective-permute-start | bytes 1769480 | tf_op jit(solution)/shard_map/ppermute | solution.py:287
  32.1 9.9 %collective-permute-start.9 = (bf16[256,1152]{1,0:T(8,128)(2,1)S(1)}, bf16[256,1152]{1,0:T(8,128)(2,1)S(1)}, u32[]{:S(2)}, u32[]{:S(2)}) collective-permute-start(bf16[256,1152]{1,0:T(8,128)(2,1)S(1)} %collective-permute-done.5.refs_2_), channel_id=1, source_target_pairs={{0,8},{1,9},{2,10},{3,11},{4,28},{5,29},{6,30},{7,31},{8,0},{9,1},... | collective-permute-start | bytes 1769480 | tf_op jit(solution)/shard_map/ppermute | solution.py:287
  38.4 8.8 %collective-permute-start.6 = (bf16[160,1152]{1,0:T(8,128)(2,1)S(1)}, bf16[160,1152]{1,0:T(8,128)(2,1)S(1)}, u32[]{:S(2)}, u32[]{:S(2)}) collective-permute-start(bf16[160,1152]{1,0:T(8,128)(2,1)S(1)} %slice.6), channel_id=1, source_target_pairs={{0,96},{1,97},{2,98},{3,99},{4,36},{5,37},{6,38},{7,39},{8,104},{9... | collective-permute-start | bytes 1105928 | tf_op jit(solution)/shard_map/ppermute | solution.py:287
  41.1 6.0 %collective-permute-start.8 = (bf16[96,1152]{1,0:T(8,128)(2,1)S(1)}, bf16[96,1152]{1,0:T(8,128)(2,1)S(1)}, u32[]{:S(2)}, u32[]{:S(2)}) collective-permute-start(bf16[96,1152]{1,0:T(8,128)(2,1)S(1)} %slice.8), channel_id=1, source_target_pairs={{0,8},{1,9},{2,10},{3,11},{4,28},{5,29},{6,30},{7,31},{8,0},{9,1},... | collective-permute-start | bytes 663560 | tf_op jit(solution)/shard_map/ppermute | solution.py:287

commit v9 on v7

--- a/solution.py
+++ b/solution.py
@@ -123,7 +123,15 @@
 
 
 def widen_kernel(queries_ref, probes_ref, slot_ref, out_ref):
-    table = rank_table(probes_ref, place_matrix(slot_ref)).T.astype(BF16)
+    lists = lax.broadcasted_iota(jnp.int32, (128, 32), 0)
+    named = jnp.zeros((128, 32), F32)
+    for j in range(8):
+        named = jnp.where(probes_ref[j : j + 1, :] == lists, 1.0, named)
+    before = lax.broadcasted_iota(jnp.int32, (32, 32), 0) <= lax.broadcasted_iota(jnp.int32, (32, 32), 1)
+    count = named * jnp.dot(named.astype(BF16), before.astype(BF16), preferred_element_type=F32)
+    place = place_matrix(slot_ref)
+    table = lax.dot_general(count.astype(BF16), place, (((0,), (1,)), ((), ())), preferred_element_type=F32)
+    table = (table - 1.0).astype(BF16)
     for copy in range(8):
         out_ref[copy, :, :D] = queries_ref[...]
         out_ref[copy, :, D:] = table

time: 67.4 us -> 67.4 us (level)
  no operation moved by 1% of the time
where the time goes in v9:
time: 67.4 us; the launch traced here: 67.1 us
  blocking collectives  32.8 us (49%)
  starting transfers between devices  13.7 us (20%)
  Pallas kernels  13 us (19%)
  waiting for transfers between devices  6.83 us (10%)
  local copies, waits for them, and re-layouts  0.71 us (1%)
    all_to_all x1, blocking collectives, per_device(): lax.all_to_all(blocks, AXES, 0, 0, axis_index_groups=CORE_GROUPS, tiled=T...  16.7 us
    all_to_all x1, blocking collectives, per_device(): lax.all_to_all(wide, AXES, 0, 0, axis_index_groups=NEAR_GROUPS, tiled=True)  16.1 us
    ppermute x8, starting transfers between devices, hop(): lax.ppermute(value, AXES, [(device, far(device, mask, False)) for device...  13.7 us
    pallas_call x2, Pallas kernels, scored(): pl.pallas_call(kernel, out_shape=out_shape, in_specs=spaces('v' * (len(ma...  6.22 us
    ppermute x8, waiting for transfers between devices, hop(): lax.ppermute(value, AXES, [(device, far(device, mask, False)) for device...  5.57 us
    pallas_call x1, Pallas kernels, per_device(): pl.pallas_call(lists_kernel, out_shape=(pltpu.VMEM((8, 256, D), BF16), pl...  2.35 us
    pallas_call x1, Pallas kernels, per_device(): pl.pallas_call(last_kernel, out_shape=shape((N_CORE, 8, 128), F32), in_sp...  1.85 us
    pallas_call x1, Pallas kernels, per_device(): pl.pallas_call(final_kernel, out_shape=shape((32, TOPK), F32), in_specs=s...  1.41 us
  transfers between devices with their start and end apart: 10, of which 7 were waited for; matrix products, arithmetic and copies ran while one was open for 0% of the time, Pallas kernels for 15%

profile of v9, /device:TPU:0, one launch (start us, length us, event | category | flops | bytes accessed | tf_op | source)
XLA Modules:
  0.0 67.1 jit_solution(13341351106141347625)
XLA Ops:
  0.0 0.0 collective-permute-start.1
  0.0 1.2 %widen.1 = bf16[8,32,1152]{2,1,0:T(8,128)(2,1)S(1)} custom-call(bf16[32,1024]{1,0:T(8,128)(2,1)} %queries_ref.1, s32[8,32]{1,0:T(8,128)} %bitcast.11, s32[1,128]{1,0:T(1,128)} %bitcast.13), custom_call_target="tpu_custom_call" | custom-call | tf_op jit(solution)/shard_map/widen/pallas_call | solution.py:292
  1.2 16.1 %all_to_all.10 = bf16[8,32,1152]{2,1,0:T(8,128)(2,1)S(1)} all-to-all(bf16[8,32,1152]{2,1,0:T(8,128)(2,1)S(1)} %widen.1), channel_id=1, replica_groups={{0,1,32,33,24,25,56,57},{3,2,35,34,27,26,59,58},{96,97,64,65,120,121,88..., dimensions={0} | all-to-all | bytes 1179648 | tf_op jit(solution)/shard_map/all_to_all | solution.py:295
  17.3 0.0 collective-permute-start
  17.3 2.7 %collective-permute-start.4 = (bf16[256,1152]{1,0:T(8,128)(2,1)S(1)}, bf16[256,1152]{1,0:T(8,128)(2,1)S(1)}, u32[]{:S(2)}, u32[]{:S(2)}) collective-permute-start(bf16[256,1152]{1,0:T(8,128)(2,1)S(1)} %bitcast.7), channel_id=1, source_target_pairs={{0,3},{1,2},{2,1},{3,0},{4,5},{5,4},{6,7},{7,6},{8,11},{9,10},{10,... | collective-permute-start | bytes 1769480 | tf_op jit(solution)/shard_map/ppermute | solution.py:285
  20.0 2.2 %collective-permute-start.5 = (bf16[256,1152]{1,0:T(8,128)(2,1)S(1)}, bf16[256,1152]{1,0:T(8,128)(2,1)S(1)}, u32[]{:S(2)}, u32[]{:S(2)}) collective-permute-start(bf16[256,1152]{1,0:T(8,128)(2,1)S(1)} %bitcast.8), channel_id=1, source_target_pairs={{0,96},{1,97},{2,98},{3,99},{4,36},{5,37},{6,38},{7,39},{8,104},{9... | collective-permute-start | bytes 1769480 | tf_op jit(solution)/shard_map/ppermute | solution.py:285
  22.2 0.0 collective-permute-start.2
  22.2 1.3 %collective-permute-done.2 = s32[4]{0:T(128)S(1)} collective-permute-done((s32[4]{0:T(128)}, s32[4]{0:T(128)S(1)}, u32[]{:S(2)}, u32[]{:S(2)}) %collective-permute-start.2) | collective-permute-done | bytes 48 | tf_op jit(solution)/shard_map/ppermute | solution.py:298
  23.5 0.0 collective-permute-done.1.sibling
  23.5 0.0 copy-start.2
  23.5 0.7 copy-done.2
  24.1 2.3 %lists.1 = (bf16[8,256,1024]{2,1,0:T(8,128)(2,1)S(1)}, f32[256,128]{1,0:T(8,128)S(1)}) custom-call(bf16[4,256,1024]{2,1,0:T(8,128)(2,1)} %own.1, bf16[4,256,1024]{2,1,0:T(8,128)(2,1)S(1)} %collective-permute-done.1.sibling, s32[1,4]{1,0:T(1,128)S(1)} %bitcast.15, s32[1,4]{1,0:T(1,128)S(1)} %bitcast.16), custom_call_target="tpu_custom_call" | custom-call | tf_op jit(solution)/shard_map/lists/pallas_call | solution.py:303
  26.5 0.7 %collective-permute-done.refs_3_ = bf16[256,1152]{1,0:T(8,128)(2,1)S(1)} collective-permute-done((bf16[256,1152]{1,0:T(8,128)(2,1)S(1)}, bf16[256,1152]{1,0:T(8,128)(2,1)S(1)}, u32[]{:S(2)}, u32[]{:S(2)}) %collective-permute-start) | collective-permute-done | bytes 589856 | tf_op jit(solution)/shard_map/ppermute | solution.py:285
  27.2 2.7 %collective-permute-start.3 = (bf16[256,1152]{1,0:T(8,128)(2,1)S(1)}, bf16[256,1152]{1,0:T(8,128)(2,1)S(1)}, u32[]{:S(2)}, u32[]{:S(2)}) collective-permute-start(bf16[256,1152]{1,0:T(8,128)(2,1)S(1)} %collective-permute-done.refs_3_), channel_id=1, source_target_pairs={{0,3},{1,2},{2,1},{3,0},{4,5},{5,4},{6,7},{7,6},{8,11},{9,10},{10,... | collective-permute-start | bytes 1769480 | tf_op jit(solution)/shard_map/ppermute | solution.py:285
  29.9 0.0 collective-permute-done.4.refs_1_
  29.9 2.2 %collective-permute-start.7 = (bf16[256,1152]{1,0:T(8,128)(2,1)S(1)}, bf16[256,1152]{1,0:T(8,128)(2,1)S(1)}, u32[]{:S(2)}, u32[]{:S(2)}) collective-permute-start(bf16[256,1152]{1,0:T(8,128)(2,1)S(1)} %collective-permute-done.4.refs_1_), channel_id=1, source_target_pairs={{0,96},{1,97},{2,98},{3,99},{4,36},{5,37},{6,38},{7,39},{8,104},{9... | collective-permute-start | bytes 1769480 | tf_op jit(solution)/shard_map/ppermute | solution.py:285
  32.1 0.0 collective-permute-done.5.refs_2_
  32.1 1.0 %collective-permute-start.9 = (bf16[256,1152]{1,0:T(8,128)(2,1)S(1)}, bf16[256,1152]{1,0:T(8,128)(2,1)S(1)}, u32[]{:S(2)}, u32[]{:S(2)}) collective-permute-start(bf16[256,1152]{1,0:T(8,128)(2,1)S(1)} %collective-permute-done.5.refs_2_), channel_id=1, source_target_pairs={{0,8},{1,9},{2,10},{3,11},{4,28},{5,29},{6,30},{7,31},{8,0},{9,1},... | collective-permute-start | bytes 1769480 | tf_op jit(solution)/shard_map/ppermute | solution.py:285
  33.1 3.1 %score_first.1.first = f32[2,128,128]{2,1,0:T(8,128)S(1)} custom-call(bf16[256,1152]{1,0:T(8,128)(2,1)S(1)} %bitcast.9, bf16[256,1152]{1,0:T(8,128)(2,1)S(1)} %collective-permute-done.4.refs_1_, bf16[256,1152]{1,0:T(8,128)(2,1)S(1)} %collective-permute-done.5.refs_2_, bf16[256,1152]{1,0:T(8,128)(2,1)S(1)} %collective-permute-done.refs_3_, ...), custom_call_target="tpu_custom_call" | custom-call | tf_op jit(solution)/shard_map/score_first/pallas_call | solution.py:312
  36.3 2.0 %collective-permute-done.3.refs_0_ = bf16[256,1152]{1,0:T(8,128)(2,1)S(1)} collective-permute-done((bf16[256,1152]{1,0:T(8,128)(2,1)S(1)}, bf16[256,1152]{1,0:T(8,128)(2,1)S(1)}, u32[]{:S(2)}, u32[]{:S(2)}) %collective-permute-start.3) | collective-permute-done | bytes 589856 | tf_op jit(solution)/shard_map/ppermute | solution.py:285
  38.4 2.3 %collective-permute-start.6 = (bf16[160,1152]{1,0:T(8,128)(2,1)S(1)}, bf16[160,1152]{1,0:T(8,128)(2,1)S(1)}, u32[]{:S(2)}, u32[]{:S(2)}) collective-permute-start(bf16[160,1152]{1,0:T(8,128)(2,1)S(1)} %slice.6), channel_id=1, source_target_pairs={{0,96},{1,97},{2,98},{3,99},{4,36},{5,37},{6,38},{7,39},{8,104},{9... | collective-permute-start | bytes 1105928 | tf_op jit(solution)/shard_map/ppermute | solution.py:285
  40.6 0.4 collective-permute-done.7.refs_1_
  41.0 0.6 collective-permute-start.8
  41.7 0.3 collective-permute-done.9.refs_2_
  42.0 0.0 copy-done
  42.0 0.0 copy-done.1
  42.0 3.1 %score_second.1 = (f32[2,128,128]{2,1,0:T(8,128)S(1)}, bf16[128,256]{1,0:T(8,128)(2,1)S(1)}, s32[8,256]{1,0:T(8,128)S(1)}) custom-call(bf16[256,1152]{1,0:T(8,128)(2,1)S(1)} %collective-permute-done.3.refs_0_, bf16[256,1152]{1,0:T(8,128)(2,1)S(1)} %collective-permute-done.7.refs_1_, bf16[256,1152]{1,0:T(8,128)(2,1)S(1)} %collective-permute-done.9.refs_2_, ...), custom_call_target="tpu_custom_call" | custom-call | tf_op jit(solution)/shard_map/score_second/pallas_call | solution.py:312
  45.1 1.9 %collective-permute-done.8.upper = bf16[96,1152]{1,0:T(8,128)(2,1)S(1)} collective-permute-done((bf16[96,1152]{1,0:T(8,128)(2,1)S(1)}, bf16[96,1152]{1,0:T(8,128)(2,1)S(1)}, u32[]{:S(2)}, u32[]{:S(2)}) %collective-permute-start.8) | collective-permute-done | bytes 221216 | tf_op jit(solution)/shard_map/ppermute | solution.py:285
  47.0 0.1 collective-permute-done.6.lower
  47.2 1.9 %score_last.1 = f32[64,8,128]{2,1,0:T(8,128)S(1)} custom-call(bf16[160,1152]{1,0:T(8,128)(2,1)S(1)} %collective-permute-done.6.lower, bf16[96,1152]{1,0:T(8,128)(2,1)S(1)} %collective-permute-done.8.upper, bf16[8,256,1024]{2,1,0:T(8,128)(2,1)S(1)} %get-tuple-element.25.refs_4_.refs_3_.lists, f32[256,128]{1,0:T(8,128)S(1)} %get-tuple-element.26.refs_5_.refs_4_.norms, ...), custom_call_target="tpu_custom_call" | custom-call | tf_op jit(solution)/shard_map/score_last/pallas_call | solution.py:324
  49.0 16.7 %all_to_all.11 = f32[64,8,128]{2,1,0:T(8,128)S(1)} all-to-all(f32[64,8,128]{2,1,0:T(8,128)S(1)} %score_last.1), channel_id=1, replica_groups={{0,1,32,33,24,25,56,57,3,2,35,34,27,26,59,58,96,97,64,65,120,121,88,89,..., dimensions={0} | all-to-all | bytes 524288 | tf_op jit(solution)/shard_map/all_to_all | solution.py:328
  65.7 1.4 %final.1 = f32[32,32]{1,0:T(8,128)} custom-call(f32[4,2,4,2,8,128]{5,4,3,2,1,0:T(8,128)S(1)} %bitcast.10, bf16[128,256]{1,0:T(8,128)(2,1)S(1)} %get-tuple-element.33.pick_ref, s32[8,256]{1,0:T(8,128)S(1)} %get-tuple-element.34.group_ref), custom_call_target="tpu_custom_call" | custom-call | tf_op jit(solution)/shard_map/final/pallas_call | solution.py:329
  (4 shorter events, 0.1 us)
Async XLA Ops:
  0.0 23.5 %collective-permute-start.1 = (bf16[4,256,1024]{2,1,0:T(8,128)(2,1)}, bf16[4,256,1024]{2,1,0:T(8,128)(2,1)S(1)}, u32[]{:S(2)}, u32[]{:S(2)}) collective-permute-start(bf16[4,256,1024]{2,1,0:T(8,128)(2,1)} %own.1), channel_id=1, source_target_pairs={{0,4},{1,5},{2,6},{3,7},{4,0},{5,1},{6,2},{7,3},{8,12},{9,13},{10,... | collective-permute-start | bytes 6291464 | tf_op jit(solution)/shard_map/ppermute | solution.py:296
  17.3 9.9 %collective-permute-start = (bf16[256,1152]{1,0:T(8,128)(2,1)S(1)}, bf16[256,1152]{1,0:T(8,128)(2,1)S(1)}, u32[]{:S(2)}, u32[]{:S(2)}) collective-permute-start(bf16[256,1152]{1,0:T(8,128)(2,1)S(1)} %bitcast.6), channel_id=1, source_target_pairs={{0,8},{1,9},{2,10},{3,11},{4,28},{5,29},{6,30},{7,31},{8,0},{9,1},... | collective-permute-start | bytes 1769480 | tf_op jit(solution)/shard_map/ppermute | solution.py:285
  17.3 12.6 %collective-permute-start.4 = (bf16[256,1152]{1,0:T(8,128)(2,1)S(1)}, bf16[256,1152]{1,0:T(8,128)(2,1)S(1)}, u32[]{:S(2)}, u32[]{:S(2)}) collective-permute-start(bf16[256,1152]{1,0:T(8,128)(2,1)S(1)} %bitcast.7), channel_id=1, source_target_pairs={{0,3},{1,2},{2,1},{3,0},{4,5},{5,4},{6,7},{7,6},{8,11},{9,10},{10,... | collective-permute-start | bytes 1769480 | tf_op jit(solution)/shard_map/ppermute | solution.py:285
  20.0 12.1 %collective-permute-start.5 = (bf16[256,1152]{1,0:T(8,128)(2,1)S(1)}, bf16[256,1152]{1,0:T(8,128)(2,1)S(1)}, u32[]{:S(2)}, u32[]{:S(2)}) collective-permute-start(bf16[256,1152]{1,0:T(8,128)(2,1)S(1)} %bitcast.8), channel_id=1, source_target_pairs={{0,96},{1,97},{2,98},{3,99},{4,36},{5,37},{6,38},{7,39},{8,104},{9... | collective-permute-start | bytes 1769480 | tf_op jit(solution)/shard_map/ppermute | solution.py:285
  22.2 1.3 %collective-permute-start.2 = (s32[4]{0:T(128)}, s32[4]{0:T(128)S(1)}, u32[]{:S(2)}, u32[]{:S(2)}) collective-permute-start(s32[4]{0:T(128)} %param.8), channel_id=1, source_target_pairs={{0,4},{1,5},{2,6},{3,7},{4,0},{5,1},{6,2},{7,3},{8,12},{9,13},{10,... | collective-permute-start | bytes 56 | tf_op jit(solution)/shard_map/ppermute | solution.py:298
  23.5 0.7 copy-start.2
  27.2 14.8 %copy-start = (s32[32,8]{0,1:T(8,128)S(1)}, s32[32,8]{0,1:T(8,128)}, u32[]{:S(2)}) copy-start(s32[32,8]{0,1:T(8,128)} %param.6) | copy-start | bytes 3076
  27.2 14.8 %copy-start.1 = (s32[128]{0:T(128)S(1)}, s32[128]{0:T(128)}, u32[]{:S(2)}) copy-start(s32[128]{0:T(128)} %param.7) | copy-start | bytes 1540
  27.2 11.1 %collective-permute-start.3 = (bf16[256,1152]{1,0:T(8,128)(2,1)S(1)}, bf16[256,1152]{1,0:T(8,128)(2,1)S(1)}, u32[]{:S(2)}, u32[]{:S(2)}) collective-permute-start(bf16[256,1152]{1,0:T(8,128)(2,1)S(1)} %collective-permute-done.refs_3_), channel_id=1, source_target_pairs={{0,3},{1,2},{2,1},{3,0},{4,5},{5,4},{6,7},{7,6},{8,11},{9,10},{10,... | collective-permute-start | bytes 1769480 | tf_op jit(solution)/shard_map/ppermute | solution.py:285
  29.9 11.1 %collective-permute-start.7 = (bf16[256,1152]{1,0:T(8,128)(2,1)S(1)}, bf16[256,1152]{1,0:T(8,128)(2,1)S(1)}, u32[]{:S(2)}, u32[]{:S(2)}) collective-permute-start(bf16[256,1152]{1,0:T(8,128)(2,1)S(1)} %collective-permute-done.4.refs_1_), channel_id=1, source_target_pairs={{0,96},{1,97},{2,98},{3,99},{4,36},{5,37},{6,38},{7,39},{8,104},{9... | collective-permute-start | bytes 1769480 | tf_op jit(solution)/shard_map/ppermute | solution.py:285
  32.1 9.9 %collective-permute-start.9 = (bf16[256,1152]{1,0:T(8,128)(2,1)S(1)}, bf16[256,1152]{1,0:T(8,128)(2,1)S(1)}, u32[]{:S(2)}, u32[]{:S(2)}) collective-permute-start(bf16[256,1152]{1,0:T(8,128)(2,1)S(1)} %collective-permute-done.5.refs_2_), channel_id=1, source_target_pairs={{0,8},{1,9},{2,10},{3,11},{4,28},{5,29},{6,30},{7,31},{8,0},{9,1},... | collective-permute-start | bytes 1769480 | tf_op jit(solution)/shard_map/ppermute | solution.py:285
  38.4 8.8 %collective-permute-start.6 = (bf16[160,1152]{1,0:T(8,128)(2,1)S(1)}, bf16[160,1152]{1,0:T(8,128)(2,1)S(1)}, u32[]{:S(2)}, u32[]{:S(2)}) collective-permute-start(bf16[160,1152]{1,0:T(8,128)(2,1)S(1)} %slice.6), channel_id=1, source_target_pairs={{0,96},{1,97},{2,98},{3,99},{4,36},{5,37},{6,38},{7,39},{8,104},{9... | collective-permute-start | bytes 1105928 | tf_op jit(solution)/shard_map/ppermute | solution.py:285
  41.0 6.0 %collective-permute-start.8 = (bf16[96,1152]{1,0:T(8,128)(2,1)S(1)}, bf16[96,1152]{1,0:T(8,128)(2,1)S(1)}, u32[]{:S(2)}, u32[]{:S(2)}) collective-permute-start(bf16[96,1152]{1,0:T(8,128)(2,1)S(1)} %slice.8), channel_id=1, source_target_pairs={{0,8},{1,9},{2,10},{3,11},{4,28},{5,29},{6,30},{7,31},{8,0},{9,1},... | collective-permute-start | bytes 663560 | tf_op jit(solution)/shard_map/ppermute | solution.py:285

commit v10 on v9

--- a/solution.py
+++ b/solution.py
@@ -154,15 +154,19 @@
         group_ref[:, 32 * j : 32 * j + 32] = jnp.broadcast_to(where & 3, (8, 32))
 
 
-def lists_kernel(own, sibling, own_valid, sibling_valid, lists, norms, sems):
+def lists_kernel(own, sibling, own_rows, sibling_valid, lists, norms, own_valid, sems):
     copies = []
     for t in range(8):
         copies.append(pltpu.make_async_copy(own.at[t] if t < 4 else sibling.at[t - 4], lists.at[t], sems.at[t]))
         copies[t].start()
+    valid_copy = pltpu.make_async_copy(own_rows, own_valid, sems.at[8])
+    valid_copy.start()
     row = lax.axis_index("replica") * 256 + lax.broadcasted_iota(jnp.int32, (256, 1), 0)
     lane = lax.broadcasted_iota(jnp.int32, (256, 128), 1)
     total = jnp.zeros((256, 128), F32)
     for t in (4, 5, 6, 7, 0, 1, 2, 3):
+        if t == 0:
+            valid_copy.wait()
         copies[t].wait()
         rows = lists[t].astype(F32)
         valid = (own_valid if t < 4 else sibling_valid)[0:1, t % 4 : t % 4 + 1]
@@ -301,9 +305,9 @@
     for mask in (1, 2, 4):
         groups[mask] = hop(near, mask)
     lists, norms = pl.pallas_call(
-        lists_kernel, out_shape=(pltpu.VMEM((8, 256, D), BF16), pltpu.VMEM((256, 128), F32)), in_specs=spaces("havv"),
-        out_specs=spaces("vv"), scratch_shapes=[pltpu.SemaphoreType.DMA((8,))], compiler_params=params(), name="lists",
-    )(pltpu.with_memory_space_constraint(database, pltpu.HBM), sibling, valid_rows.reshape(1, 4), sibling_valid.reshape(1, 4))
+        lists_kernel, out_shape=(pltpu.VMEM((8, 256, D), BF16), pltpu.VMEM((256, 128), F32)), in_specs=spaces("hahv"),
+        out_specs=spaces("vv"), scratch_shapes=[pltpu.VMEM((1, 4), jnp.int32), pltpu.SemaphoreType.DMA((9,))], compiler_params=params(), name="lists",
+    )(pltpu.with_memory_space_constraint(database, pltpu.HBM), sibling, pltpu.with_memory_space_constraint(valid_rows.reshape(1, 4), pltpu.HBM), sibling_valid.reshape(1, 4))
     groups[4], lists, norms = lax.optimization_barrier((groups[4], lists, norms))
     for mask, source, step in ((3, 1, 2), (6, 2, 4), (5, 4, 1)):
         groups[mask] = hop(groups[source], step)

time: 67.4 us -> 67.4 us (level)
  no operation moved by 1% of the time
where the time goes in v10:
time: 67.4 us; the launch traced here: 67.1 us
  blocking collectives  32.8 us (49%)
  starting transfers between devices  13.7 us (20%)
  Pallas kernels  13.1 us (19%)
  waiting for transfers between devices  7.42 us (11%)
    all_to_all x1, blocking collectives, per_device(): lax.all_to_all(blocks, AXES, 0, 0, axis_index_groups=CORE_GROUPS, tiled=T...  16.7 us
    all_to_all x1, blocking collectives, per_device(): lax.all_to_all(wide, AXES, 0, 0, axis_index_groups=NEAR_GROUPS, tiled=True)  16.1 us
    ppermute x8, starting transfers between devices, hop(): lax.ppermute(value, AXES, [(device, far(device, mask, False)) for device...  13.7 us
    pallas_call x2, Pallas kernels, scored(): pl.pallas_call(kernel, out_shape=out_shape, in_specs=spaces('v' * (len(ma...  6.24 us
    ppermute x8, waiting for transfers between devices, hop(): lax.ppermute(value, AXES, [(device, far(device, mask, False)) for device...  6.17 us
    pallas_call x1, Pallas kernels, per_device(): pl.pallas_call(lists_kernel, out_shape=(pltpu.VMEM((8, 256, D), BF16), pl...  2.39 us
    pallas_call x1, Pallas kernels, per_device(): pl.pallas_call(last_kernel, out_shape=shape((N_CORE, 8, 128), F32), in_sp...  1.86 us
    pallas_call x1, Pallas kernels, per_device(): pl.pallas_call(final_kernel, out_shape=shape((32, TOPK), F32), in_specs=s...  1.41 us
  transfers between devices with their start and end apart: 10, of which 7 were waited for; matrix products, arithmetic and copies ran while one was open for 0% of the time, Pallas kernels for 15%

profile of v10, /device:TPU:0, one launch (start us, length us, event | category | flops | bytes accessed | tf_op | source)
XLA Modules:
  0.0 67.1 jit_solution(2871546999679329677)
XLA Ops:
  0.0 0.0 collective-permute-start.1
  0.0 1.2 %widen.1 = bf16[8,32,1152]{2,1,0:T(8,128)(2,1)S(1)} custom-call(bf16[32,1024]{1,0:T(8,128)(2,1)} %queries_ref.1, s32[8,32]{1,0:T(8,128)} %bitcast.11, s32[1,128]{1,0:T(1,128)} %bitcast.13), custom_call_target="tpu_custom_call" | custom-call | tf_op jit(solution)/shard_map/widen/pallas_call | solution.py:296
  1.2 16.1 %all_to_all.10 = bf16[8,32,1152]{2,1,0:T(8,128)(2,1)S(1)} all-to-all(bf16[8,32,1152]{2,1,0:T(8,128)(2,1)S(1)} %widen.1), channel_id=1, replica_groups={{0,1,32,33,24,25,56,57},{3,2,35,34,27,26,59,58},{96,97,64,65,120,121,88..., dimensions={0} | all-to-all | bytes 1179648 | tf_op jit(solution)/shard_map/all_to_all | solution.py:299
  17.3 0.0 collective-permute-start
  17.3 2.7 %collective-permute-start.4 = (bf16[256,1152]{1,0:T(8,128)(2,1)S(1)}, bf16[256,1152]{1,0:T(8,128)(2,1)S(1)}, u32[]{:S(2)}, u32[]{:S(2)}) collective-permute-start(bf16[256,1152]{1,0:T(8,128)(2,1)S(1)} %bitcast.7), channel_id=1, source_target_pairs={{0,3},{1,2},{2,1},{3,0},{4,5},{5,4},{6,7},{7,6},{8,11},{9,10},{10,... | collective-permute-start | bytes 1769480 | tf_op jit(solution)/shard_map/ppermute | solution.py:289
  20.0 2.2 %collective-permute-start.5 = (bf16[256,1152]{1,0:T(8,128)(2,1)S(1)}, bf16[256,1152]{1,0:T(8,128)(2,1)S(1)}, u32[]{:S(2)}, u32[]{:S(2)}) collective-permute-start(bf16[256,1152]{1,0:T(8,128)(2,1)S(1)} %bitcast.8), channel_id=1, source_target_pairs={{0,96},{1,97},{2,98},{3,99},{4,36},{5,37},{6,38},{7,39},{8,104},{9... | collective-permute-start | bytes 1769480 | tf_op jit(solution)/shard_map/ppermute | solution.py:289
  22.2 0.0 collective-permute-start.2
  22.2 1.3 %collective-permute-done.2 = s32[4]{0:T(128)S(1)} collective-permute-done((s32[4]{0:T(128)}, s32[4]{0:T(128)S(1)}, u32[]{:S(2)}, u32[]{:S(2)}) %collective-permute-start.2) | collective-permute-done | bytes 48 | tf_op jit(solution)/shard_map/ppermute | solution.py:302
  23.5 0.0 collective-permute-done.1.sibling
  23.5 2.4 %lists.1 = (bf16[8,256,1024]{2,1,0:T(8,128)(2,1)S(1)}, f32[256,128]{1,0:T(8,128)S(1)}) custom-call(bf16[4,256,1024]{2,1,0:T(8,128)(2,1)} %own.1, bf16[4,256,1024]{2,1,0:T(8,128)(2,1)S(1)} %collective-permute-done.1.sibling, s32[1,4]{1,0:T(1,128)} %bitcast.16, s32[1,4]{1,0:T(1,128)S(1)} %bitcast.15), custom_call_target="tpu_custom_call" | custom-call | tf_op jit(solution)/shard_map/lists/pallas_call | solution.py:307
  25.9 1.4 %collective-permute-done.refs_3_ = bf16[256,1152]{1,0:T(8,128)(2,1)S(1)} collective-permute-done((bf16[256,1152]{1,0:T(8,128)(2,1)S(1)}, bf16[256,1152]{1,0:T(8,128)(2,1)S(1)}, u32[]{:S(2)}, u32[]{:S(2)}) %collective-permute-start) | collective-permute-done | bytes 589856 | tf_op jit(solution)/shard_map/ppermute | solution.py:289
  27.2 0.0 copy-start
  27.2 0.0 copy-start.1
  27.2 2.7 %collective-permute-start.3 = (bf16[256,1152]{1,0:T(8,128)(2,1)S(1)}, bf16[256,1152]{1,0:T(8,128)(2,1)S(1)}, u32[]{:S(2)}, u32[]{:S(2)}) collective-permute-start(bf16[256,1152]{1,0:T(8,128)(2,1)S(1)} %collective-permute-done.refs_3_), channel_id=1, source_target_pairs={{0,3},{1,2},{2,1},{3,0},{4,5},{5,4},{6,7},{7,6},{8,11},{9,10},{10,... | collective-permute-start | bytes 1769480 | tf_op jit(solution)/shard_map/ppermute | solution.py:289
  29.9 0.0 collective-permute-done.4.refs_1_
  29.9 2.2 %collective-permute-start.7 = (bf16[256,1152]{1,0:T(8,128)(2,1)S(1)}, bf16[256,1152]{1,0:T(8,128)(2,1)S(1)}, u32[]{:S(2)}, u32[]{:S(2)}) collective-permute-start(bf16[256,1152]{1,0:T(8,128)(2,1)S(1)} %collective-permute-done.4.refs_1_), channel_id=1, source_target_pairs={{0,96},{1,97},{2,98},{3,99},{4,36},{5,37},{6,38},{7,39},{8,104},{9... | collective-permute-start | bytes 1769480 | tf_op jit(solution)/shard_map/ppermute | solution.py:289
  32.1 0.0 collective-permute-done.5.refs_2_
  32.1 1.0 %collective-permute-start.9 = (bf16[256,1152]{1,0:T(8,128)(2,1)S(1)}, bf16[256,1152]{1,0:T(8,128)(2,1)S(1)}, u32[]{:S(2)}, u32[]{:S(2)}) collective-permute-start(bf16[256,1152]{1,0:T(8,128)(2,1)S(1)} %collective-permute-done.5.refs_2_), channel_id=1, source_target_pairs={{0,8},{1,9},{2,10},{3,11},{4,28},{5,29},{6,30},{7,31},{8,0},{9,1},... | collective-permute-start | bytes 1769480 | tf_op jit(solution)/shard_map/ppermute | solution.py:289
  33.1 3.1 %score_first.1.first = f32[2,128,128]{2,1,0:T(8,128)S(1)} custom-call(bf16[256,1152]{1,0:T(8,128)(2,1)S(1)} %bitcast.9, bf16[256,1152]{1,0:T(8,128)(2,1)S(1)} %collective-permute-done.4.refs_1_, bf16[256,1152]{1,0:T(8,128)(2,1)S(1)} %collective-permute-done.5.refs_2_, bf16[256,1152]{1,0:T(8,128)(2,1)S(1)} %collective-permute-done.refs_3_, ...), custom_call_target="tpu_custom_call" | custom-call | tf_op jit(solution)/shard_map/score_first/pallas_call | solution.py:316
  36.3 2.0 %collective-permute-done.3.refs_0_ = bf16[256,1152]{1,0:T(8,128)(2,1)S(1)} collective-permute-done((bf16[256,1152]{1,0:T(8,128)(2,1)S(1)}, bf16[256,1152]{1,0:T(8,128)(2,1)S(1)}, u32[]{:S(2)}, u32[]{:S(2)}) %collective-permute-start.3) | collective-permute-done | bytes 589856 | tf_op jit(solution)/shard_map/ppermute | solution.py:289
  38.4 2.3 %collective-permute-start.6 = (bf16[160,1152]{1,0:T(8,128)(2,1)S(1)}, bf16[160,1152]{1,0:T(8,128)(2,1)S(1)}, u32[]{:S(2)}, u32[]{:S(2)}) collective-permute-start(bf16[160,1152]{1,0:T(8,128)(2,1)S(1)} %slice.6), channel_id=1, source_target_pairs={{0,96},{1,97},{2,98},{3,99},{4,36},{5,37},{6,38},{7,39},{8,104},{9... | collective-permute-start | bytes 1105928 | tf_op jit(solution)/shard_map/ppermute | solution.py:289
  40.6 0.4 collective-permute-done.7.refs_1_
  41.0 0.6 collective-permute-start.8
  41.7 0.3 collective-permute-done.9.refs_2_
  42.0 0.0 copy-done
  42.0 0.0 copy-done.1
  42.0 3.1 %score_second.1 = (f32[2,128,128]{2,1,0:T(8,128)S(1)}, bf16[128,256]{1,0:T(8,128)(2,1)S(1)}, s32[8,256]{1,0:T(8,128)S(1)}) custom-call(bf16[256,1152]{1,0:T(8,128)(2,1)S(1)} %collective-permute-done.3.refs_0_, bf16[256,1152]{1,0:T(8,128)(2,1)S(1)} %collective-permute-done.7.refs_1_, bf16[256,1152]{1,0:T(8,128)(2,1)S(1)} %collective-permute-done.9.refs_2_, ...), custom_call_target="tpu_custom_call" | custom-call | tf_op jit(solution)/shard_map/score_second/pallas_call | solution.py:316
  45.1 1.9 %collective-permute-done.8.upper = bf16[96,1152]{1,0:T(8,128)(2,1)S(1)} collective-permute-done((bf16[96,1152]{1,0:T(8,128)(2,1)S(1)}, bf16[96,1152]{1,0:T(8,128)(2,1)S(1)}, u32[]{:S(2)}, u32[]{:S(2)}) %collective-permute-start.8) | collective-permute-done | bytes 221216 | tf_op jit(solution)/shard_map/ppermute | solution.py:289
  47.0 0.1 collective-permute-done.6.lower
  47.2 1.9 %score_last.1 = f32[64,8,128]{2,1,0:T(8,128)S(1)} custom-call(bf16[160,1152]{1,0:T(8,128)(2,1)S(1)} %collective-permute-done.6.lower, bf16[96,1152]{1,0:T(8,128)(2,1)S(1)} %collective-permute-done.8.upper, bf16[8,256,1024]{2,1,0:T(8,128)(2,1)S(1)} %get-tuple-element.25.refs_4_.refs_3_.lists, f32[256,128]{1,0:T(8,128)S(1)} %get-tuple-element.26.refs_5_.refs_4_.norms, ...), custom_call_target="tpu_custom_call" | custom-call | tf_op jit(solution)/shard_map/score_last/pallas_call | solution.py:328
  49.0 16.7 %all_to_all.11 = f32[64,8,128]{2,1,0:T(8,128)S(1)} all-to-all(f32[64,8,128]{2,1,0:T(8,128)S(1)} %score_last.1), channel_id=1, replica_groups={{0,1,32,33,24,25,56,57,3,2,35,34,27,26,59,58,96,97,64,65,120,121,88,89,..., dimensions={0} | all-to-all | bytes 524288 | tf_op jit(solution)/shard_map/all_to_all | solution.py:332
  65.7 1.4 %final.1 = f32[32,32]{1,0:T(8,128)} custom-call(f32[4,2,4,2,8,128]{5,4,3,2,1,0:T(8,128)S(1)} %bitcast.10, bf16[128,256]{1,0:T(8,128)(2,1)S(1)} %get-tuple-element.33.pick_ref, s32[8,256]{1,0:T(8,128)S(1)} %get-tuple-element.34.group_ref), custom_call_target="tpu_custom_call" | custom-call | tf_op jit(solution)/shard_map/final/pallas_call | solution.py:333
  (2 shorter events, 0.0 us)
Async XLA Ops:
  0.0 23.5 %collective-permute-start.1 = (bf16[4,256,1024]{2,1,0:T(8,128)(2,1)}, bf16[4,256,1024]{2,1,0:T(8,128)(2,1)S(1)}, u32[]{:S(2)}, u32[]{:S(2)}) collective-permute-start(bf16[4,256,1024]{2,1,0:T(8,128)(2,1)} %own.1), channel_id=1, source_target_pairs={{0,4},{1,5},{2,6},{3,7},{4,0},{5,1},{6,2},{7,3},{8,12},{9,13},{10,... | collective-permute-start | bytes 6291464 | tf_op jit(solution)/shard_map/ppermute | solution.py:300
  17.3 9.9 %collective-permute-start = (bf16[256,1152]{1,0:T(8,128)(2,1)S(1)}, bf16[256,1152]{1,0:T(8,128)(2,1)S(1)}, u32[]{:S(2)}, u32[]{:S(2)}) collective-permute-start(bf16[256,1152]{1,0:T(8,128)(2,1)S(1)} %bitcast.6), channel_id=1, source_target_pairs={{0,8},{1,9},{2,10},{3,11},{4,28},{5,29},{6,30},{7,31},{8,0},{9,1},... | collective-permute-start | bytes 1769480 | tf_op jit(solution)/shard_map/ppermute | solution.py:289
  17.3 12.6 %collective-permute-start.4 = (bf16[256,1152]{1,0:T(8,128)(2,1)S(1)}, bf16[256,1152]{1,0:T(8,128)(2,1)S(1)}, u32[]{:S(2)}, u32[]{:S(2)}) collective-permute-start(bf16[256,1152]{1,0:T(8,128)(2,1)S(1)} %bitcast.7), channel_id=1, source_target_pairs={{0,3},{1,2},{2,1},{3,0},{4,5},{5,4},{6,7},{7,6},{8,11},{9,10},{10,... | collective-permute-start | bytes 1769480 | tf_op jit(solution)/shard_map/ppermute | solution.py:289
  20.0 12.1 %collective-permute-start.5 = (bf16[256,1152]{1,0:T(8,128)(2,1)S(1)}, bf16[256,1152]{1,0:T(8,128)(2,1)S(1)}, u32[]{:S(2)}, u32[]{:S(2)}) collective-permute-start(bf16[256,1152]{1,0:T(8,128)(2,1)S(1)} %bitcast.8), channel_id=1, source_target_pairs={{0,96},{1,97},{2,98},{3,99},{4,36},{5,37},{6,38},{7,39},{8,104},{9... | collective-permute-start | bytes 1769480 | tf_op jit(solution)/shard_map/ppermute | solution.py:289
  22.2 1.3 %collective-permute-start.2 = (s32[4]{0:T(128)}, s32[4]{0:T(128)S(1)}, u32[]{:S(2)}, u32[]{:S(2)}) collective-permute-start(s32[4]{0:T(128)} %param.8), channel_id=1, source_target_pairs={{0,4},{1,5},{2,6},{3,7},{4,0},{5,1},{6,2},{7,3},{8,12},{9,13},{10,... | collective-permute-start | bytes 56 | tf_op jit(solution)/shard_map/ppermute | solution.py:302
  27.2 14.8 %copy-start = (s32[32,8]{0,1:T(8,128)S(1)}, s32[32,8]{0,1:T(8,128)}, u32[]{:S(2)}) copy-start(s32[32,8]{0,1:T(8,128)} %param.6) | copy-start | bytes 3076
  27.2 14.8 %copy-start.1 = (s32[128]{0:T(128)S(1)}, s32[128]{0:T(128)}, u32[]{:S(2)}) copy-start(s32[128]{0:T(128)} %param.7) | copy-start | bytes 1540
  27.2 11.1 %collective-permute-start.3 = (bf16[256,1152]{1,0:T(8,128)(2,1)S(1)}, bf16[256,1152]{1,0:T(8,128)(2,1)S(1)}, u32[]{:S(2)}, u32[]{:S(2)}) collective-permute-start(bf16[256,1152]{1,0:T(8,128)(2,1)S(1)} %collective-permute-done.refs_3_), channel_id=1, source_target_pairs={{0,3},{1,2},{2,1},{3,0},{4,5},{5,4},{6,7},{7,6},{8,11},{9,10},{10,... | collective-permute-start | bytes 1769480 | tf_op jit(solution)/shard_map/ppermute | solution.py:289
  29.9 11.1 %collective-permute-start.7 = (bf16[256,1152]{1,0:T(8,128)(2,1)S(1)}, bf16[256,1152]{1,0:T(8,128)(2,1)S(1)}, u32[]{:S(2)}, u32[]{:S(2)}) collective-permute-start(bf16[256,1152]{1,0:T(8,128)(2,1)S(1)} %collective-permute-done.4.refs_1_), channel_id=1, source_target_pairs={{0,96},{1,97},{2,98},{3,99},{4,36},{5,37},{6,38},{7,39},{8,104},{9... | collective-permute-start | bytes 1769480 | tf_op jit(solution)/shard_map/ppermute | solution.py:289
  32.1 9.9 %collective-permute-start.9 = (bf16[256,1152]{1,0:T(8,128)(2,1)S(1)}, bf16[256,1152]{1,0:T(8,128)(2,1)S(1)}, u32[]{:S(2)}, u32[]{:S(2)}) collective-permute-start(bf16[256,1152]{1,0:T(8,128)(2,1)S(1)} %collective-permute-done.5.refs_2_), channel_id=1, source_target_pairs={{0,8},{1,9},{2,10},{3,11},{4,28},{5,29},{6,30},{7,31},{8,0},{9,1},... | collective-permute-start | bytes 1769480 | tf_op jit(solution)/shard_map/ppermute | solution.py:289
  38.4 8.8 %collective-permute-start.6 = (bf16[160,1152]{1,0:T(8,128)(2,1)S(1)}, bf16[160,1152]{1,0:T(8,128)(2,1)S(1)}, u32[]{:S(2)}, u32[]{:S(2)}) collective-permute-start(bf16[160,1152]{1,0:T(8,128)(2,1)S(1)} %slice.6), channel_id=1, source_target_pairs={{0,96},{1,97},{2,98},{3,99},{4,36},{5,37},{6,38},{7,39},{8,104},{9... | collective-permute-start | bytes 1105928 | tf_op jit(solution)/shard_map/ppermute | solution.py:289
  41.0 6.0 %collective-permute-start.8 = (bf16[96,1152]{1,0:T(8,128)(2,1)S(1)}, bf16[96,1152]{1,0:T(8,128)(2,1)S(1)}, u32[]{:S(2)}, u32[]{:S(2)}) collective-permute-start(bf16[96,1152]{1,0:T(8,128)(2,1)S(1)} %slice.8), channel_id=1, source_target_pairs={{0,8},{1,9},{2,10},{3,11},{4,28},{5,29},{6,30},{7,31},{8,0},{9,1},... | collective-permute-start | bytes 663560 | tf_op jit(solution)/shard_map/ppermute | solution.py:289
